TPU v7x, 32 devices: a whole 2x2x4 slice. The times are simulated.
32 devices in a mesh: rep: 2 (over y), gx: 4 (over z), gy: 2 (over x), gz: 2 (over core).
Axes of the slice: x: 2, y: 2, z: 4, core: 2. Of those that a mesh axis runs over, the one named last changes fastest.
Arguments:
- seed_state: float32 [9, 16, 32, 256], P(None, ('rep', 'gx'), 'gy', 'gz'), parts along dimension 1, may hold values from -6 to 6
- costate: float32 [9, 16, 32, 256], P(None, ('rep', 'gx'), 'gy', 'gz'), parts along dimension 1, may hold values from -6 to 6
- step_count: int32 [2], P('rep'), parts along dimension 0, may hold values from 4 to 16
Outputs:
- next_state: float32 [9, 16, 32, 256], P(None, ('rep', 'gx'), 'gy', 'gz'), parts along dimension 1
- seed_gradient: float32 [9, 16, 32, 256], P(None, ('rep', 'gx'), 'gy', 'gz'), parts along dimension 1
There are 2 independent parts, one for each index of `rep`. A program takes and returns all parts, laid end to end along the dimension named above; each array names one. Nothing has to cross between parts.
All inputs are finite; a program needn't handle non-finite values.
Results may differ from a plain program's by a relative error of at most 0.00002.
Values sent between devices are 32-bit elements; how exact they have to be, the bound alone decides.
No kernel may reach another device: no remote copies, remote signals or barrier semaphores. Data moves between devices by JAX's collectives and lax.ppermute only.
A program may use at most 128 MiB of HBM per device.

v0:
```python
import jax
import jax.numpy as jnp
from jax import lax
from jax.sharding import PartitionSpec as P

VISCOSITY = 0.5
DIFFUSIVITY = 0.2
WEISSENBERG = 2.0
EXTENSIBILITY = 100.0
HORIZON = 1.0
COMPONENT = ((3, 6, 7), (6, 4, 8), (7, 8, 5))
PAIRS = ((0, 0), (1, 1), (2, 2), (0, 1), (0, 2), (1, 2))


def padded_2(array, sides, width):
    for axis, dim in sides:
        size, length = (lax.axis_size(axis), array.shape[dim])
        up = [(i, (i + 1) % size) for i in range(size)]
        down = [(j, i) for i, j in up]
        last = lax.slice_in_dim(array, length - width, length, axis=dim)
        leading = lax.slice_in_dim(array, 0, width, axis=dim)
        before = lax.ppermute(last, axis, up)
        after = lax.ppermute(leading, axis, down)
        array = jnp.concatenate([before, array, after], axis=dim)
    return array


def swapped(array, axis, bit):
    return lax.ppermute(array, axis, [(i, i ^ 1 << bit) for i in range(lax.axis_size(axis))])


def shifted(padded, axis_dim, offset):
    slices = [slice(None), slice(1, -1), slice(1, -1), slice(1, -1)]
    length = padded.shape[axis_dim]
    slices[axis_dim] = slice(1 + offset, length - 1 + offset)
    return padded[tuple(slices)]


def centred(padded, axis_dim):
    return 0.5 * (shifted(padded, axis_dim, 1) - shifted(padded, axis_dim, -1))


def advance(padded, time_step):
    centre = padded[:, 1:-1, 1:-1, 1:-1]
    laplace = -6.0 * centre
    for axis_dim in (1, 2, 3):
        laplace = laplace + shifted(padded, axis_dim, 1) + shifted(padded, axis_dim, -1)
    identity = jnp.array([1.0, 1.0, 1.0, 0.0, 0.0, 0.0], jnp.float32)[:, None, None, None]
    factor = (EXTENSIBILITY - 3.0) / (EXTENSIBILITY - (padded[3] + padded[4] + padded[5]))
    stress = (factor[None] * padded[3:9] - identity) / WEISSENBERG
    stress_slopes = [centred(stress, axis_dim) for axis_dim in (1, 2, 3)]
    grads = [centred(padded[0:3], axis_dim) for axis_dim in (1, 2, 3)]
    outputs = []
    for comp_i in range(3):
        divergence = stress_slopes[0][COMPONENT[comp_i][0] - 3]
        divergence = (
            divergence
            + stress_slopes[1][COMPONENT[comp_i][1] - 3]
            + stress_slopes[2][COMPONENT[comp_i][2] - 3]
        )
        outputs.append(centre[comp_i] + time_step * (VISCOSITY * laplace[comp_i] + divergence))
    stress_centre = stress[:, 1:-1, 1:-1, 1:-1]
    for number in range(6):
        comp_i, comp_j = PAIRS[number]
        stretch = jnp.zeros_like(centre[0])
        for axis_k in range(3):
            stretch = stretch + grads[axis_k][comp_i] * centre[COMPONENT[axis_k][comp_j]]
            stretch = stretch + centre[COMPONENT[comp_i][axis_k]] * grads[axis_k][comp_j]
        update = DIFFUSIVITY * laplace[3 + number] + stretch - stress_centre[number]
        outputs.append(centre[3 + number] + time_step * update)
    return jnp.stack(outputs, 0)


def clean_rims(padded, width):
    shape_full = padded.shape
    flags = []
    for axis_dim in (1, 2, 3):
        shape_line = [1, 1, 1, 1]
        shape_line[axis_dim] = shape_full[axis_dim]
        position = lax.broadcasted_iota(jnp.int32, tuple(shape_line), axis_dim)
        flags.append(position)
    ghost_count = jnp.zeros((1, 1, 1, 1), jnp.int32)
    for axis_dim, position in zip((1, 2, 3), flags):
        outside = (position < width) | (position >= shape_full[axis_dim] - width)
        ghost_count = ghost_count + outside.astype(jnp.int32)
    wall_index = lax.axis_index("gy")
    wall_count = lax.axis_size("gy")
    rows_y = flags[1]
    beyond = (wall_index == 0) & (rows_y < width) | (wall_index == wall_count - 1) & (
        rows_y >= shape_full[2] - width
    )
    keep = jnp.logical_not(beyond) & (ghost_count < 2)
    return jnp.where(keep, padded, jnp.zeros_like(padded))


def per_device(seed_state, costate, step_count):
    time_step = HORIZON / step_count[0].astype(jnp.float32)
    stacked = jnp.concatenate([seed_state, costate], 0)
    nearby = padded_2(seed_state, (("gx", 1), ("gy", 2), ("gz", 3)), 1)
    nearby = clean_rims(nearby, 1)
    both = padded_2(stacked, (("gx", 1), ("gy", 2), ("gz", 3)), 2)
    both = clean_rims(both, 2)
    next_state = advance(nearby, time_step)
    outer = both[:9]
    cycle = both[9:, 1:-1, 1:-1, 1:-1]

    def extended(inner):
        full = outer.at[:, 2:-2, 2:-2, 2:-2].set(inner)
        return advance(full, time_step)

    extended_out, pullback = jax.vjp(extended, seed_state)
    (raw_gradient,) = pullback(cycle)
    partner = raw_gradient
    for bit_number in range(lax.axis_size("gy").bit_length() - 1):
        partner = swapped(partner, "gy", bit_number)
    partner = jnp.flip(partner, axis=2)
    signs = jnp.array([1.0, -1.0, 1.0, 1.0, 1.0, 1.0, -1.0, 1.0, -1.0], jnp.float32)[
        :, None, None, None
    ]
    seed_gradient = 0.5 * (raw_gradient + partner * signs)
    return (next_state, seed_gradient)


def solution(mesh):
    placed = (P(None, ("rep", "gx"), "gy", "gz"), P(None, ("rep", "gx"), "gy", "gz"), P("rep"))
    return jax.shard_map(
        per_device,
        mesh=mesh,
        in_specs=placed,
        out_specs=(P(None, ("rep", "gx"), "gy", "gz"), P(None, ("rep", "gx"), "gy", "gz")),
        check_vma=False,
    )
```

profile of v0, /device:TPU:0, one launch (start us, length us, event | category | flops | bytes accessed | tf_op | source)
XLA Modules:
  0.0 103.8 jit_solution(3377234256959573339)
XLA Ops:
  0.6 0.9 fusion.74
  1.6 3.1 %collective-permute-start = (f32[9,1,16,128]{3,2,1,0:T(8,128)S(1)}, f32[9,1,16,128]{3,2,1,0:T(8,128)S(1)}, u32[]{:S(2)}, u32[]{:S(2)}) collective-permute-start(f32[9,1,16,128]{3,2,1,0:T(8,128)S(1)} %get-tuple-element.134), channel_id=1, source_target_pairs={{0,4},{4,8},{8,12},{12,0},{1,5},{5,9},{9,13},{13,1},{2,6},{6,10},{... | collective-permute-start | bytes 221192 | tf_op jit(solution)/shard_map/ppermute | solution.py:22
  4.6 2.1 %collective-permute-start.1 = (f32[9,1,16,128]{3,2,1,0:T(8,128)S(1)}, f32[9,1,16,128]{3,2,1,0:T(8,128)S(1)}, u32[]{:S(2)}, u32[]{:S(2)}) collective-permute-start(f32[9,1,16,128]{3,2,1,0:T(8,128)S(1)} %get-tuple-element.133), channel_id=1, source_target_pairs={{4,0},{8,4},{12,8},{0,12},{5,1},{9,5},{13,9},{1,13},{6,2},{10,6},{... | collective-permute-start | bytes 221192 | tf_op jit(solution)/shard_map/ppermute | solution.py:23
  6.9 0.7 fusion.17
  7.7 1.6 %collective-permute-done = f32[9,1,16,128]{3,2,1,0:T(8,128)S(1)} collective-permute-done((f32[9,1,16,128]{3,2,1,0:T(8,128)S(1)}, f32[9,1,16,128]{3,2,1,0:T(8,128)S(1)}, u32[]{:S(2)}, u32[]{:S(2)}) %collective-permute-start) | collective-permute-done | bytes 73760 | tf_op jit(solution)/shard_map/ppermute | solution.py:22
  9.2 0.9 constant_dynamic-update-slice_fusion.13
  10.3 2.0 %collective-permute-start.3 = (f32[9,4,1,128]{3,0,2,1:T(8,128)S(1)}, f32[9,4,1,128]{3,0,2,1:T(8,128)S(1)}, u32[]{:S(2)}, u32[]{:S(2)}) collective-permute-start(f32[9,4,1,128]{3,0,2,1:T(8,128)S(1)} %copy.40), channel_id=1, source_target_pairs={{2,0},{0,2},{3,1},{1,3},{6,4},{4,6},{7,5},{5,7},{10,8},{8,10},{11,... | collective-permute-start | bytes 55304 | tf_op jit(solution)/shard_map/ppermute | solution.py:23
  12.4 0.1 fusion.24
  13.2 1.1 %collective-permute-done.3 = f32[9,4,1,128]{3,0,2,1:T(8,128)S(1)} collective-permute-done((f32[9,4,1,128]{3,0,2,1:T(8,128)S(1)}, f32[9,4,1,128]{3,0,2,1:T(8,128)S(1)}, u32[]{:S(2)}, u32[]{:S(2)}) %collective-permute-start.3) | collective-permute-done | bytes 18464 | tf_op jit(solution)/shard_map/ppermute | solution.py:23
  14.3 1.9 %collective-permute-done.2 = f32[9,4,1,128]{3,0,2,1:T(8,128)S(1)} collective-permute-done((f32[9,4,1,128]{3,0,2,1:T(8,128)S(1)}, f32[9,4,1,128]{3,0,2,1:T(8,128)S(1)}, u32[]{:S(2)}, u32[]{:S(2)}) %collective-permute-start.2) | collective-permute-done | bytes 18464 | tf_op jit(solution)/shard_map/ppermute | solution.py:22
  16.3 0.2 fusion.72
  16.6 0.5 collective-permute-start.4
  17.1 2.4 %collective-permute-start.7 = (f32[18,2,16,128]{3,2,1,0:T(8,128)S(1)}, f32[18,2,16,128]{3,2,1,0:T(8,128)S(1)}, u32[]{:S(2)}, u32[]{:S(2)}) collective-permute-start(f32[18,2,16,128]{3,2,1,0:T(8,128)S(1)} %constant_dynamic-update-slice_fusion.12), channel_id=1, source_target_pairs={{4,0},{8,4},{12,8},{0,12},{5,1},{9,5},{13,9},{1,13},{6,2},{10,6},{... | collective-permute-start | bytes 884744 | tf_op jit(solution)/shard_map/ppermute | solution.py:23
  19.5 0.6 maximum_select_fusion.1
  20.1 0.3 slice_add_fusion.2
  20.5 0.1 fusion.27
  20.6 0.2 copy-done.11
  20.8 0.1 fusion.8
  20.9 0.2 fusion.20
  21.1 0.7 constant_dynamic-update-slice_fusion.11
  21.8 0.7 constant_dynamic-update-slice_fusion.10
  22.5 0.7 constant_dynamic-update-slice_fusion.9
  23.1 0.7 constant_dynamic-update-slice_fusion.8
  23.8 0.7 constant_dynamic-update-slice_fusion.7
  24.5 0.7 constant_dynamic-update-slice_fusion.6
  25.2 1.7 %collective-permute-done.7 = f32[18,2,16,128]{3,2,1,0:T(8,128)S(1)} collective-permute-done((f32[18,2,16,128]{3,2,1,0:T(8,128)S(1)}, f32[18,2,16,128]{3,2,1,0:T(8,128)S(1)}, u32[]{:S(2)}, u32[]{:S(2)}) %collective-permute-start.7) | collective-permute-done | bytes 294944 | tf_op jit(solution)/shard_map/ppermute | solution.py:23
  26.9 6.1 %collective-permute-done.6 = f32[18,2,16,128]{3,2,1,0:T(8,128)S(1)} collective-permute-done((f32[18,2,16,128]{3,2,1,0:T(8,128)S(1)}, f32[18,2,16,128]{3,2,1,0:T(8,128)S(1)}, u32[]{:S(2)}, u32[]{:S(2)}) %collective-permute-start.6) | collective-permute-done | bytes 294944 | tf_op jit(solution)/shard_map/ppermute | solution.py:22
  33.3 0.4 collective-permute-start.9
  33.7 1.7 %collective-permute-start.8 = (f32[18,6,2,128]{3,1,2,0:T(8,128)S(1)}, f32[18,6,2,128]{3,1,2,0:T(8,128)S(1)}, u32[]{:S(2)}, u32[]{:S(2)}) collective-permute-start(f32[18,6,2,128]{3,1,2,0:T(8,128)S(1)} %copy.41), channel_id=1, source_target_pairs={{0,2},{2,0},{1,3},{3,1},{4,6},{6,4},{5,7},{7,5},{8,10},{10,8},{9,1... | collective-permute-start | bytes 331784 | tf_op jit(solution)/shard_map/ppermute | solution.py:22
  35.4 0.7 constant_dynamic-update-slice_fusion.5
  36.1 5.2 %copy.34 = f32[18,6,16,128]{2,1,3,0:T(8,128)} copy(f32[18,6,16,128]{3,2,1,0:T(8,128)S(1)} %pad_maximum_fusion.1) | data formatting | bytes 1769472 | tf_op jit(solution)/shard_map/concatenate | solution.py:24
  41.3 5.2 %copy.35 = f32[18,6,2,128]{2,1,3,0:T(8,128)} copy(f32[18,6,2,128]{3,1,2,0:T(8,128)S(1)} %collective-permute-done.9) | data formatting | bytes 221184 | tf_op jit(solution)/shard_map/ppermute | solution.py:23
  46.5 5.2 %copy.33 = f32[18,6,2,128]{2,1,3,0:T(8,128)} copy(f32[18,6,2,128]{3,1,2,0:T(8,128)S(1)} %collective-permute-done.8) | data formatting | bytes 221184 | tf_op jit(solution)/shard_map/ppermute | solution.py:22
  51.6 11.1 %pad_maximum_fusion = f32[18,6,20,128]{2,1,3,0:T(8,128)S(1)} fusion(f32[18,6,2,128]{2,1,3,0:T(8,128)} %copy.35, f32[18,6,16,128]{2,1,3,0:T(8,128)} %copy.34, f32[18,6,2,128]{2,1,3,0:T(8,128)} %copy.33), kind=kLoop, calls=%fused_computation | loop fusion | flops 552960 | bytes 2211840 | tf_op jit(solution)/shard_map/concatenate | solution.py:24
  62.7 3.6 %copy-done = f32[18,6,20,128]{2,1,3,0:T(8,128)} copy-done((f32[18,6,20,128]{2,1,3,0:T(8,128)}, f32[18,6,20,128]{2,1,3,0:T(8,128)S(1)}, u32[]{:S(2)}) %copy-start) | copy-done | bytes 1105944
  66.5 0.5 collective-permute-start.10
  67.0 0.7 constant_dynamic-update-slice_fusion.4
  67.7 6.3 %copy.37 = f32[18,6,20,128]{3,2,1,0:T(8,128)} copy(f32[18,6,20,128]{2,1,3,0:T(8,128)} %copy-done) | data formatting | bytes 2211840 | tf_op jit(solution)/shard_map/concatenate | solution.py:24
  74.0 1.9 %copy.38 = f32[18,6,20,2]{3,2,1,0:T(8,128)} copy(f32[18,6,20,2]{2,1,3,0:T(8,128)S(1)} %collective-permute-done.11) | data formatting | bytes 34560 | tf_op jit(solution)/shard_map/ppermute | solution.py:23
  75.9 1.8 %copy.36 = f32[18,6,20,2]{3,2,1,0:T(8,128)} copy(f32[18,6,20,2]{2,1,3,0:T(8,128)S(1)} %collective-permute-done.10) | data formatting | bytes 34560 | tf_op jit(solution)/shard_map/ppermute | solution.py:22
  77.7 3.2 %maximum_select_fusion = f32[18,6,20,132]{3,2,1,0:T(8,128)S(1)} fusion(f32[18,6,20,2]{3,2,1,0:T(8,128)} %copy.38, f32[18,6,20,128]{3,2,1,0:T(8,128)} %copy.37, f32[18,6,20,2]{3,2,1,0:T(8,128)} %copy.36, pred[6,20,132]{2,1,0:T(8,128)(4,1)} %fusion.17), kind=kLoop, calls=%fused_computation.1 | loop fusion | flops 855360 | bytes 2296800 | tf_op jit(solution)/shard_map/jit(_where)/select_n | solution.py:93
  80.9 1.2 %slice.682 = f32[9,6,20,132]{3,2,1,0:T(8,128)} slice(f32[18,6,20,132]{3,2,1,0:T(8,128)S(1)} %maximum_select_fusion), slice={[0:9], [0:6], [0:20], [0:132]} | slice | bytes 1140480 | tf_op jit(solution)/shard_map/slice | solution.py:104
  82.1 7.2 %scatter.4 = f32[9,6,20,132]{3,2,1,0:T(8,128)} dynamic-update-slice(f32[9,6,20,132]{3,2,1,0:T(8,128)} %slice.682, f32[9,2,16,128]{3,2,1,0:T(8,128)} %param.7, s32[]{:T(128)} %constant.37.clone.1, s32[]{:T(128)} %constant.84.clone.1, s32[]{:T(128)} %constant.84.clone.1, s32[]{:T(128)} %constant.84.clone.1) | dynamic-update-slice | bytes 294916 | tf_op jit(solution)/shard_map/jvp()/scatter | solution.py:108
  89.3 1.6 %slice_multiply_fusion.35 = (f32[1,4,18,130]{3,2,1,0:T(8,128)S(1)}, f32[1,4,18,130]{3,2,1,0:T(8,128)S(1)}, f32[1,4,18,130]{3,2,1,0:T(8,128)S(1)}, f32[1,4,18,130...) fusion(f32[9,6,20,132]{3,2,1,0:T(8,128)} %scatter.4, ...), kind=kLoop, calls=%fused_computation.121 | loop fusion | flops 84240 | bytes 936004 | tf_op jit(solution)/shard_map/transpose(jvp())/mul | solution.py:68
  90.9 0.5 fusion.14
  91.3 0.3 fusion.28
  91.7 0.3 slice_multiply_fusion.37
  92.1 0.3 slice_multiply_fusion.38
  92.4 0.2 slice_multiply_fusion.17
  92.6 0.2 slice_multiply_fusion.23
  92.9 0.2 slice_multiply_fusion.29
  93.1 0.4 fusion.61
  93.5 1.2 %broadcast_multiply_fusion = (f32[6,6,20,132]{3,2,1,0:T(8,128)S(1)}, f32[6,6,20,132]{3,2,1,0:T(8,128)S(1)}) fusion(f32[6,20,132]{2,1,0:T(8,128)S(1)} %multiply_bitcast_fusion, f32[6,4,18,130]{3,2,1,0:T(8,128)S(1)} %get-tuple-element.126, f32[6,4,18,130]{3,2,1,0:T(8,128)S(1)} %get-tuple-element.125, f32[6,4,18,130]{3,2,1,0:T(8,128)S(1)} %get-tuple-element.127, ...), kind=kLoop, calls=%fused_computation.32 | loop fusion | flops 665280 | bytes 2396160 | tf_op jit(solution)/shard_map/transpose(jvp())/mul | solution.py:50
  94.7 0.1 fusion.6
  95.0 0.2 pad_add_fusion.4
  95.2 0.2 fusion.64
  95.4 0.3 pad_add_fusion.5
  95.8 0.3 pad_add_fusion
  96.1 0.7 fusion.5
  96.8 0.3 pad_add_fusion.7
  97.1 0.4 collective-permute-start.12
  97.6 1.5 %constant_dynamic-update-slice_fusion.3 = f32[9,2,16,128]{3,2,1,0:T(8,128)} fusion(f32[9,2,16,128]{3,2,1,0:T(8,128)} %constant_dynamic-update-slice_fusion.4, f32[6,4,18,130]{3,2,1,0:T(8,128)} %copy-done.2, f32[9,2,16,128]{3,2,1,0:T(8,128)} %copy-done.9, f32[3,2,16,128]{3,2,1,0:T(8,128)S(1)} %copy-done.8, f32[3,2,16,128]{3,2,1,0:T(8,128)S(1)} %copy-done.6, ...), kind=kLoop, calls=%fused_computation.167 | loop fusion | flops 65536 | bytes 229888 | tf_op jit(solution)/shard_map/stack | solution.py:71
  99.1 3.9 %collective-permute-done.12 = f32[9,2,16,128]{3,2,1,0:T(8,128)S(1)} collective-permute-done((f32[9,2,16,128]{3,2,1,0:T(8,128)S(1)}, f32[9,2,16,128]{3,2,1,0:T(8,128)S(1)}, u32[]{:S(2)}, u32[]{:S(2)}) %collective-permute-start.12) | collective-permute-done | bytes 147488 | tf_op jit(solution)/shard_map/ppermute | solution.py:29
  103.0 0.7 add_multiply_fusion.3
  (66 shorter events, 1.2 us)
Async XLA Ops:
  1.6 7.7 %collective-permute-start = (f32[9,1,16,128]{3,2,1,0:T(8,128)S(1)}, f32[9,1,16,128]{3,2,1,0:T(8,128)S(1)}, u32[]{:S(2)}, u32[]{:S(2)}) collective-permute-start(f32[9,1,16,128]{3,2,1,0:T(8,128)S(1)} %get-tuple-element.134), channel_id=1, source_target_pairs={{0,4},{4,8},{8,12},{12,0},{1,5},{5,9},{9,13},{13,1},{2,6},{6,10},{... | collective-permute-start | bytes 221192 | tf_op jit(solution)/shard_map/ppermute | solution.py:22
  4.6 5.5 %collective-permute-start.1 = (f32[9,1,16,128]{3,2,1,0:T(8,128)S(1)}, f32[9,1,16,128]{3,2,1,0:T(8,128)S(1)}, u32[]{:S(2)}, u32[]{:S(2)}) collective-permute-start(f32[9,1,16,128]{3,2,1,0:T(8,128)S(1)} %get-tuple-element.133), channel_id=1, source_target_pairs={{4,0},{8,4},{12,8},{0,12},{5,1},{9,5},{13,9},{1,13},{6,2},{10,6},{... | collective-permute-start | bytes 221192 | tf_op jit(solution)/shard_map/ppermute | solution.py:23
  10.3 4.0 %collective-permute-start.3 = (f32[9,4,1,128]{3,0,2,1:T(8,128)S(1)}, f32[9,4,1,128]{3,0,2,1:T(8,128)S(1)}, u32[]{:S(2)}, u32[]{:S(2)}) collective-permute-start(f32[9,4,1,128]{3,0,2,1:T(8,128)S(1)} %copy.40), channel_id=1, source_target_pairs={{2,0},{0,2},{3,1},{1,3},{6,4},{4,6},{7,5},{5,7},{10,8},{8,10},{11,... | collective-permute-start | bytes 55304 | tf_op jit(solution)/shard_map/ppermute | solution.py:23
  12.3 3.9 %collective-permute-start.2 = (f32[9,4,1,128]{3,0,2,1:T(8,128)S(1)}, f32[9,4,1,128]{3,0,2,1:T(8,128)S(1)}, u32[]{:S(2)}, u32[]{:S(2)}) collective-permute-start(f32[9,4,1,128]{3,0,2,1:T(8,128)S(1)} %copy.39), channel_id=1, source_target_pairs={{0,2},{2,0},{1,3},{3,1},{4,6},{6,4},{5,7},{7,5},{8,10},{10,8},{9,1... | collective-permute-start | bytes 55304 | tf_op jit(solution)/shard_map/ppermute | solution.py:22
  13.1 3.9 %copy-start.10 = (f32[9,2,16,128]{3,2,1,0:T(8,128)S(1)}, f32[9,2,16,128]{3,2,1,0:T(8,128)}, u32[]{:S(2)}) copy-start(f32[9,2,16,128]{3,2,1,0:T(8,128)} %param.8) | copy-start | bytes 442372
  16.5 3.0 %collective-permute-start.5 = (f32[9,4,18,1]{3,2,1,0:T(8,128)S(1)}, f32[9,4,18,1]{3,2,1,0:T(8,128)S(1)}, u32[]{:S(2)}, u32[]{:S(2)}) collective-permute-start(f32[9,4,18,1]{3,2,1,0:T(8,128)S(1)} %get-tuple-element.122), channel_id=1, source_target_pairs={{1,0},{0,1},{3,2},{2,3},{5,4},{4,5},{7,6},{6,7},{9,8},{8,9},{11,10... | collective-permute-start | bytes 7784 | tf_op jit(solution)/shard_map/ppermute | solution.py:23
  16.6 2.9 %collective-permute-start.4 = (f32[9,4,18,1]{3,2,1,0:T(8,128)S(1)}, f32[9,4,18,1]{3,2,1,0:T(8,128)S(1)}, u32[]{:S(2)}, u32[]{:S(2)}) collective-permute-start(f32[9,4,18,1]{3,2,1,0:T(8,128)S(1)} %get-tuple-element.121), channel_id=1, source_target_pairs={{0,1},{1,0},{2,3},{3,2},{4,5},{5,4},{6,7},{7,6},{8,9},{9,8},{10,11... | collective-permute-start | bytes 7784 | tf_op jit(solution)/shard_map/ppermute | solution.py:22
  17.1 9.8 %collective-permute-start.7 = (f32[18,2,16,128]{3,2,1,0:T(8,128)S(1)}, f32[18,2,16,128]{3,2,1,0:T(8,128)S(1)}, u32[]{:S(2)}, u32[]{:S(2)}) collective-permute-start(f32[18,2,16,128]{3,2,1,0:T(8,128)S(1)} %constant_dynamic-update-slice_fusion.12), channel_id=1, source_target_pairs={{4,0},{8,4},{12,8},{0,12},{5,1},{9,5},{13,9},{1,13},{6,2},{10,6},{... | collective-permute-start | bytes 884744 | tf_op jit(solution)/shard_map/ppermute | solution.py:23
  19.5 13.6 %collective-permute-start.6 = (f32[18,2,16,128]{3,2,1,0:T(8,128)S(1)}, f32[18,2,16,128]{3,2,1,0:T(8,128)S(1)}, u32[]{:S(2)}, u32[]{:S(2)}) collective-permute-start(f32[18,2,16,128]{3,2,1,0:T(8,128)S(1)} %constant_dynamic-update-slice_fusion.12), channel_id=1, source_target_pairs={{0,4},{4,8},{8,12},{12,0},{1,5},{5,9},{9,13},{13,1},{2,6},{6,10},{... | collective-permute-start | bytes 884744 | tf_op jit(solution)/shard_map/ppermute | solution.py:22
  20.1 0.7 copy-start.11
  20.4 46.5 %copy-start.9 = (f32[9,2,16,128]{3,2,1,0:T(8,128)}, f32[9,2,16,128]{3,2,1,0:T(8,128)S(1)}, u32[]{:S(2)}) copy-start(f32[9,2,16,128]{3,2,1,0:T(8,128)S(1)} %slice_add_fusion.2) | copy-start | bytes 442372
  20.8 46.2 %copy-start.3 = (f32[3,2,16,128]{3,2,1,0:T(8,128)}, f32[3,2,16,128]{3,2,1,0:T(8,128)S(1)}, u32[]{:S(2)}) copy-start(f32[3,2,16,128]{3,2,1,0:T(8,128)S(1)} %get-tuple-element.115) | copy-start | bytes 147460
  20.8 46.2 %copy-start.5 = (f32[3,2,16,128]{3,2,1,0:T(8,128)}, f32[3,2,16,128]{3,2,1,0:T(8,128)S(1)}, u32[]{:S(2)}) copy-start(f32[3,2,16,128]{3,2,1,0:T(8,128)S(1)} %get-tuple-element.116) | copy-start | bytes 147460
  20.8 46.2 %copy-start.7 = (f32[3,2,16,128]{3,2,1,0:T(8,128)}, f32[3,2,16,128]{3,2,1,0:T(8,128)S(1)}, u32[]{:S(2)}) copy-start(f32[3,2,16,128]{3,2,1,0:T(8,128)S(1)} %get-tuple-element.117) | copy-start | bytes 147460
  20.9 46.1 %copy-start.2 = (f32[6,4,18,130]{3,2,1,0:T(8,128)}, f32[6,4,18,130]{3,2,1,0:T(8,128)S(1)}, u32[]{:S(2)}) copy-start(f32[6,4,18,130]{3,2,1,0:T(8,128)S(1)} %fusion.8) | copy-start | bytes 673924
  33.3 8.1 %collective-permute-start.9 = (f32[18,6,2,128]{3,1,2,0:T(8,128)S(1)}, f32[18,6,2,128]{3,1,2,0:T(8,128)S(1)}, u32[]{:S(2)}, u32[]{:S(2)}) collective-permute-start(f32[18,6,2,128]{3,1,2,0:T(8,128)S(1)} %copy.42), channel_id=1, source_target_pairs={{2,0},{0,2},{3,1},{1,3},{6,4},{4,6},{7,5},{5,7},{10,8},{8,10},{11,... | collective-permute-start | bytes 331784 | tf_op jit(solution)/shard_map/ppermute | solution.py:23
  33.7 12.8 %collective-permute-start.8 = (f32[18,6,2,128]{3,1,2,0:T(8,128)S(1)}, f32[18,6,2,128]{3,1,2,0:T(8,128)S(1)}, u32[]{:S(2)}, u32[]{:S(2)}) collective-permute-start(f32[18,6,2,128]{3,1,2,0:T(8,128)S(1)} %copy.41), channel_id=1, source_target_pairs={{0,2},{2,0},{1,3},{3,1},{4,6},{6,4},{5,7},{7,5},{8,10},{10,8},{9,1... | collective-permute-start | bytes 331784 | tf_op jit(solution)/shard_map/ppermute | solution.py:22
  62.7 3.6 %copy-start = (f32[18,6,20,128]{2,1,3,0:T(8,128)}, f32[18,6,20,128]{2,1,3,0:T(8,128)S(1)}, u32[]{:S(2)}) copy-start(f32[18,6,20,128]{2,1,3,0:T(8,128)S(1)} %pad_maximum_fusion) | copy-start | bytes 3317764
  66.4 7.6 %collective-permute-start.11 = (f32[18,6,20,2]{2,1,3,0:T(8,128)S(1)}, f32[18,6,20,2]{2,1,3,0:T(8,128)S(1)}, u32[]{:S(2)}, u32[]{:S(2)}) collective-permute-start(f32[18,6,20,2]{2,1,3,0:T(8,128)S(1)} %get-tuple-element.31), channel_id=1, source_target_pairs={{1,0},{0,1},{3,2},{2,3},{5,4},{4,5},{7,6},{6,7},{9,8},{8,9},{11,10... | collective-permute-start | bytes 51848 | tf_op jit(solution)/shard_map/ppermute | solution.py:23
  66.5 9.4 %collective-permute-start.10 = (f32[18,6,20,2]{2,1,3,0:T(8,128)S(1)}, f32[18,6,20,2]{2,1,3,0:T(8,128)S(1)}, u32[]{:S(2)}, u32[]{:S(2)}) collective-permute-start(f32[18,6,20,2]{2,1,3,0:T(8,128)S(1)} %get-tuple-element.30), channel_id=1, source_target_pairs={{0,1},{1,0},{2,3},{3,2},{4,5},{5,4},{6,7},{7,6},{8,9},{9,8},{10,11... | collective-permute-start | bytes 51848 | tf_op jit(solution)/shard_map/ppermute | solution.py:22
  89.3 1.6 %copy-start.1 = (f32[9,6,20,132]{3,2,1,0:T(8,128)S(1)}, f32[9,6,20,132]{3,2,1,0:T(8,128)}, u32[]{:S(2)}) copy-start(f32[9,6,20,132]{3,2,1,0:T(8,128)} %scatter.4) | copy-start | bytes 1710724
  96.8 0.8 copy-start.4
  96.8 0.8 copy-start.6
  96.8 0.8 copy-start.8
  96.8 6.3 %copy-start.12 = (f32[9]{0:T(128)S(1)}, f32[9]{0:T(128)}, u32[]{:S(2)}) copy-start(f32[9]{0:T(128)} %constant.97.clone) | copy-start | bytes 112
  97.1 5.9 %collective-permute-start.12 = (f32[9,2,16,128]{3,2,1,0:T(8,128)S(1)}, f32[9,2,16,128]{3,2,1,0:T(8,128)S(1)}, u32[]{:S(2)}, u32[]{:S(2)}) collective-permute-start(f32[9,2,16,128]{3,2,1,0:T(8,128)S(1)} %pad_add_fusion.7), channel_id=1, source_target_pairs={{0,2},{2,0},{1,3},{3,1},{4,6},{6,4},{5,7},{7,5},{8,10},{10,8},{9,1... | collective-permute-start | bytes 442376 | tf_op jit(solution)/shard_map/ppermute | solution.py:29
where the time goes:
time: 104 us
  local copies, waits for them, and re-layouts  40 us (38%)
  other arithmetic  32.2 us (31%)
  waiting for transfers between devices  16.4 us (16%)
  starting transfers between devices  13.4 us (13%)
  between operations  1.8 us (2%)
    concatenate x3, local copies, waits for them, and re-layouts, padded_2(): array = jnp.concatenate([before, array, after], axis=dim)  11.5 us
    concatenate x3, other arithmetic, padded_2(): array = jnp.concatenate([before, array, after], axis=dim)  11.2 us
    ppermute x6, waiting for transfers between devices, padded_2(): before = lax.ppermute(last, axis, up)  9.67 us
    scatter x1, local copies, waits for them, and re-layouts, extended(): full = outer.at[:, 2:-2, 2:-2, 2:-2].set(inner)  7.16 us
    ppermute x6, starting transfers between devices, padded_2(): after = lax.ppermute(leading, axis, down)  7.12 us
    ppermute x3, local copies, waits for them, and re-layouts, padded_2(): after = lax.ppermute(leading, axis, down)  7.04 us
    ppermute x3, local copies, waits for them, and re-layouts, padded_2(): before = lax.ppermute(last, axis, up)  7 us
    ppermute x6, starting transfers between devices, padded_2(): before = lax.ppermute(last, axis, up)  5.87 us
  transfers between devices with their start and end apart: 13, of which 6 were waited for; matrix products, arithmetic and copies ran while one was open for 28% of the time, Pallas kernels for 0%

commit v1 on v0

v1 whole, which is shorter than its diff:
```python
import jax
import jax.numpy as jnp
from jax import lax
from jax.experimental import pallas as pl
from jax.experimental.pallas import tpu as pltpu
from jax.sharding import PartitionSpec as P

VISCOSITY = 0.5
DIFFUSIVITY = 0.2
EXTENSIBILITY = 100.0
HORIZON = 1.0
COMP = ((0, 3, 4), (3, 1, 5), (4, 5, 2))
PAIRS = ((0, 0), (1, 1), (2, 2), (0, 1), (0, 2), (1, 2))
SIGNS = (1.0, -1.0, 1.0, 1.0, 1.0, 1.0, -1.0, 1.0, -1.0)


def swap_even(array, axis):
    size = lax.axis_size(axis)
    return lax.ppermute(array, axis, [(i, i ^ 1) for i in range(size)])


def swap_odd(array, axis):
    size = lax.axis_size(axis)
    pairs = [(i, (i + 1) % size if i % 2 else (i - 1) % size) for i in range(size)]
    return lax.ppermute(array, axis, pairs)


def exchange_x(first, last):
    size = lax.axis_size("gx")
    if size % 2:
        below = lax.ppermute(last, "gx", [(i, (i + 1) % size) for i in range(size)])
        above = lax.ppermute(first, "gx", [((i + 1) % size, i) for i in range(size)])
        return below, above
    even = lax.axis_index("gx") % 2 == 0
    far = swap_odd(jnp.where(even, first, last), "gx")
    near = swap_even(jnp.where(even, last, first), "gx")
    return far, near


def neighbours_y(brick):
    size = lax.axis_size("gy")
    if size == 1:
        return brick
    if size == 2:
        return swap_even(brick, "gy")
    below = lax.ppermute(brick, "gy", [(i, i + 1) for i in range(size - 1)])
    above = lax.ppermute(brick, "gy", [(i + 1, i) for i in range(size - 1)])
    half = brick.shape[2] // 2
    return jnp.concatenate([above[:, :, :half], below[:, :, half:]], axis=2)


def neighbours_z(brick):
    size = lax.axis_size("gz")
    if size == 1:
        return brick
    if size == 2:
        return swap_even(brick, "gz")
    below = lax.ppermute(brick, "gz", [(i, (i + 1) % size) for i in range(size)])
    above = lax.ppermute(brick, "gz", [((i + 1) % size, i) for i in range(size)])
    half = brick.shape[3] // 2
    return jnp.concatenate([above[..., :half], below[..., half:]], axis=3)


class Shifts:
    def __init__(self, rows, lanes):
        self.rows, self.lanes = rows, lanes
        self.row = lax.broadcasted_iota(jnp.int32, (rows, lanes), 0)
        self.lane = lax.broadcasted_iota(jnp.int32, (rows, lanes), 1)
        wall, walls = lax.axis_index("gy"), lax.axis_size("gy")
        self.beyond = ((self.row == 0) & (wall == walls - 1)) | ((self.row == rows - 1) & (wall == 0))

    def clean(self, edge):
        return jnp.where(self.beyond, 0.0, edge)

    def y(self, plane, edge):
        up = pltpu.roll(jnp.where(self.row == 0, edge, plane), self.rows - 1, 0)
        down = pltpu.roll(jnp.where(self.row == self.rows - 1, edge, plane), 1, 0)
        return up, down

    def z(self, plane, edge):
        up = pltpu.roll(jnp.where(self.lane == 0, edge, plane), self.lanes - 1, 1)
        down = pltpu.roll(jnp.where(self.lane == self.lanes - 1, edge, plane), 1, 1)
        return up, down


def stretch_pull(conf, dual, column):
    out = []
    for m in range(3):
        total = 0.0
        for j in range(3):
            term = dual[COMP[m][j]] * conf[COMP[j][column]]
            total = total + (term + term if j == m else term)
        out.append(total)
    return out


def half_factor(conf):
    return (0.5 * (EXTENSIBILITY - 3.0)) / (EXTENSIBILITY - (conf[0] + conf[1] + conf[2]))


def pick_x(far_ref, near_ref, field):
    far, near = far_ref[field], near_ref[field]
    if lax.axis_size("gx") % 2:
        return far, near
    even = jnp.full(far.shape, lax.axis_index("gx") % 2, jnp.int32) == 0
    return jnp.where(even, far, near), jnp.where(even, near, far)


def halo_planes(ref, offset, far_ref, near_ref, count):
    fields = []
    for f in range(count):
        below, above = pick_x(far_ref, near_ref, offset + f)
        fields.append([below] + [ref[f, p] for p in range(ref.shape[1])] + [above])
    return fields


def raw_kernel(steps_ref, seed_ref, dual_ref, far_ref, near_ref, ys_ref, yd_ref, zs_ref, zd_ref, raw_ref):
    _, depth, rows, lanes = seed_ref.shape
    shift = Shifts(rows, lanes)
    time_step = HORIZON / jnp.full((rows, lanes), steps_ref[0], jnp.int32).astype(jnp.float32)
    seed = halo_planes(seed_ref, 0, far_ref, near_ref, 9)
    dual = halo_planes(dual_ref, 9, far_ref, near_ref, 9)
    pull_x = [
        stretch_pull([c[p] for c in seed[3:]], [c[p] for c in dual[3:]], 0) for p in range(depth + 2)
    ]
    for p in range(depth):
        at = p + 1
        conf = [c[at] for c in seed[3:]]
        pulled = [c[at] for c in dual[3:]]
        ey = [shift.clean(yd_ref[f, p]) for f in range(9)]
        ez = [zd_ref[f, p] for f in range(9)]
        eys = [shift.clean(ys_ref[f, p]) for f in range(9)]
        ezs = [zs_ref[f, p] for f in range(9)]
        laps, slopes = [], []
        for f in range(9):
            here = dual[f][at]
            yu, yd = shift.y(here, ey[f])
            zu, zd = shift.z(here, ez[f])
            xu, xd = dual[f][at + 1], dual[f][at - 1]
            laps.append((xu + xd) + (yu + yd) + (zu + zd) - 6.0 * here)
            if f < 3:
                slopes.append((0.5 * (xu - xd), 0.5 * (yu - yd), 0.5 * (zu - zd)))
        grads = []
        for f in range(3):
            here = seed[f][at]
            yu, yd = shift.y(here, eys[f])
            zu, zd = shift.z(here, ezs[f])
            xu, xd = seed[f][at + 1], seed[f][at - 1]
            grads.append((0.5 * (xu - xd), 0.5 * (yu - yd), 0.5 * (zu - zd)))
        pull_y = stretch_pull(conf, pulled, 1)
        pull_z = stretch_pull(conf, pulled, 2)
        edge_y = stretch_pull(eys[3:], ey[3:], 1)
        edge_z = stretch_pull(ezs[3:], ez[3:], 2)
        for m in range(3):
            yu, yd = shift.y(pull_y[m], edge_y[m])
            zu, zd = shift.z(pull_z[m], edge_z[m])
            flux = (pull_x[at + 1][m] - pull_x[at - 1][m]) + (yu - yd) + (zu - zd)
            raw_ref[m, p] = dual[m][at] + time_step * (VISCOSITY * laps[m] - 0.5 * flux)
        half = half_factor(conf)
        stress = []
        for n, (i, j) in enumerate(PAIRS):
            slope = slopes[i][j] if i == j else slopes[i][j] + slopes[j][i]
            stress.append(-(slope + pulled[n]))
        inner = 0.0
        for n in range(6):
            inner = inner + stress[n] * conf[n]
        inner = inner * (half * half) * (2.0 / (EXTENSIBILITY - 3.0))

        def weight(k, j):
            total = 0.0
            for m in range(3):
                term = grads[m][k] * pulled[COMP[m][j]]
                total = total + (term + term if m == j else term)
            return total

        for n, (i, j) in enumerate(PAIRS):
            change = DIFFUSIVITY * laps[3 + n] + half * stress[n]
            change = change + (weight(i, i) + inner if i == j else weight(i, j) + weight(j, i))
            raw_ref[3 + n, p] = pulled[n] + time_step * change


def next_kernel(steps_ref, seed_ref, far_ref, near_ref, ys_ref, zs_ref, next_ref):
    _, depth, rows, lanes = seed_ref.shape
    shift = Shifts(rows, lanes)
    time_step = HORIZON / jnp.full((rows, lanes), steps_ref[0], jnp.int32).astype(jnp.float32)
    seed = halo_planes(seed_ref, 0, far_ref, near_ref, 9)
    halves = [half_factor([c[p] for c in seed[3:]]) for p in range(depth + 2)]
    for p in range(depth):
        at = p + 1
        conf = [c[at] for c in seed[3:]]
        ey = [shift.clean(ys_ref[f, p]) for f in range(9)]
        ez = [zs_ref[f, p] for f in range(9)]
        laps, grads = [], []
        for f in range(9):
            here = seed[f][at]
            yu, yd = shift.y(here, ey[f])
            zu, zd = shift.z(here, ez[f])
            xu, xd = seed[f][at + 1], seed[f][at - 1]
            laps.append((xu + xd) + (yu + yd) + (zu + zd) - 6.0 * here)
            if f < 3:
                grads.append((0.5 * (xu - xd), 0.5 * (yu - yd), 0.5 * (zu - zd)))
        half = halves[at]
        half_y, half_z = half_factor(ey[3:]), half_factor(ez[3:])
        for i in range(3):
            cx, cy, cz = COMP[i]
            yu, yd = shift.y(half * conf[cy], half_y * ey[3 + cy])
            zu, zd = shift.z(half * conf[cz], half_z * ez[3 + cz])
            xu = halves[at + 1] * seed[3 + cx][at + 1]
            xd = halves[at - 1] * seed[3 + cx][at - 1]
            divergence = 0.5 * ((xu - xd) + (yu - yd) + (zu - zd))
            next_ref[i, p] = seed[i][at] + time_step * (VISCOSITY * laps[i] + divergence)
        for n, (i, j) in enumerate(PAIRS):
            stretch = 0.0
            for k in range(3):
                term = grads[i][k] * conf[COMP[k][j]]
                stretch = stretch + (term + term if i == j else term + grads[j][k] * conf[COMP[k][i]])
            stress = half * conf[n] - (0.5 if i == j else 0.0)
            next_ref[3 + n, p] = conf[n] + time_step * (DIFFUSIVITY * laps[3 + n] + stretch - stress)


def call(kernel, shape, steps, *arrays):
    vmem = pl.BlockSpec(memory_space=pltpu.VMEM)
    return pl.pallas_call(
        kernel,
        out_shape=jax.ShapeDtypeStruct(shape, jnp.float32),
        in_specs=[pl.BlockSpec(memory_space=pltpu.SMEM)] + [vmem] * len(arrays),
        out_specs=vmem,
        cost_estimate=pl.CostEstimate(flops=4_000_000, bytes_accessed=1_000_000, transcendentals=0),
        compiler_params=pltpu.CompilerParams(vmem_limit_bytes=16 * 1024 * 1024),
    )(steps, *arrays)


def per_device(seed_state, costate, step_count):
    first = jnp.concatenate([seed_state[:, 0], costate[:, 0]], 0)
    last = jnp.concatenate([seed_state[:, -1], costate[:, -1]], 0)
    far, near = exchange_x(first, last)
    ys, yd = neighbours_y(seed_state), neighbours_y(costate)
    zs, zd = neighbours_z(seed_state), neighbours_z(costate)
    raw = call(raw_kernel, seed_state.shape, step_count, seed_state, costate, far, near, ys, yd, zs, zd)
    walls = lax.axis_size("gy")
    partner = lax.ppermute(raw, "gy", [(i, walls - 1 - i) for i in range(walls)])
    next_state = call(next_kernel, seed_state.shape, step_count, seed_state, far, near, ys, zs)
    signs = jnp.array(SIGNS, jnp.float32)[:, None, None, None]
    seed_gradient = 0.5 * (raw + jnp.flip(partner, axis=2) * signs)
    return next_state, seed_gradient


def solution(mesh):
    placed = P(None, ("rep", "gx"), "gy", "gz")
    return jax.shard_map(
        per_device,
        mesh=mesh,
        in_specs=(placed, placed, P("rep")),
        out_specs=(placed, placed),
        check_vma=False,
    )
```

time: 104 us -> 22.2 us (0.21)
  local copies, waits for them, and re-layouts: 40 us -> 1.02 us
  other arithmetic: 32.2 us -> 0.77 us
  waiting for transfers between devices: 16.4 us -> 8.92 us
  starting transfers between devices: 13.4 us -> 8.77 us
  Pallas kernels: 0 us -> 1.16 us
    ppermute x6 -> x0, local copies, waits for them, and re-layouts: 14 us -> none  [the longest x3 7.04 us: padded_2(): after = lax.ppermute(leading, axis, down)]
    concatenate x4 -> x0, local copies, waits for them, and re-layouts: 11.5 us -> none  [the longest x3 11.5 us: padded_2(): array = jnp.concatenate([before, array, after], axis=dim)]
    concatenate x3 -> x0, other arithmetic: 11.2 us -> none  [padded_2(): array = jnp.concatenate([before, array, after], axis=dim)]
    ppermute x13 -> x7, waiting for transfers between devices: 16.4 us -> 8.92 us  [the longest x1 4.08 us: per_device(): lax.ppermute(raw, 'gy', [(i, walls - 1 - i) for i in range(walls)])]
    scatter x1 -> x0, local copies, waits for them, and re-layouts: 7.16 us -> none  [extended(): full = outer.at[:, 2:-2, 2:-2, 2:-2].set(inner)]
    unnamed x8 -> x0, other arithmetic: 5.54 us -> none
    mul x14 -> x1, other arithmetic: 5.74 us -> 0.75 us  [per_device(): seed_gradient = 0.5 * (raw + jnp.flip(partner, axis=2) * signs)]
    unnamed x32 -> x6, local copies, waits for them, and re-layouts: 4.87 us -> 0.01 us
  transfers between devices with their start and end apart: 13 -> 7, of which waited for: 6 -> 3; matrix products, arithmetic and copies ran while one was open for 28% -> 0% of each run, Pallas kernels for 0% -> 4%
where the time goes in v1:
time: 22.2 us; the launch traced here: 22 us
  waiting for transfers between devices  8.92 us (40%)
  starting transfers between devices  8.77 us (40%)
  between operations  1.36 us (6%)
  Pallas kernels  1.16 us (5%)
  local copies, waits for them, and re-layouts  1.02 us (5%)
  other arithmetic  0.77 us (3%)
    ppermute x5, starting transfers between devices, swap_even(): return lax.ppermute(array, axis, [(i, i ^ 1) for i in range(size)])  5.35 us
    ppermute x1, waiting for transfers between devices, per_device(): lax.ppermute(raw, 'gy', [(i, walls - 1 - i) for i in range(walls)])  4.08 us
    ppermute x1, waiting for transfers between devices, swap_odd(): return lax.ppermute(array, axis, pairs)  3.56 us
    ppermute x1, starting transfers between devices, swap_odd(): return lax.ppermute(array, axis, pairs)  2.83 us
    ppermute x5, waiting for transfers between devices, swap_even(): return lax.ppermute(array, axis, [(i, i ^ 1) for i in range(size)])  1.28 us
    pallas_call x2, Pallas kernels, call(): pl.pallas_call(kernel, out_shape=jax.ShapeDtypeStruct(shape, jnp.float32)...  1.16 us
    squeeze x2, local copies, waits for them, and re-layouts, per_device(): first = jnp.concatenate([seed_state[:, 0], costate[:, 0]], 0)  0.99 us
    mul x1, other arithmetic, per_device(): seed_gradient = 0.5 * (raw + jnp.flip(partner, axis=2) * signs)  0.75 us
  transfers between devices with their start and end apart: 7, of which 3 were waited for; matrix products, arithmetic and copies ran while one was open for 0% of the time, Pallas kernels for 4%

profile of v1, /device:TPU:0, one launch (start us, length us, event | category | flops | bytes accessed | tf_op | source)
XLA Modules:
  0.0 22.0 jit_solution(12746811986666756497)
XLA Ops:
  0.6 0.0 copy-start
  0.7 1.0 %slice_bitcast_fusion.2 = (f32[9,16,128]{2,1,0:T(8,128)S(1)}, f32[9,16,128]{2,1,0:T(8,128)S(1)}) fusion(f32[9,2,16,128]{3,2,1,0:T(8,128)} %dual_ref.1), kind=kLoop, calls=%fused_computation.7 | loop fusion | bytes 294912 | tf_op jit(solution)/shard_map/squeeze | solution.py:234
  1.6 0.0 copy-done
  1.7 0.0 copy-start.1
  1.7 3.1 %collective-permute-start.1 = (f32[18,16,128]{2,1,0:T(8,128)S(1)}, f32[18,16,128]{2,1,0:T(8,128)S(1)}, u32[]{:S(2)}, u32[]{:S(2)}) collective-permute-start(f32[18,16,128]{2,1,0:T(8,128)S(1)} %get-tuple-element.2), channel_id=1, source_target_pairs={{0,4},{4,0},{8,12},{12,8},{1,5},{5,1},{9,13},{13,9},{2,6},{6,2},{1... | collective-permute-start | bytes 442376 | tf_op jit(solution)/shard_map/ppermute | solution.py:19
  4.8 0.0 copy-done.1
  4.8 1.5 %collective-permute-start.4 = (f32[9,2,16,128]{3,2,1,0:T(8,128)S(1)}, f32[9,2,16,128]{3,2,1,0:T(8,128)S(1)}, u32[]{:S(2)}, u32[]{:S(2)}) collective-permute-start(f32[9,2,16,128]{3,2,1,0:T(8,128)S(1)} %copy-done.1), channel_id=1, source_target_pairs={{0,2},{2,0},{1,3},{3,1},{4,6},{6,4},{5,7},{7,5},{8,10},{10,8},{9,1... | collective-permute-start | bytes 442376 | tf_op jit(solution)/shard_map/ppermute | solution.py:19
  6.3 2.8 %collective-permute-start = (f32[18,16,128]{2,1,0:T(8,128)S(1)}, f32[18,16,128]{2,1,0:T(8,128)S(1)}, u32[]{:S(2)}, u32[]{:S(2)}) collective-permute-start(f32[18,16,128]{2,1,0:T(8,128)S(1)} %get-tuple-element.3), channel_id=1, source_target_pairs={{0,12},{4,8},{8,4},{12,0},{1,13},{5,9},{9,5},{13,1},{2,14},{6,10},... | collective-permute-start | bytes 442376 | tf_op jit(solution)/shard_map/ppermute | solution.py:25
  9.1 0.0 collective-permute-start.5
  9.1 0.5 %collective-permute-start.2 = (f32[9,2,16,128]{3,2,1,0:T(8,128)S(1)}, f32[9,2,16,128]{3,2,1,0:T(8,128)S(1)}, u32[]{:S(2)}, u32[]{:S(2)}) collective-permute-start(f32[9,2,16,128]{3,2,1,0:T(8,128)S(1)} %copy-done), channel_id=1, source_target_pairs={{0,2},{2,0},{1,3},{3,1},{4,6},{6,4},{5,7},{7,5},{8,10},{10,8},{9,1... | collective-permute-start | bytes 442376 | tf_op jit(solution)/shard_map/ppermute | solution.py:19
  9.7 0.0 collective-permute-done.1.near_ref
  9.7 0.2 %collective-permute-start.3 = (f32[9,2,16,128]{3,2,1,0:T(8,128)S(1)}, f32[9,2,16,128]{3,2,1,0:T(8,128)S(1)}, u32[]{:S(2)}, u32[]{:S(2)}) collective-permute-start(f32[9,2,16,128]{3,2,1,0:T(8,128)S(1)} %copy-done), channel_id=1, source_target_pairs={{0,1},{1,0},{2,3},{3,2},{4,5},{5,4},{6,7},{7,6},{8,9},{9,8},{10,11... | collective-permute-start | bytes 442376 | tf_op jit(solution)/shard_map/ppermute | solution.py:19
  10.5 3.6 %collective-permute-done.far_ref = f32[18,16,128]{2,1,0:T(8,128)S(1)} collective-permute-done((f32[18,16,128]{2,1,0:T(8,128)S(1)}, f32[18,16,128]{2,1,0:T(8,128)S(1)}, u32[]{:S(2)}, u32[]{:S(2)}) %collective-permute-start) | collective-permute-done | bytes 147488 | tf_op jit(solution)/shard_map/ppermute | solution.py:25
  14.1 0.0 collective-permute-done.4.yd_ref
  14.1 0.0 collective-permute-done.5.zd_ref
  14.1 1.3 %collective-permute-done.2.ys_ref = f32[9,2,16,128]{3,2,1,0:T(8,128)S(1)} collective-permute-done((f32[9,2,16,128]{3,2,1,0:T(8,128)S(1)}, f32[9,2,16,128]{3,2,1,0:T(8,128)S(1)}, u32[]{:S(2)}, u32[]{:S(2)}) %collective-permute-start.2) | collective-permute-done | bytes 147488 | tf_op jit(solution)/shard_map/ppermute | solution.py:19
  15.4 0.0 collective-permute-done.3.zs_ref
  15.4 0.3 %shard_map.60 = f32[9,2,16,128]{3,2,1,0:T(8,128)S(1)} custom-call(s32[1]{0:T(128)S(6)} %copy.14.steps_ref, f32[9,2,16,128]{3,2,1,0:T(8,128)S(1)} %copy-done, f32[9,2,16,128]{3,2,1,0:T(8,128)S(1)} %copy-done.1, f32[18,16,128]{2,1,0:T(8,128)S(1)} %collective-permute-done.far_ref, f32[18,16,128]{2,1,0:T(8,128)S(1)} %collective-permute-done.1.near_ref, ...), custom_call_target="tpu_custom_call" | custom-call | flops 4000000 | bytes 1000000 | tf_op jit(solution)/shard_map/pallas_call | solution.py:223
  15.7 0.6 %collective-permute-start.6 = (f32[9,2,16,128]{3,2,1,0:T(8,128)S(1)}, f32[9,2,16,128]{3,2,1,0:T(8,128)S(1)}, u32[]{:S(2)}, u32[]{:S(2)}) collective-permute-start(f32[9,2,16,128]{3,2,1,0:T(8,128)S(1)} %shard_map.60), channel_id=1, source_target_pairs={{0,2},{2,0},{1,3},{3,1},{4,6},{6,4},{5,7},{7,5},{8,10},{10,8},{9,1... | collective-permute-start | bytes 442376 | tf_op jit(solution)/shard_map/ppermute | solution.py:241
  16.3 0.9 %shard_map.59 = f32[9,2,16,128]{3,2,1,0:T(8,128)} custom-call(s32[1]{0:T(128)S(6)} %copy.14.steps_ref, f32[9,2,16,128]{3,2,1,0:T(8,128)S(1)} %copy-done, f32[18,16,128]{2,1,0:T(8,128)S(1)} %collective-permute-done.far_ref, f32[18,16,128]{2,1,0:T(8,128)S(1)} %collective-permute-done.1.near_ref, f32[9,2,16,128]{3,2,1,0:T(8,128)S(1)} %collective-permute-done.2.ys_ref, ...), custom_call_target="tpu_custom_call" | custom-call | flops 4000000 | bytes 1000000 | tf_op jit(solution)/shard_map/pallas_call | solution.py:223
  17.1 0.0 copy-start.2
  17.1 4.1 %collective-permute-done.6 = f32[9,2,16,128]{3,2,1,0:T(8,128)S(1)} collective-permute-done((f32[9,2,16,128]{3,2,1,0:T(8,128)S(1)}, f32[9,2,16,128]{3,2,1,0:T(8,128)S(1)}, u32[]{:S(2)}, u32[]{:S(2)}) %collective-permute-start.6) | collective-permute-done | bytes 147488 | tf_op jit(solution)/shard_map/ppermute | solution.py:241
  21.2 0.0 copy-done.2
  21.3 0.7 %add_multiply_fusion = f32[9,2,16,128]{3,2,1,0:T(8,128)} fusion(f32[9,2,16,128]{3,2,1,0:T(8,128)S(1)} %shard_map.60, f32[9,2,16,128]{3,2,1,0:T(8,128)S(1)} %rev.4, f32[9]{0:T(128)S(1)} %copy-done.2), kind=kLoop, calls=%fused_computation.2 | loop fusion | flops 110592 | bytes 442404 | tf_op jit(solution)/shard_map/mul | solution.py:244
  (3 shorter events, 0.1 us)
Async XLA Ops:
  0.6 1.0 %copy-start = (f32[9,2,16,128]{3,2,1,0:T(8,128)S(1)}, f32[9,2,16,128]{3,2,1,0:T(8,128)}, u32[]{:S(2)}) copy-start(f32[9,2,16,128]{3,2,1,0:T(8,128)} %seed_ref.3) | copy-start | bytes 442372
  1.7 3.1 %copy-start.1 = (f32[9,2,16,128]{3,2,1,0:T(8,128)S(1)}, f32[9,2,16,128]{3,2,1,0:T(8,128)}, u32[]{:S(2)}) copy-start(f32[9,2,16,128]{3,2,1,0:T(8,128)} %dual_ref.1) | copy-start | bytes 442372
  1.7 8.0 %collective-permute-start.1 = (f32[18,16,128]{2,1,0:T(8,128)S(1)}, f32[18,16,128]{2,1,0:T(8,128)S(1)}, u32[]{:S(2)}, u32[]{:S(2)}) collective-permute-start(f32[18,16,128]{2,1,0:T(8,128)S(1)} %get-tuple-element.2), channel_id=1, source_target_pairs={{0,4},{4,0},{8,12},{12,8},{1,5},{5,1},{9,13},{13,9},{2,6},{6,2},{1... | collective-permute-start | bytes 442376 | tf_op jit(solution)/shard_map/ppermute | solution.py:19
  4.8 9.3 %collective-permute-start.4 = (f32[9,2,16,128]{3,2,1,0:T(8,128)S(1)}, f32[9,2,16,128]{3,2,1,0:T(8,128)S(1)}, u32[]{:S(2)}, u32[]{:S(2)}) collective-permute-start(f32[9,2,16,128]{3,2,1,0:T(8,128)S(1)} %copy-done.1), channel_id=1, source_target_pairs={{0,2},{2,0},{1,3},{3,1},{4,6},{6,4},{5,7},{7,5},{8,10},{10,8},{9,1... | collective-permute-start | bytes 442376 | tf_op jit(solution)/shard_map/ppermute | solution.py:19
  6.3 7.8 %collective-permute-start = (f32[18,16,128]{2,1,0:T(8,128)S(1)}, f32[18,16,128]{2,1,0:T(8,128)S(1)}, u32[]{:S(2)}, u32[]{:S(2)}) collective-permute-start(f32[18,16,128]{2,1,0:T(8,128)S(1)} %get-tuple-element.3), channel_id=1, source_target_pairs={{0,12},{4,8},{8,4},{12,0},{1,13},{5,9},{9,5},{13,1},{2,14},{6,10},... | collective-permute-start | bytes 442376 | tf_op jit(solution)/shard_map/ppermute | solution.py:25
  9.1 5.0 %collective-permute-start.5 = (f32[9,2,16,128]{3,2,1,0:T(8,128)S(1)}, f32[9,2,16,128]{3,2,1,0:T(8,128)S(1)}, u32[]{:S(2)}, u32[]{:S(2)}) collective-permute-start(f32[9,2,16,128]{3,2,1,0:T(8,128)S(1)} %copy-done.1), channel_id=1, source_target_pairs={{0,1},{1,0},{2,3},{3,2},{4,5},{5,4},{6,7},{7,6},{8,9},{9,8},{10,11... | collective-permute-start | bytes 442376 | tf_op jit(solution)/shard_map/ppermute | solution.py:19
  9.1 6.3 %collective-permute-start.2 = (f32[9,2,16,128]{3,2,1,0:T(8,128)S(1)}, f32[9,2,16,128]{3,2,1,0:T(8,128)S(1)}, u32[]{:S(2)}, u32[]{:S(2)}) collective-permute-start(f32[9,2,16,128]{3,2,1,0:T(8,128)S(1)} %copy-done), channel_id=1, source_target_pairs={{0,2},{2,0},{1,3},{3,1},{4,6},{6,4},{5,7},{7,5},{8,10},{10,8},{9,1... | collective-permute-start | bytes 442376 | tf_op jit(solution)/shard_map/ppermute | solution.py:19
  9.7 5.7 %collective-permute-start.3 = (f32[9,2,16,128]{3,2,1,0:T(8,128)S(1)}, f32[9,2,16,128]{3,2,1,0:T(8,128)S(1)}, u32[]{:S(2)}, u32[]{:S(2)}) collective-permute-start(f32[9,2,16,128]{3,2,1,0:T(8,128)S(1)} %copy-done), channel_id=1, source_target_pairs={{0,1},{1,0},{2,3},{3,2},{4,5},{5,4},{6,7},{7,6},{8,9},{9,8},{10,11... | collective-permute-start | bytes 442376 | tf_op jit(solution)/shard_map/ppermute | solution.py:19
  15.7 5.5 %collective-permute-start.6 = (f32[9,2,16,128]{3,2,1,0:T(8,128)S(1)}, f32[9,2,16,128]{3,2,1,0:T(8,128)S(1)}, u32[]{:S(2)}, u32[]{:S(2)}) collective-permute-start(f32[9,2,16,128]{3,2,1,0:T(8,128)S(1)} %shard_map.60), channel_id=1, source_target_pairs={{0,2},{2,0},{1,3},{3,1},{4,6},{6,4},{5,7},{7,5},{8,10},{10,8},{9,1... | collective-permute-start | bytes 442376 | tf_op jit(solution)/shard_map/ppermute | solution.py:241
  17.1 4.1 %copy-start.2 = (f32[9]{0:T(128)S(1)}, f32[9]{0:T(128)}, u32[]{:S(2)}) copy-start(f32[9]{0:T(128)} %constant.23.clone) | copy-start | bytes 112

commit v2 on v1

v2 whole, which is shorter than its diff:
```python
import functools

import jax
import jax.numpy as jnp
from jax import lax
from jax.experimental import pallas as pl
from jax.experimental.pallas import tpu as pltpu
from jax.sharding import PartitionSpec as P

VISCOSITY = 0.5
DIFFUSIVITY = 0.2
EXTENSIBILITY = 100.0
HORIZON = 1.0
COMP = ((0, 3, 4), (3, 1, 5), (4, 5, 2))
PAIRS = ((0, 0), (1, 1), (2, 2), (0, 1), (0, 2), (1, 2))
SIGNS = (1.0, -1.0, 1.0, 1.0, 1.0, 1.0, -1.0, 1.0, -1.0)


def ring(array, axis, step):
    size = lax.axis_size(axis)
    return lax.ppermute(array, axis, [(i, (i + step) % size) for i in range(size)])


def line(array, axis, step):
    size = lax.axis_size(axis)
    return lax.ppermute(array, axis, [(i, i + step) for i in range(size) if 0 <= i + step < size])


def rows_y(bricks):
    size = lax.axis_size("gy")
    fields, planes, _, lanes = bricks.shape
    first = bricks[:, :, 0].reshape(fields * planes, lanes)
    last = bricks[:, :, -1].reshape(fields * planes, lanes)
    if size == 1:
        return first, last
    if size == 2:
        other = ring(jnp.where(lax.axis_index("gy") == 0, last, first), "gy", 1)
        return other, other
    return line(first, "gy", -1), line(last, "gy", 1)


def neighbours_z(bricks):
    size = lax.axis_size("gz")
    if size == 1:
        return bricks
    if size == 2:
        return ring(bricks, "gz", 1)
    half = bricks.shape[3] // 2
    return jnp.concatenate([ring(bricks, "gz", -1)[..., :half], ring(bricks, "gz", 1)[..., half:]], axis=3)


class Shifts:
    def __init__(self, rows, lanes):
        self.rows, self.lanes = rows, lanes
        self.row = lax.broadcasted_iota(jnp.int32, (rows, lanes), 0)
        self.lane = lax.broadcasted_iota(jnp.int32, (rows, lanes), 1)
        wall, walls = lax.axis_index("gy"), lax.axis_size("gy")
        self.last_wall = jnp.full((rows, lanes), wall, jnp.int32) == walls - 1
        self.first_wall = jnp.full((rows, lanes), wall, jnp.int32) == 0

    def edges(self, above_ref, below_ref, place):
        shape = (self.rows, self.lanes)
        above = jnp.broadcast_to(above_ref[pl.ds(place, 1), :], shape)
        below = jnp.broadcast_to(below_ref[pl.ds(place, 1), :], shape)
        return jnp.where(self.last_wall, 0.0, above), jnp.where(self.first_wall, 0.0, below)

    def y(self, plane, above, below):
        up = jnp.where(self.row == self.rows - 1, above, pltpu.roll(plane, self.rows - 1, 0))
        down = jnp.where(self.row == 0, below, pltpu.roll(plane, 1, 0))
        return up, down

    def z(self, plane, edge):
        up = pltpu.roll(jnp.where(self.lane == 0, edge, plane), self.lanes - 1, 1)
        down = pltpu.roll(jnp.where(self.lane == self.lanes - 1, edge, plane), 1, 1)
        return up, down


def stretch_pull(conf, dual, column):
    out = []
    for m in range(3):
        total = 0.0
        for j in range(3):
            term = dual[COMP[m][j]] * conf[COMP[j][column]]
            total = total + (term + term if j == m else term)
        out.append(total)
    return out


def half_factor(conf):
    return (0.5 * (EXTENSIBILITY - 3.0)) / (EXTENSIBILITY - (conf[0] + conf[1] + conf[2]))


def halo_planes(ref, start, count, offset, below_ref, above_ref):
    depth = ref.shape[1]
    fields = []
    for f in range(ref.shape[0]):
        planes = []
        for p in range(start - 1, start + count + 1):
            if p < 0:
                planes.append(below_ref[offset + f])
            elif p == depth:
                planes.append(above_ref[offset + f])
            else:
                planes.append(ref[f, p])
        fields.append(planes)
    return fields


def raw_kernel(start, count, has_below, has_above, *refs):
    steps_ref, seed_ref, dual_ref, ya_ref, yb_ref, z_ref, *halo_refs, raw_ref = refs
    below_ref = halo_refs[0] if has_below else None
    above_ref = halo_refs[-1] if has_above else None
    _, depth, rows, lanes = seed_ref.shape
    shift = Shifts(rows, lanes)
    time_step = HORIZON / jnp.full((rows, lanes), steps_ref[0], jnp.int32).astype(jnp.float32)
    seed = halo_planes(seed_ref, start, count, 0, below_ref, above_ref)
    dual = halo_planes(dual_ref, start, count, 9, below_ref, above_ref)
    pull_x = [
        stretch_pull([c[p] for c in seed[3:]], [c[p] for c in dual[3:]], 0) for p in range(count + 2)
    ]
    for q in range(count):
        p, at = start + q, q + 1
        conf = [c[at] for c in seed[3:]]
        pulled = [c[at] for c in dual[3:]]
        seed_y = [shift.edges(ya_ref, yb_ref, f * depth + p) for f in range(9)]
        dual_y = [shift.edges(ya_ref, yb_ref, (9 + f) * depth + p) for f in range(9)]
        seed_z = [z_ref[f, p] for f in range(9)]
        dual_z = [z_ref[9 + f, p] for f in range(9)]
        laps, slopes = [], []
        for f in range(9):
            here = dual[f][at]
            yu, yd = shift.y(here, *dual_y[f])
            zu, zd = shift.z(here, dual_z[f])
            xu, xd = dual[f][at + 1], dual[f][at - 1]
            laps.append((xu + xd) + (yu + yd) + (zu + zd) - 6.0 * here)
            if f < 3:
                slopes.append((0.5 * (xu - xd), 0.5 * (yu - yd), 0.5 * (zu - zd)))
        grads = []
        for f in range(3):
            here = seed[f][at]
            yu, yd = shift.y(here, *seed_y[f])
            zu, zd = shift.z(here, seed_z[f])
            xu, xd = seed[f][at + 1], seed[f][at - 1]
            grads.append((0.5 * (xu - xd), 0.5 * (yu - yd), 0.5 * (zu - zd)))
        pull_y = stretch_pull(conf, pulled, 1)
        pull_z = stretch_pull(conf, pulled, 2)
        above_y = stretch_pull([c[0] for c in seed_y[3:]], [c[0] for c in dual_y[3:]], 1)
        below_y = stretch_pull([c[1] for c in seed_y[3:]], [c[1] for c in dual_y[3:]], 1)
        edge_z = stretch_pull(seed_z[3:], dual_z[3:], 2)
        for m in range(3):
            yu, yd = shift.y(pull_y[m], above_y[m], below_y[m])
            zu, zd = shift.z(pull_z[m], edge_z[m])
            flux = (pull_x[at + 1][m] - pull_x[at - 1][m]) + (yu - yd) + (zu - zd)
            raw_ref[m, q] = dual[m][at] + time_step * (VISCOSITY * laps[m] - 0.5 * flux)
        half = half_factor(conf)
        stress = []
        for n, (i, j) in enumerate(PAIRS):
            slope = slopes[i][j] if i == j else slopes[i][j] + slopes[j][i]
            stress.append(-(slope + pulled[n]))
        inner = 0.0
        for n in range(6):
            inner = inner + stress[n] * conf[n]
        inner = inner * (half * half) * (2.0 / (EXTENSIBILITY - 3.0))

        def weight(k, j):
            total = 0.0
            for m in range(3):
                term = grads[m][k] * pulled[COMP[m][j]]
                total = total + (term + term if m == j else term)
            return total

        for n, (i, j) in enumerate(PAIRS):
            change = DIFFUSIVITY * laps[3 + n] + half * stress[n]
            change = change + (weight(i, i) + inner if i == j else weight(i, j) + weight(j, i))
            raw_ref[3 + n, q] = pulled[n] + time_step * change


def next_kernel(steps_ref, seed_ref, ya_ref, yb_ref, z_ref, below_ref, above_ref, next_ref):
    _, depth, rows, lanes = seed_ref.shape
    shift = Shifts(rows, lanes)
    time_step = HORIZON / jnp.full((rows, lanes), steps_ref[0], jnp.int32).astype(jnp.float32)
    seed = halo_planes(seed_ref, 0, depth, 0, below_ref, above_ref)
    halves = [half_factor([c[p] for c in seed[3:]]) for p in range(depth + 2)]
    for p in range(depth):
        at = p + 1
        conf = [c[at] for c in seed[3:]]
        ey = [shift.edges(ya_ref, yb_ref, f * depth + p) for f in range(9)]
        ez = [z_ref[f, p] for f in range(9)]
        laps, grads = [], []
        for f in range(9):
            here = seed[f][at]
            yu, yd = shift.y(here, *ey[f])
            zu, zd = shift.z(here, ez[f])
            xu, xd = seed[f][at + 1], seed[f][at - 1]
            laps.append((xu + xd) + (yu + yd) + (zu + zd) - 6.0 * here)
            if f < 3:
                grads.append((0.5 * (xu - xd), 0.5 * (yu - yd), 0.5 * (zu - zd)))
        half = halves[at]
        half_above, half_below = half_factor([c[0] for c in ey[3:]]), half_factor([c[1] for c in ey[3:]])
        half_z = half_factor(ez[3:])
        for i in range(3):
            cx, cy, cz = COMP[i]
            yu, yd = shift.y(half * conf[cy], half_above * ey[3 + cy][0], half_below * ey[3 + cy][1])
            zu, zd = shift.z(half * conf[cz], half_z * ez[3 + cz])
            xu = halves[at + 1] * seed[3 + cx][at + 1]
            xd = halves[at - 1] * seed[3 + cx][at - 1]
            divergence = 0.5 * ((xu - xd) + (yu - yd) + (zu - zd))
            next_ref[i, p] = seed[i][at] + time_step * (VISCOSITY * laps[i] + divergence)
        for n, (i, j) in enumerate(PAIRS):
            stretch = 0.0
            for k in range(3):
                term = grads[i][k] * conf[COMP[k][j]]
                stretch = stretch + (term + term if i == j else term + grads[j][k] * conf[COMP[k][i]])
            stress = half * conf[n] - (0.5 if i == j else 0.0)
            next_ref[3 + n, p] = conf[n] + time_step * (DIFFUSIVITY * laps[3 + n] + stretch - stress)


def call(kernel, shape, steps, *arrays):
    vmem = pl.BlockSpec(memory_space=pltpu.VMEM)
    return pl.pallas_call(
        kernel,
        out_shape=jax.ShapeDtypeStruct(shape, jnp.float32),
        in_specs=[pl.BlockSpec(memory_space=pltpu.SMEM)] + [vmem] * len(arrays),
        out_specs=vmem,
        cost_estimate=pl.CostEstimate(flops=4_000_000, bytes_accessed=1_000_000, transcendentals=0),
        compiler_params=pltpu.CompilerParams(vmem_limit_bytes=16 * 1024 * 1024),
    )(steps, *arrays)


def per_device(seed_state, costate, step_count):
    depth = seed_state.shape[1]
    first = jnp.concatenate([seed_state[:, 0], costate[:, 0]], 0)
    last = jnp.concatenate([seed_state[:, -1], costate[:, -1]], 0)
    below = ring(last, "gx", 1)
    above = ring(first, "gx", -1)
    both = jnp.concatenate([seed_state, costate], 0)
    ya, yb = rows_y(both)
    z = neighbours_z(both)
    walls = lax.axis_size("gy")
    signs = jnp.array(SIGNS, jnp.float32)[:, None, None, None]
    parts = []
    for start, count in ((0, depth - 1), (depth - 1, 1)):
        if count == 0:
            continue
        has_below, has_above = start == 0, start + count == depth
        raw = call(
            functools.partial(raw_kernel, start, count, has_below, has_above),
            (9, count) + seed_state.shape[2:],
            step_count,
            *(seed_state, costate, ya, yb, z),
            *((below,) if has_below else ()),
            *((above,) if has_above else ()),
        )
        partner = lax.ppermute(raw, "gy", [(i, walls - 1 - i) for i in range(walls)])
        parts.append(0.5 * (raw + jnp.flip(partner, axis=2) * signs))
    next_state = call(next_kernel, seed_state.shape, step_count, seed_state, ya, yb, z, below, above)
    return next_state, jnp.concatenate(parts, axis=1)


def solution(mesh):
    placed = P(None, ("rep", "gx"), "gy", "gz")
    return jax.shard_map(
        per_device,
        mesh=mesh,
        in_specs=(placed, placed, P("rep")),
        out_specs=(placed, placed),
        check_vma=False,
    )
```

time: 22.2 us -> 19.9 us (0.90)
  waiting for transfers between devices: 8.92 us -> 4.25 us
  starting transfers between devices: 8.77 us -> 10.6 us
  local copies, waits for them, and re-layouts: 1.02 us -> 1.43 us
    ppermute x6 -> x4, waiting for transfers between devices: 4.85 us -> 2.13 us  [ring(): lax.ppermute(array, axis, [(i, (i + step) % size) for i in range(size)])]
    ppermute x1 -> x2, starting transfers between devices: 0.6 us -> 3.19 us  [per_device(): lax.ppermute(raw, 'gy', [(i, walls - 1 - i) for i in range(walls)])]
    ppermute x1 -> x2, waiting for transfers between devices: 4.08 us -> 2.12 us  [per_device(): lax.ppermute(raw, 'gy', [(i, walls - 1 - i) for i in range(walls)])]
    unnamed x6 -> x7, local copies, waits for them, and re-layouts: 0.01 us -> 1.35 us
    squeeze x2, local copies, waits for them, and re-layouts: 0.99 us -> 0.02 us  [per_device(): first = jnp.concatenate([seed_state[:, 0], costate[:, 0]], 0)]
    ppermute x6 -> x4, starting transfers between devices: 8.17 us -> 7.45 us  [ring(): lax.ppermute(array, axis, [(i, (i + step) % size) for i in range(size)])]
    concatenate x0 -> x3, other arithmetic: none -> 0.7 us  [the longest x1 0.68 us: per_device(): return (next_state, jnp.concatenate(parts, axis=1))]
    mul x1, other arithmetic: 0.75 us -> 0.09 us  [per_device(): parts.append(0.5 * (raw + jnp.flip(partner, axis=2) * signs))]
  transfers between devices with their start and end apart: 7 -> 6, of which waited for: 3 -> 4; matrix products, arithmetic and copies ran while one was open for 0% -> 1% of each run, Pallas kernels for 4% -> 6%
where the time goes in v2:
time: 19.9 us; the launch traced here: 19.7 us
  starting transfers between devices  10.6 us (53%)
  waiting for transfers between devices  4.25 us (21%)
  local copies, waits for them, and re-layouts  1.43 us (7%)
  between operations  1.36 us (7%)
  Pallas kernels  1.14 us (6%)
  other arithmetic  0.86 us (4%)
    ppermute x4, starting transfers between devices, ring(): lax.ppermute(array, axis, [(i, (i + step) % size) for i in range(size)])  7.45 us
    ppermute x2, starting transfers between devices, per_device(): lax.ppermute(raw, 'gy', [(i, walls - 1 - i) for i in range(walls)])  3.19 us
    ppermute x4, waiting for transfers between devices, ring(): lax.ppermute(array, axis, [(i, (i + step) % size) for i in range(size)])  2.13 us
    ppermute x2, waiting for transfers between devices, per_device(): lax.ppermute(raw, 'gy', [(i, walls - 1 - i) for i in range(walls)])  2.12 us
    unnamed x7, local copies, waits for them, and re-layouts  1.35 us
    pallas_call x3, Pallas kernels, call(): pl.pallas_call(kernel, out_shape=jax.ShapeDtypeStruct(shape, jnp.float32)...  1.14 us
    concatenate x1, other arithmetic, per_device(): return (next_state, jnp.concatenate(parts, axis=1))  0.68 us
  transfers between devices with their start and end apart: 6, of which 4 were waited for; matrix products, arithmetic and copies ran while one was open for 1% of the time, Pallas kernels for 6%

profile of v2, /device:TPU:0, one launch (start us, length us, event | category | flops | bytes accessed | tf_op | source)
XLA Modules:
  0.0 19.7 jit_solution(9282781766454895977)
XLA Ops:
  0.6 0.0 copy-start.1
  0.6 1.0 %constant_dynamic-update-slice_fusion.1 = f32[18,2,16,128]{3,2,1,0:T(8,128)S(1)} fusion(f32[9,2,16,128]{3,2,1,0:T(8,128)} %refs_1_.3), kind=kLoop, calls=%fused_computation.12 | loop fusion | bytes 294912
  1.6 0.0 copy-done.1
  1.6 0.0 copy-start
  1.6 0.5 %collective-permute-start.1 = (f32[18,2,16,128]{3,2,1,0:T(8,128)S(1)}, f32[18,2,16,128]{3,2,1,0:T(8,128)S(1)}, u32[]{:S(2)}, u32[]{:S(2)}) collective-permute-start(f32[18,2,16,128]{3,2,1,0:T(8,128)S(1)} %constant_dynamic-update-slice_fusion), channel_id=1, source_target_pairs={{0,1},{1,0},{2,3},{3,2},{4,5},{5,4},{6,7},{7,6},{8,9},{9,8},{10,11... | collective-permute-start | bytes 884744 | tf_op jit(solution)/shard_map/ppermute | solution.py:21
  2.2 0.4 %copy-done = f32[9,2,16,128]{3,2,1,0:T(8,128)S(1)} copy-done((f32[9,2,16,128]{3,2,1,0:T(8,128)S(1)}, f32[9,2,16,128]{3,2,1,0:T(8,128)}, u32[]{:S(2)}) %copy-start) | copy-done | bytes 147480
  2.6 3.1 %collective-permute-start.2 = (f32[18,16,128]{2,1,0:T(8,128)S(1)}, f32[18,16,128]{2,1,0:T(8,128)S(1)}, u32[]{:S(2)}, u32[]{:S(2)}) collective-permute-start(f32[18,16,128]{2,1,0:T(8,128)S(1)} %pad_maximum_fusion), channel_id=1, source_target_pairs={{0,4},{4,8},{8,12},{12,0},{1,5},{5,9},{9,13},{13,1},{2,6},{6,10},{... | collective-permute-start | bytes 442376 | tf_op jit(solution)/shard_map/ppermute | solution.py:21
  5.7 2.1 %collective-permute-start.3 = (f32[18,16,128]{2,1,0:T(8,128)S(1)}, f32[18,16,128]{2,1,0:T(8,128)S(1)}, u32[]{:S(2)}, u32[]{:S(2)}) collective-permute-start(f32[18,16,128]{2,1,0:T(8,128)S(1)} %pad_maximum_fusion.1), channel_id=1, source_target_pairs={{0,12},{4,0},{8,4},{12,8},{1,13},{5,1},{9,5},{13,9},{2,14},{6,2},{... | collective-permute-start | bytes 442376 | tf_op jit(solution)/shard_map/ppermute | solution.py:21
  7.8 0.1 fusion
  7.9 1.8 %collective-permute-start = (f32[36,128]{1,0:T(8,128)S(1)}, f32[36,128]{1,0:T(8,128)S(1)}, u32[]{:S(2)}, u32[]{:S(2)}) collective-permute-start(f32[36,128]{1,0:T(8,128)S(1)} %select_n.13), channel_id=1, source_target_pairs={{0,2},{2,0},{1,3},{3,1},{4,6},{6,4},{5,7},{7,5},{8,10},{10,8},{9,1... | collective-permute-start | bytes 55304 | tf_op jit(solution)/shard_map/ppermute | solution.py:21
  10.3 1.4 %collective-permute-done.ya_ref.yb_ref.refs_3_.refs_4_ = f32[36,128]{1,0:T(8,128)S(1)} collective-permute-done((f32[36,128]{1,0:T(8,128)S(1)}, f32[36,128]{1,0:T(8,128)S(1)}, u32[]{:S(2)}, u32[]{:S(2)}) %collective-permute-start) | collective-permute-done | bytes 18464 | tf_op jit(solution)/shard_map/ppermute | solution.py:21
  11.7 0.7 %collective-permute-done.2.below_ref.refs_6_ = f32[18,16,128]{2,1,0:T(8,128)S(1)} collective-permute-done((f32[18,16,128]{2,1,0:T(8,128)S(1)}, f32[18,16,128]{2,1,0:T(8,128)S(1)}, u32[]{:S(2)}, u32[]{:S(2)}) %collective-permute-start.2) | collective-permute-done | bytes 147488 | tf_op jit(solution)/shard_map/ppermute | solution.py:21
  12.4 0.0 collective-permute-done.1.z_ref.refs_5_
  12.4 0.1 shard_map.60
  12.5 1.8 %collective-permute-start.4 = (f32[9,1,16,128]{3,2,1,0:T(8,128)S(1)}, f32[9,1,16,128]{3,2,1,0:T(8,128)S(1)}, u32[]{:S(2)}, u32[]{:S(2)}) collective-permute-start(f32[9,1,16,128]{3,2,1,0:T(8,128)S(1)} %shard_map.60), channel_id=1, source_target_pairs={{0,2},{2,0},{1,3},{3,1},{4,6},{6,4},{5,7},{7,5},{8,10},{10,8},{9,1... | collective-permute-start | bytes 221192 | tf_op jit(solution)/shard_map/ppermute | solution.py:254
  14.3 0.0 collective-permute-done.3.above_ref.refs_6_
  14.3 0.1 shard_map.61
  14.5 1.4 %collective-permute-start.5 = (f32[9,1,16,128]{3,2,1,0:T(8,128)S(1)}, f32[9,1,16,128]{3,2,1,0:T(8,128)S(1)}, u32[]{:S(2)}, u32[]{:S(2)}) collective-permute-start(f32[9,1,16,128]{3,2,1,0:T(8,128)S(1)} %shard_map.61), channel_id=1, source_target_pairs={{0,2},{2,0},{1,3},{3,1},{4,6},{6,4},{5,7},{7,5},{8,10},{10,8},{9,1... | collective-permute-start | bytes 221192 | tf_op jit(solution)/shard_map/ppermute | solution.py:254
  15.9 0.9 %shard_map.59 = f32[9,2,16,128]{3,2,1,0:T(8,128)} custom-call(s32[1]{0:T(128)S(6)} %copy.18.steps_ref.refs_0_, f32[9,2,16,128]{3,2,1,0:T(8,128)S(1)} %copy-done, f32[36,128]{1,0:T(8,128)S(1)} %collective-permute-done.ya_ref.yb_ref.refs_3_.refs_4_, f32[36,128]{1,0:T(8,128)S(1)} %collective-permute-done.ya_ref.yb_ref.refs_3_.refs_4_, ...), custom_call_target="tpu_custom_call" | custom-call | flops 4000000 | bytes 1000000 | tf_op jit(solution)/shard_map/pallas_call | solution.py:220
  16.8 0.7 %collective-permute-done.4 = f32[9,1,16,128]{3,2,1,0:T(8,128)S(1)} collective-permute-done((f32[9,1,16,128]{3,2,1,0:T(8,128)S(1)}, f32[9,1,16,128]{3,2,1,0:T(8,128)S(1)}, u32[]{:S(2)}, u32[]{:S(2)}) %collective-permute-start.4) | collective-permute-done | bytes 73760 | tf_op jit(solution)/shard_map/ppermute | solution.py:254
  17.5 0.0 copy-start.2
  17.5 1.4 %collective-permute-done.5 = f32[9,1,16,128]{3,2,1,0:T(8,128)S(1)} collective-permute-done((f32[9,1,16,128]{3,2,1,0:T(8,128)S(1)}, f32[9,1,16,128]{3,2,1,0:T(8,128)S(1)}, u32[]{:S(2)}, u32[]{:S(2)}) %collective-permute-start.5) | collective-permute-done | bytes 73760 | tf_op jit(solution)/shard_map/ppermute | solution.py:254
  18.9 0.0 copy-done.2
  18.9 0.1 add_multiply_fusion.1
  19.0 0.7 %pad_maximum_fusion.2 = f32[9,2,16,128]{3,2,1,0:T(8,128)} fusion(f32[9,1,16,128]{3,2,1,0:T(8,128)S(1)} %get-tuple-element.7, f32[9,1,16,128]{3,2,1,0:T(8,128)S(1)} %get-tuple-element.6), kind=kLoop, calls=%fused_computation.2 | loop fusion | flops 36864 | bytes 294912 | tf_op jit(solution)/shard_map/concatenate | solution.py:257
  (8 shorter events, 0.1 us)
Async XLA Ops:
  0.6 1.0 %copy-start.1 = (f32[9,2,16,128]{3,2,1,0:T(8,128)S(1)}, f32[9,2,16,128]{3,2,1,0:T(8,128)}, u32[]{:S(2)}) copy-start(f32[9,2,16,128]{3,2,1,0:T(8,128)} %refs_2_.3) | copy-start | bytes 442372
  1.6 0.9 %copy-start = (f32[9,2,16,128]{3,2,1,0:T(8,128)S(1)}, f32[9,2,16,128]{3,2,1,0:T(8,128)}, u32[]{:S(2)}) copy-start(f32[9,2,16,128]{3,2,1,0:T(8,128)} %refs_1_.3) | copy-start | bytes 442372
  1.6 10.8 %collective-permute-start.1 = (f32[18,2,16,128]{3,2,1,0:T(8,128)S(1)}, f32[18,2,16,128]{3,2,1,0:T(8,128)S(1)}, u32[]{:S(2)}, u32[]{:S(2)}) collective-permute-start(f32[18,2,16,128]{3,2,1,0:T(8,128)S(1)} %constant_dynamic-update-slice_fusion), channel_id=1, source_target_pairs={{0,1},{1,0},{2,3},{3,2},{4,5},{5,4},{6,7},{7,6},{8,9},{9,8},{10,11... | collective-permute-start | bytes 884744 | tf_op jit(solution)/shard_map/ppermute | solution.py:21
  2.6 9.8 %collective-permute-start.2 = (f32[18,16,128]{2,1,0:T(8,128)S(1)}, f32[18,16,128]{2,1,0:T(8,128)S(1)}, u32[]{:S(2)}, u32[]{:S(2)}) collective-permute-start(f32[18,16,128]{2,1,0:T(8,128)S(1)} %pad_maximum_fusion), channel_id=1, source_target_pairs={{0,4},{4,8},{8,12},{12,0},{1,5},{5,9},{9,13},{13,1},{2,6},{6,10},{... | collective-permute-start | bytes 442376 | tf_op jit(solution)/shard_map/ppermute | solution.py:21
  5.7 8.7 %collective-permute-start.3 = (f32[18,16,128]{2,1,0:T(8,128)S(1)}, f32[18,16,128]{2,1,0:T(8,128)S(1)}, u32[]{:S(2)}, u32[]{:S(2)}) collective-permute-start(f32[18,16,128]{2,1,0:T(8,128)S(1)} %pad_maximum_fusion.1), channel_id=1, source_target_pairs={{0,12},{4,0},{8,4},{12,8},{1,13},{5,1},{9,5},{13,9},{2,14},{6,2},{... | collective-permute-start | bytes 442376 | tf_op jit(solution)/shard_map/ppermute | solution.py:21
  7.9 3.8 %collective-permute-start = (f32[36,128]{1,0:T(8,128)S(1)}, f32[36,128]{1,0:T(8,128)S(1)}, u32[]{:S(2)}, u32[]{:S(2)}) collective-permute-start(f32[36,128]{1,0:T(8,128)S(1)} %select_n.13), channel_id=1, source_target_pairs={{0,2},{2,0},{1,3},{3,1},{4,6},{6,4},{5,7},{7,5},{8,10},{10,8},{9,1... | collective-permute-start | bytes 55304 | tf_op jit(solution)/shard_map/ppermute | solution.py:21
  12.5 4.9 %collective-permute-start.4 = (f32[9,1,16,128]{3,2,1,0:T(8,128)S(1)}, f32[9,1,16,128]{3,2,1,0:T(8,128)S(1)}, u32[]{:S(2)}, u32[]{:S(2)}) collective-permute-start(f32[9,1,16,128]{3,2,1,0:T(8,128)S(1)} %shard_map.60), channel_id=1, source_target_pairs={{0,2},{2,0},{1,3},{3,1},{4,6},{6,4},{5,7},{7,5},{8,10},{10,8},{9,1... | collective-permute-start | bytes 221192 | tf_op jit(solution)/shard_map/ppermute | solution.py:254
  14.5 4.4 %collective-permute-start.5 = (f32[9,1,16,128]{3,2,1,0:T(8,128)S(1)}, f32[9,1,16,128]{3,2,1,0:T(8,128)S(1)}, u32[]{:S(2)}, u32[]{:S(2)}) collective-permute-start(f32[9,1,16,128]{3,2,1,0:T(8,128)S(1)} %shard_map.61), channel_id=1, source_target_pairs={{0,2},{2,0},{1,3},{3,1},{4,6},{6,4},{5,7},{7,5},{8,10},{10,8},{9,1... | collective-permute-start | bytes 221192 | tf_op jit(solution)/shard_map/ppermute | solution.py:254
  17.5 1.4 %copy-start.2 = (f32[9]{0:T(128)S(1)}, f32[9]{0:T(128)}, u32[]{:S(2)}) copy-start(f32[9]{0:T(128)} %constant.10.clone) | copy-start | bytes 112

commit v3 on v2

--- a/solution.py
+++ b/solution.py
@@ -16,6 +16,24 @@
 SIGNS = (1.0, -1.0, 1.0, 1.0, 1.0, 1.0, -1.0, 1.0, -1.0)
 
 
+def facing():
+    return lax.axis_index("gz") % 2
+
+
+def place_of(step, depth):
+    return jnp.where(facing() == 0, step, depth - 1 - step)
+
+
+def ahead(array, step):
+    size, cores = lax.axis_size("gx"), lax.axis_size("gz")
+    pairs = []
+    for i in range(size):
+        for core in range(cores):
+            way = step if core % 2 == 0 else -step
+            pairs.append((i * cores + core, (i + way) % size * cores + core))
+    return lax.ppermute(array, ("gx", "gz"), pairs)
+
+
 def ring(array, axis, step):
     size = lax.axis_size(axis)
     return lax.ppermute(array, axis, [(i, (i + step) % size) for i in range(size)])
@@ -26,27 +44,90 @@
     return lax.ppermute(array, axis, [(i, i + step) for i in range(size) if 0 <= i + step < size])
 
 
-def rows_y(bricks):
-    size = lax.axis_size("gy")
-    fields, planes, _, lanes = bricks.shape
-    first = bricks[:, :, 0].reshape(fields * planes, lanes)
-    last = bricks[:, :, -1].reshape(fields * planes, lanes)
-    if size == 1:
+def pack_kernel(seed_ref, dual_ref, lanes_ref, *rows_refs):
+    fields, depth, rows, lanes = seed_ref.shape
+    half = lanes // 2
+    if len(rows_refs) == 1:
+        places = [jnp.where(lax.axis_index("gy") == 0, rows - 1, 0)]
+    else:
+        places = [0, rows - 1]
+    lane = lax.broadcasted_iota(jnp.int32, (rows, lanes), 1)
+    packed = [jnp.zeros((rows, lanes), jnp.float32)] * lanes_ref.shape[0]
+    for f in range(2 * fields):
+        ref = seed_ref if f < fields else dual_ref
+        for p in range(depth):
+            n = f * depth + p
+            for place, rows_ref in zip(places, rows_refs):
+                rows_ref[pl.ds(n, 1), :] = ref[f % fields, p, pl.ds(place, 1), :]
+            group, slot = divmod(n, half)
+            plane = ref[f % fields, p]
+            first = turned(plane, slot)
+            last = turned(plane, half + slot + 1 - lanes)
+            packed[group] = jnp.where(lane == slot, first, jnp.where(lane == half + slot, last, packed[group]))
+    for group, plane in enumerate(packed):
+        lanes_ref[group] = plane
+
+
+def unpack_kernel(above_ref, below_ref, edges_ref):
+    fields, depth, rows, lanes = edges_ref.shape
+    half = lanes // 2
+    lane = lax.broadcasted_iota(jnp.int32, (rows, lanes), 1)
+    for f in range(fields):
+        for p in range(depth):
+            group, slot = divmod(f * depth + p, half)
+            above = turned(above_ref[group], -slot)
+            below = turned(below_ref[group], lanes - 1 - half - slot)
+            edges_ref[f, p] = jnp.where(lane < half, above, below)
+
+
+def turned(plane, step):
+    step = step % plane.shape[1]
+    return pltpu.roll(plane, step, 1) if step else plane
+
+
+def estimate(bytes_accessed):
+    return pl.CostEstimate(flops=1_000_000, bytes_accessed=bytes_accessed, transcendentals=0)
+
+
+def grant():
+    return pltpu.CompilerParams(vmem_limit_bytes=16 * 1024 * 1024)
+
+
+def pack(seed_state, costate):
+    fields, depth, rows, lanes = seed_state.shape
+    count = 2 * fields * depth
+    groups = -(-count // (lanes // 2))
+    vmem = pl.BlockSpec(memory_space=pltpu.VMEM)
+    shapes = [jax.ShapeDtypeStruct((groups, rows, lanes), jnp.float32)]
+    shapes += [jax.ShapeDtypeStruct((count, lanes), jnp.float32)] * (1 if lax.axis_size("gy") == 2 else 2)
+    return pl.pallas_call(
+        pack_kernel,
+        out_shape=shapes,
+        in_specs=[vmem] * 2,
+        out_specs=[vmem] * len(shapes),
+        cost_estimate=estimate(300_000),
+        compiler_params=grant(),
+    )(seed_state, costate)
+
+
+def rows_y(packed):
+    if len(packed) == 1:
+        other = ring(packed[0], "gy", 1)
+        return other, other
+    first, last = packed
+    if lax.axis_size("gy") == 1:
         return first, last
-    if size == 2:
-        other = ring(jnp.where(lax.axis_index("gy") == 0, last, first), "gy", 1)
-        return other, other
     return line(first, "gy", -1), line(last, "gy", 1)
 
 
-def neighbours_z(bricks):
+def lanes_z(packed):
     size = lax.axis_size("gz")
     if size == 1:
-        return bricks
+        return packed, packed
     if size == 2:
-        return ring(bricks, "gz", 1)
-    half = bricks.shape[3] // 2
-    return jnp.concatenate([ring(bricks, "gz", -1)[..., :half], ring(bricks, "gz", 1)[..., half:]], axis=3)
+        other = ring(packed, "gz", 1)
+        return other, other
+    return ring(packed, "gz", -1), ring(packed, "gz", 1)
 
 
 class Shifts:
@@ -90,36 +171,41 @@
     return (0.5 * (EXTENSIBILITY - 3.0)) / (EXTENSIBILITY - (conf[0] + conf[1] + conf[2]))
 
 
-def halo_planes(ref, start, count, offset, below_ref, above_ref):
+def halo_planes(ref, start, count, offset, behind_ref, ahead_ref):
     depth = ref.shape[1]
     fields = []
-    for f in range(ref.shape[0]):
+    for f in range(9):
         planes = []
-        for p in range(start - 1, start + count + 1):
-            if p < 0:
-                planes.append(below_ref[offset + f])
-            elif p == depth:
-                planes.append(above_ref[offset + f])
+        for q in range(start - 1, start + count + 1):
+            if q < 0:
+                planes.append(behind_ref[offset + f])
+            elif q == depth:
+                planes.append(ahead_ref[offset + f])
             else:
-                planes.append(ref[f, p])
+                planes.append(ref[f, place_of(q, depth)])
         fields.append(planes)
     return fields
 
 
-def raw_kernel(start, count, has_below, has_above, *refs):
+def half_way(shape):
+    return jnp.where(jnp.full(shape, facing(), jnp.int32) == 0, 0.5, -0.5)
+
+
+def raw_kernel(start, count, has_behind, has_ahead, *refs):
     steps_ref, seed_ref, dual_ref, ya_ref, yb_ref, z_ref, *halo_refs, raw_ref = refs
-    below_ref = halo_refs[0] if has_below else None
-    above_ref = halo_refs[-1] if has_above else None
+    behind_ref = halo_refs[0] if has_behind else None
+    ahead_ref = halo_refs[-1] if has_ahead else None
     _, depth, rows, lanes = seed_ref.shape
     shift = Shifts(rows, lanes)
+    way = half_way((rows, lanes))
     time_step = HORIZON / jnp.full((rows, lanes), steps_ref[0], jnp.int32).astype(jnp.float32)
-    seed = halo_planes(seed_ref, start, count, 0, below_ref, above_ref)
-    dual = halo_planes(dual_ref, start, count, 9, below_ref, above_ref)
+    seed = halo_planes(seed_ref, start, count, 0, behind_ref, ahead_ref)
+    dual = halo_planes(dual_ref, start, count, 9, behind_ref, ahead_ref)
     pull_x = [
         stretch_pull([c[p] for c in seed[3:]], [c[p] for c in dual[3:]], 0) for p in range(count + 2)
     ]
     for q in range(count):
-        p, at = start + q, q + 1
+        p, at = place_of(start + q, depth), q + 1
         conf = [c[at] for c in seed[3:]]
         pulled = [c[at] for c in dual[3:]]
         seed_y = [shift.edges(ya_ref, yb_ref, f * depth + p) for f in range(9)]
@@ -134,14 +220,14 @@
             xu, xd = dual[f][at + 1], dual[f][at - 1]
             laps.append((xu + xd) + (yu + yd) + (zu + zd) - 6.0 * here)
             if f < 3:
-                slopes.append((0.5 * (xu - xd), 0.5 * (yu - yd), 0.5 * (zu - zd)))
+                slopes.append((way * (xu - xd), 0.5 * (yu - yd), 0.5 * (zu - zd)))
         grads = []
         for f in range(3):
             here = seed[f][at]
             yu, yd = shift.y(here, *seed_y[f])
             zu, zd = shift.z(here, seed_z[f])
             xu, xd = seed[f][at + 1], seed[f][at - 1]
-            grads.append((0.5 * (xu - xd), 0.5 * (yu - yd), 0.5 * (zu - zd)))
+            grads.append((way * (xu - xd), 0.5 * (yu - yd), 0.5 * (zu - zd)))
         pull_y = stretch_pull(conf, pulled, 1)
         pull_z = stretch_pull(conf, pulled, 2)
         above_y = stretch_pull([c[0] for c in seed_y[3:]], [c[0] for c in dual_y[3:]], 1)
@@ -150,8 +236,8 @@
         for m in range(3):
             yu, yd = shift.y(pull_y[m], above_y[m], below_y[m])
             zu, zd = shift.z(pull_z[m], edge_z[m])
-            flux = (pull_x[at + 1][m] - pull_x[at - 1][m]) + (yu - yd) + (zu - zd)
-            raw_ref[m, q] = dual[m][at] + time_step * (VISCOSITY * laps[m] - 0.5 * flux)
+            flux = way * (pull_x[at + 1][m] - pull_x[at - 1][m]) + 0.5 * ((yu - yd) + (zu - zd))
+            raw_ref[m, q] = dual[m][at] + time_step * (VISCOSITY * laps[m] - flux)
         half = half_factor(conf)
         stress = []
         for n, (i, j) in enumerate(PAIRS):
@@ -175,14 +261,15 @@
             raw_ref[3 + n, q] = pulled[n] + time_step * change
 
 
-def next_kernel(steps_ref, seed_ref, ya_ref, yb_ref, z_ref, below_ref, above_ref, next_ref):
+def next_kernel(steps_ref, seed_ref, ya_ref, yb_ref, z_ref, behind_ref, ahead_ref, next_ref):
     _, depth, rows, lanes = seed_ref.shape
     shift = Shifts(rows, lanes)
+    way = half_way((rows, lanes))
     time_step = HORIZON / jnp.full((rows, lanes), steps_ref[0], jnp.int32).astype(jnp.float32)
-    seed = halo_planes(seed_ref, 0, depth, 0, below_ref, above_ref)
+    seed = halo_planes(seed_ref, 0, depth, 0, behind_ref, ahead_ref)
     halves = [half_factor([c[p] for c in seed[3:]]) for p in range(depth + 2)]
-    for p in range(depth):
-        at = p + 1
+    for q in range(depth):
+        p, at = place_of(q, depth), q + 1
         conf = [c[at] for c in seed[3:]]
         ey = [shift.edges(ya_ref, yb_ref, f * depth + p) for f in range(9)]
         ez = [z_ref[f, p] for f in range(9)]
@@ -194,7 +281,7 @@
             xu, xd = seed[f][at + 1], seed[f][at - 1]
             laps.append((xu + xd) + (yu + yd) + (zu + zd) - 6.0 * here)
             if f < 3:
-                grads.append((0.5 * (xu - xd), 0.5 * (yu - yd), 0.5 * (zu - zd)))
+                grads.append((way * (xu - xd), 0.5 * (yu - yd), 0.5 * (zu - zd)))
         half = halves[at]
         half_above, half_below = half_factor([c[0] for c in ey[3:]]), half_factor([c[1] for c in ey[3:]])
         half_z = half_factor(ez[3:])
@@ -204,7 +291,7 @@
             zu, zd = shift.z(half * conf[cz], half_z * ez[3 + cz])
             xu = halves[at + 1] * seed[3 + cx][at + 1]
             xd = halves[at - 1] * seed[3 + cx][at - 1]
-            divergence = 0.5 * ((xu - xd) + (yu - yd) + (zu - zd))
+            divergence = way * (xu - xd) + 0.5 * ((yu - yd) + (zu - zd))
             next_ref[i, p] = seed[i][at] + time_step * (VISCOSITY * laps[i] + divergence)
         for n, (i, j) in enumerate(PAIRS):
             stretch = 0.0
@@ -215,46 +302,60 @@
             next_ref[3 + n, p] = conf[n] + time_step * (DIFFUSIVITY * laps[3 + n] + stretch - stress)
 
 
+def average_kernel(*refs):
+    *pairs, out_ref = refs
+    step = 0
+    for raw_ref, image_ref in zip(pairs[::2], pairs[1::2]):
+        for q in range(raw_ref.shape[1]):
+            place = place_of(step, out_ref.shape[1])
+            for f, sign in enumerate(SIGNS):
+                raw, image = raw_ref[f, q], image_ref[f, q]
+                out_ref[f, place] = 0.5 * (raw + image if sign > 0 else raw - image)
+            step += 1
+
+
 def call(kernel, shape, steps, *arrays):
     vmem = pl.BlockSpec(memory_space=pltpu.VMEM)
+    scalars = [pl.BlockSpec(memory_space=pltpu.SMEM)] * len(steps)
     return pl.pallas_call(
         kernel,
         out_shape=jax.ShapeDtypeStruct(shape, jnp.float32),
-        in_specs=[pl.BlockSpec(memory_space=pltpu.SMEM)] + [vmem] * len(arrays),
+        in_specs=scalars + [vmem] * len(arrays),
         out_specs=vmem,
-        cost_estimate=pl.CostEstimate(flops=4_000_000, bytes_accessed=1_000_000, transcendentals=0),
-        compiler_params=pltpu.CompilerParams(vmem_limit_bytes=16 * 1024 * 1024),
-    )(steps, *arrays)
+        cost_estimate=estimate(1_000_000),
+        compiler_params=grant(),
+    )(*steps, *arrays)
 
 
 def per_device(seed_state, costate, step_count):
     depth = seed_state.shape[1]
-    first = jnp.concatenate([seed_state[:, 0], costate[:, 0]], 0)
-    last = jnp.concatenate([seed_state[:, -1], costate[:, -1]], 0)
-    below = ring(last, "gx", 1)
-    above = ring(first, "gx", -1)
-    both = jnp.concatenate([seed_state, costate], 0)
-    ya, yb = rows_y(both)
-    z = neighbours_z(both)
+    start_face, end_face = (jnp.concatenate([x[:, p] for x in (seed_state, costate)], 0) for p in (0, -1))
+    upwards = facing() == 0
+    last = jnp.where(upwards, end_face, start_face)
+    first = jnp.where(upwards, start_face, end_face)
+    behind = ahead(last, 1)
+    front = ahead(first, -1)
+    lanes, *rows = pack(seed_state, costate)
+    ya, yb = rows_y(rows)
+    z = call(unpack_kernel, (18,) + seed_state.shape[1:], (), *lanes_z(lanes))
     walls = lax.axis_size("gy")
-    signs = jnp.array(SIGNS, jnp.float32)[:, None, None, None]
-    parts = []
+    pairs = []
     for start, count in ((0, depth - 1), (depth - 1, 1)):
         if count == 0:
             continue
-        has_below, has_above = start == 0, start + count == depth
+        has_behind, has_ahead = start == 0, start + count == depth
         raw = call(
-            functools.partial(raw_kernel, start, count, has_below, has_above),
+            functools.partial(raw_kernel, start, count, has_behind, has_ahead),
             (9, count) + seed_state.shape[2:],
-            step_count,
+            (step_count,),
             *(seed_state, costate, ya, yb, z),
-            *((below,) if has_below else ()),
-            *((above,) if has_above else ()),
+            *((behind,) if has_behind else ()),
+            *((front,) if has_ahead else ()),
         )
         partner = lax.ppermute(raw, "gy", [(i, walls - 1 - i) for i in range(walls)])
-        parts.append(0.5 * (raw + jnp.flip(partner, axis=2) * signs))
-    next_state = call(next_kernel, seed_state.shape, step_count, seed_state, ya, yb, z, below, above)
-    return next_state, jnp.concatenate(parts, axis=1)
+        pairs += [raw, jnp.flip(partner, axis=2)]
+    next_state = call(next_kernel, seed_state.shape, (step_count,), seed_state, ya, yb, z, behind, front)
+    return next_state, call(average_kernel, seed_state.shape, (), *pairs)
 
 
 def solution(mesh):

time: 19.9 us -> 19.1 us (0.960)
  Pallas kernels: 1.14 us -> 2.3 us
  starting transfers between devices: 10.6 us -> 9.49 us
  other arithmetic: 0.86 us -> 0.03 us
  waiting for transfers between devices: 4.25 us -> 4.68 us
  local copies, waits for them, and re-layouts: 1.43 us -> 1.07 us
    ppermute x4 -> x2, starting transfers between devices: 7.45 us -> 1.72 us  [ring(): lax.ppermute(array, axis, [(i, (i + step) % size) for i in range(size)])]
    ppermute x0 -> x2, starting transfers between devices: none -> 5.17 us  [ahead(): return lax.ppermute(array, ('gx', 'gz'), pairs)]
    unnamed x7 -> x4, local copies, waits for them, and re-layouts: 1.35 us -> 0.01 us
    ppermute x2, waiting for transfers between devices: 2.12 us -> 3.39 us  [per_device(): lax.ppermute(raw, 'gy', [(i, walls - 1 - i) for i in range(walls)])]
    squeeze x2 -> x1, local copies, waits for them, and re-layouts: 0.02 us -> 1.03 us  [per_device(): x[:, p]]
    pallas_call x3 -> x5, Pallas kernels: 1.14 us -> 2.09 us  [call(): pl.pallas_call(kernel, out_shape=jax.ShapeDtypeStruct(shape, jnp.float32)...]
    ppermute x4 -> x2, waiting for transfers between devices: 2.13 us -> 1.26 us  [ring(): lax.ppermute(array, axis, [(i, (i + step) % size) for i in range(size)])]
    concatenate x3 -> x0, other arithmetic: 0.7 us -> none  [the longest x1 0.68 us: per_device(): return (next_state, jnp.concatenate(parts, axis=1))]
  transfers between devices with their start and end apart: 6 -> 6, of which waited for: 4 -> 4; matrix products, arithmetic and copies ran while one was open for 1% -> 0% of each run, Pallas kernels for 6% -> 9%
where the time goes in v3:
time: 19.1 us; the launch traced here: 18.9 us
  starting transfers between devices  9.49 us (50%)
  waiting for transfers between devices  4.68 us (25%)
  Pallas kernels  2.3 us (12%)
  between operations  1.34 us (7%)
  local copies, waits for them, and re-layouts  1.07 us (6%)
    ppermute x2, starting transfers between devices, ahead(): return lax.ppermute(array, ('gx', 'gz'), pairs)  5.17 us
    ppermute x2, waiting for transfers between devices, per_device(): lax.ppermute(raw, 'gy', [(i, walls - 1 - i) for i in range(walls)])  3.39 us
    ppermute x2, starting transfers between devices, per_device(): lax.ppermute(raw, 'gy', [(i, walls - 1 - i) for i in range(walls)])  2.61 us
    pallas_call x5, Pallas kernels, call(): pl.pallas_call(kernel, out_shape=jax.ShapeDtypeStruct(shape, jnp.float32)...  2.09 us
    ppermute x2, starting transfers between devices, ring(): lax.ppermute(array, axis, [(i, (i + step) % size) for i in range(size)])  1.72 us
    ppermute x2, waiting for transfers between devices, ring(): lax.ppermute(array, axis, [(i, (i + step) % size) for i in range(size)])  1.26 us
    squeeze x1, local copies, waits for them, and re-layouts, per_device(): x[:, p]  1.03 us
  transfers between devices with their start and end apart: 6, of which 4 were waited for; matrix products, arithmetic and copies ran while one was open for 0% of the time, Pallas kernels for 9%

profile of v3, /device:TPU:0, one launch (start us, length us, event | category | flops | bytes accessed | tf_op | source)
XLA Modules:
  0.0 18.9 jit_solution(12915174943930940662)
XLA Ops:
  0.6 1.0 %slice_bitcast_fusion.2 = (f32[9,16,128]{2,1,0:T(8,128)S(1)}, f32[9,16,128]{2,1,0:T(8,128)S(1)}, f32[9,16,128]{2,1,0:T(8,128)S(1)}, f32[9,16,128]{2,1,0:T(8,128)S(1)}) fusion(f32[9,2,16,128]{3,2,1,0:T(8,128)} %refs_2_.3, f32[9,2,16,128]{3,2,1,0:T(8,128)} %refs_1_.3), kind=kLoop, calls=%fused_computation.6 | loop fusion | bytes 589824 | tf_op jit(solution)/shard_map/squeeze | solution.py:332
  1.7 0.0 copy-start
  1.7 0.0 copy-start.1
  1.7 3.1 %collective-permute-start.2 = (f32[18,16,128]{2,1,0:T(8,128)S(1)}, f32[18,16,128]{2,1,0:T(8,128)S(1)}, u32[]{:S(2)}, u32[]{:S(2)}) collective-permute-start(f32[18,16,128]{2,1,0:T(8,128)S(1)} %get-tuple-element.7), channel_id=1, source_target_pairs={{0,4},{1,13},{4,8},{5,1},{8,12},{9,5},{12,0},{13,9},{2,6},{3,15},{... | collective-permute-start | bytes 442376 | tf_op jit(solution)/shard_map/ppermute | solution.py:34
  4.8 2.1 %collective-permute-start.3 = (f32[18,16,128]{2,1,0:T(8,128)S(1)}, f32[18,16,128]{2,1,0:T(8,128)S(1)}, u32[]{:S(2)}, u32[]{:S(2)}) collective-permute-start(f32[18,16,128]{2,1,0:T(8,128)S(1)} %get-tuple-element.6), channel_id=1, source_target_pairs={{0,12},{1,5},{4,0},{5,9},{8,4},{9,13},{12,8},{13,1},{2,14},{3,7},{... | collective-permute-start | bytes 442376 | tf_op jit(solution)/shard_map/ppermute | solution.py:34
  6.9 0.0 copy-done
  6.9 0.0 copy-done.1
  6.9 0.2 %shard_map.50 = (f32[1,16,128]{2,1,0:T(8,128)S(1)}, f32[36,128]{1,0:T(8,128)S(1)}) custom-call(f32[9,2,16,128]{3,2,1,0:T(8,128)S(1)} %copy-done, f32[9,2,16,128]{3,2,1,0:T(8,128)S(1)} %copy-done.1), custom_call_target="tpu_custom_call" | custom-call | flops 1000000 | bytes 300000 | tf_op jit(solution)/shard_map/pallas_call | solution.py:103
  7.1 1.7 %collective-permute-start = (f32[36,128]{1,0:T(8,128)S(1)}, f32[36,128]{1,0:T(8,128)S(1)}, u32[]{:S(2)}, u32[]{:S(2)}) collective-permute-start(f32[36,128]{1,0:T(8,128)S(1)} %get-tuple-element.4), channel_id=1, source_target_pairs={{0,2},{2,0},{1,3},{3,1},{4,6},{6,4},{5,7},{7,5},{8,10},{10,8},{9,1... | collective-permute-start | bytes 55304 | tf_op jit(solution)/shard_map/ppermute | solution.py:39
  8.8 0.0 collective-permute-start.1
  9.5 0.5 %collective-permute-done.1.above_ref.below_ref = f32[1,16,128]{2,1,0:T(8,128)S(1)} collective-permute-done((f32[1,16,128]{2,1,0:T(8,128)S(1)}, f32[1,16,128]{2,1,0:T(8,128)S(1)}, u32[]{:S(2)}, u32[]{:S(2)}) %collective-permute-start.1) | collective-permute-done | bytes 8224 | tf_op jit(solution)/shard_map/ppermute | solution.py:39
  10.0 0.2 %shard_map.51.z_ref.refs_5_ = f32[18,2,16,128]{3,2,1,0:T(8,128)S(1)} custom-call(f32[1,16,128]{2,1,0:T(8,128)S(1)} %collective-permute-done.1.above_ref.below_ref, f32[1,16,128]{2,1,0:T(8,128)S(1)} %collective-permute-done.1.above_ref.below_ref), custom_call_target="tpu_custom_call" | custom-call | flops 1000000 | bytes 1000000 | tf_op jit(solution)/shard_map/pallas_call | solution.py:320
  10.2 0.7 %collective-permute-done.ya_ref.yb_ref.refs_3_.refs_4_ = f32[36,128]{1,0:T(8,128)S(1)} collective-permute-done((f32[36,128]{1,0:T(8,128)S(1)}, f32[36,128]{1,0:T(8,128)S(1)}, u32[]{:S(2)}, u32[]{:S(2)}) %collective-permute-start) | collective-permute-done | bytes 18464 | tf_op jit(solution)/shard_map/ppermute | solution.py:39
  11.0 0.0 collective-permute-done.2.behind_ref.refs_6_
  11.0 0.2 shard_map.53.refs_0_
  11.2 1.7 %collective-permute-start.4 = (f32[9,1,16,128]{3,2,1,0:T(8,128)S(1)}, f32[9,1,16,128]{3,2,1,0:T(8,128)S(1)}, u32[]{:S(2)}, u32[]{:S(2)}) collective-permute-start(f32[9,1,16,128]{3,2,1,0:T(8,128)S(1)} %shard_map.53.refs_0_), channel_id=1, source_target_pairs={{0,2},{2,0},{1,3},{3,1},{4,6},{6,4},{5,7},{7,5},{8,10},{10,8},{9,1... | collective-permute-start | bytes 221192 | tf_op jit(solution)/shard_map/ppermute | solution.py:355
  12.8 0.0 collective-permute-done.3.ahead_ref.refs_6_
  12.8 0.2 shard_map.54.refs_2_
  13.0 0.9 %collective-permute-start.5 = (f32[9,1,16,128]{3,2,1,0:T(8,128)S(1)}, f32[9,1,16,128]{3,2,1,0:T(8,128)S(1)}, u32[]{:S(2)}, u32[]{:S(2)}) collective-permute-start(f32[9,1,16,128]{3,2,1,0:T(8,128)S(1)} %shard_map.54.refs_2_), channel_id=1, source_target_pairs={{0,2},{2,0},{1,3},{3,1},{4,6},{6,4},{5,7},{7,5},{8,10},{10,8},{9,1... | collective-permute-start | bytes 221192 | tf_op jit(solution)/shard_map/ppermute | solution.py:355
  13.9 0.9 %shard_map.52 = f32[9,2,16,128]{3,2,1,0:T(8,128)} custom-call(s32[1]{0:T(128)S(6)} %copy.13.steps_ref.refs_0_, f32[9,2,16,128]{3,2,1,0:T(8,128)S(1)} %copy-done, f32[36,128]{1,0:T(8,128)S(1)} %collective-permute-done.ya_ref.yb_ref.refs_3_.refs_4_, f32[36,128]{1,0:T(8,128)S(1)} %collective-permute-done.ya_ref.yb_ref.refs_3_.refs_4_, ...), custom_call_target="tpu_custom_call" | custom-call | flops 1000000 | bytes 1000000 | tf_op jit(solution)/shard_map/pallas_call | solution.py:320
  14.8 0.8 %collective-permute-done.4 = f32[9,1,16,128]{3,2,1,0:T(8,128)S(1)} collective-permute-done((f32[9,1,16,128]{3,2,1,0:T(8,128)S(1)}, f32[9,1,16,128]{3,2,1,0:T(8,128)S(1)}, u32[]{:S(2)}, u32[]{:S(2)}) %collective-permute-start.4) | collective-permute-done | bytes 73760 | tf_op jit(solution)/shard_map/ppermute | solution.py:355
  15.6 2.6 %collective-permute-done.5 = f32[9,1,16,128]{3,2,1,0:T(8,128)S(1)} collective-permute-done((f32[9,1,16,128]{3,2,1,0:T(8,128)S(1)}, f32[9,1,16,128]{3,2,1,0:T(8,128)S(1)}, u32[]{:S(2)}, u32[]{:S(2)}) %collective-permute-start.5) | collective-permute-done | bytes 73760 | tf_op jit(solution)/shard_map/ppermute | solution.py:355
  18.2 0.7 %shard_map.55 = f32[9,2,16,128]{3,2,1,0:T(8,128)} custom-call(f32[9,1,16,128]{3,2,1,0:T(8,128)S(1)} %shard_map.53.refs_0_, f32[9,1,16,128]{3,2,1,0:T(8,128)S(1)} %rev.7.refs_1_, f32[9,1,16,128]{3,2,1,0:T(8,128)S(1)} %shard_map.54.refs_2_, f32[9,1,16,128]{3,2,1,0:T(8,128)S(1)} %rev.8.refs_3_), custom_call_target="tpu_custom_call" | custom-call | flops 1000000 | bytes 1000000 | tf_op jit(solution)/shard_map/pallas_call | solution.py:320
  (3 shorter events, 0.1 us)
Async XLA Ops:
  1.7 5.2 %copy-start = (f32[9,2,16,128]{3,2,1,0:T(8,128)S(1)}, f32[9,2,16,128]{3,2,1,0:T(8,128)}, u32[]{:S(2)}) copy-start(f32[9,2,16,128]{3,2,1,0:T(8,128)} %refs_1_.3) | copy-start | bytes 442372
  1.7 5.2 %copy-start.1 = (f32[9,2,16,128]{3,2,1,0:T(8,128)S(1)}, f32[9,2,16,128]{3,2,1,0:T(8,128)}, u32[]{:S(2)}) copy-start(f32[9,2,16,128]{3,2,1,0:T(8,128)} %refs_2_.3) | copy-start | bytes 442372
  1.7 9.3 %collective-permute-start.2 = (f32[18,16,128]{2,1,0:T(8,128)S(1)}, f32[18,16,128]{2,1,0:T(8,128)S(1)}, u32[]{:S(2)}, u32[]{:S(2)}) collective-permute-start(f32[18,16,128]{2,1,0:T(8,128)S(1)} %get-tuple-element.7), channel_id=1, source_target_pairs={{0,4},{1,13},{4,8},{5,1},{8,12},{9,5},{12,0},{13,9},{2,6},{3,15},{... | collective-permute-start | bytes 442376 | tf_op jit(solution)/shard_map/ppermute | solution.py:34
  4.8 8.0 %collective-permute-start.3 = (f32[18,16,128]{2,1,0:T(8,128)S(1)}, f32[18,16,128]{2,1,0:T(8,128)S(1)}, u32[]{:S(2)}, u32[]{:S(2)}) collective-permute-start(f32[18,16,128]{2,1,0:T(8,128)S(1)} %get-tuple-element.6), channel_id=1, source_target_pairs={{0,12},{1,5},{4,0},{5,9},{8,4},{9,13},{12,8},{13,1},{2,14},{3,7},{... | collective-permute-start | bytes 442376 | tf_op jit(solution)/shard_map/ppermute | solution.py:34
  7.1 3.8 %collective-permute-start = (f32[36,128]{1,0:T(8,128)S(1)}, f32[36,128]{1,0:T(8,128)S(1)}, u32[]{:S(2)}, u32[]{:S(2)}) collective-permute-start(f32[36,128]{1,0:T(8,128)S(1)} %get-tuple-element.4), channel_id=1, source_target_pairs={{0,2},{2,0},{1,3},{3,1},{4,6},{6,4},{5,7},{7,5},{8,10},{10,8},{9,1... | collective-permute-start | bytes 55304 | tf_op jit(solution)/shard_map/ppermute | solution.py:39
  8.8 1.2 %collective-permute-start.1 = (f32[1,16,128]{2,1,0:T(8,128)S(1)}, f32[1,16,128]{2,1,0:T(8,128)S(1)}, u32[]{:S(2)}, u32[]{:S(2)}) collective-permute-start(f32[1,16,128]{2,1,0:T(8,128)S(1)} %get-tuple-element.5), channel_id=1, source_target_pairs={{0,1},{1,0},{2,3},{3,2},{4,5},{5,4},{6,7},{7,6},{8,9},{9,8},{10,11... | collective-permute-start | bytes 24584 | tf_op jit(solution)/shard_map/ppermute | solution.py:39
  11.2 4.4 %collective-permute-start.4 = (f32[9,1,16,128]{3,2,1,0:T(8,128)S(1)}, f32[9,1,16,128]{3,2,1,0:T(8,128)S(1)}, u32[]{:S(2)}, u32[]{:S(2)}) collective-permute-start(f32[9,1,16,128]{3,2,1,0:T(8,128)S(1)} %shard_map.53.refs_0_), channel_id=1, source_target_pairs={{0,2},{2,0},{1,3},{3,1},{4,6},{6,4},{5,7},{7,5},{8,10},{10,8},{9,1... | collective-permute-start | bytes 221192 | tf_op jit(solution)/shard_map/ppermute | solution.py:355
  13.0 5.2 %collective-permute-start.5 = (f32[9,1,16,128]{3,2,1,0:T(8,128)S(1)}, f32[9,1,16,128]{3,2,1,0:T(8,128)S(1)}, u32[]{:S(2)}, u32[]{:S(2)}) collective-permute-start(f32[9,1,16,128]{3,2,1,0:T(8,128)S(1)} %shard_map.54.refs_2_), channel_id=1, source_target_pairs={{0,2},{2,0},{1,3},{3,1},{4,6},{6,4},{5,7},{7,5},{8,10},{10,8},{9,1... | collective-permute-start | bytes 221192 | tf_op jit(solution)/shard_map/ppermute | solution.py:355

commit v4 on v3

--- a/solution.py
+++ b/solution.py
@@ -14,24 +14,6 @@
 COMP = ((0, 3, 4), (3, 1, 5), (4, 5, 2))
 PAIRS = ((0, 0), (1, 1), (2, 2), (0, 1), (0, 2), (1, 2))
 SIGNS = (1.0, -1.0, 1.0, 1.0, 1.0, 1.0, -1.0, 1.0, -1.0)
-
-
-def facing():
-    return lax.axis_index("gz") % 2
-
-
-def place_of(step, depth):
-    return jnp.where(facing() == 0, step, depth - 1 - step)
-
-
-def ahead(array, step):
-    size, cores = lax.axis_size("gx"), lax.axis_size("gz")
-    pairs = []
-    for i in range(size):
-        for core in range(cores):
-            way = step if core % 2 == 0 else -step
-            pairs.append((i * cores + core, (i + way) % size * cores + core))
-    return lax.ppermute(array, ("gx", "gz"), pairs)
 
 
 def ring(array, axis, step):
@@ -171,41 +153,36 @@
     return (0.5 * (EXTENSIBILITY - 3.0)) / (EXTENSIBILITY - (conf[0] + conf[1] + conf[2]))
 
 
-def halo_planes(ref, start, count, offset, behind_ref, ahead_ref):
+def halo_planes(ref, start, count, offset, below_ref, above_ref):
     depth = ref.shape[1]
     fields = []
     for f in range(9):
         planes = []
-        for q in range(start - 1, start + count + 1):
-            if q < 0:
-                planes.append(behind_ref[offset + f])
-            elif q == depth:
-                planes.append(ahead_ref[offset + f])
+        for p in range(start - 1, start + count + 1):
+            if p < 0:
+                planes.append(below_ref[offset + f])
+            elif p == depth:
+                planes.append(above_ref[offset + f])
             else:
-                planes.append(ref[f, place_of(q, depth)])
+                planes.append(ref[f, p])
         fields.append(planes)
     return fields
 
 
-def half_way(shape):
-    return jnp.where(jnp.full(shape, facing(), jnp.int32) == 0, 0.5, -0.5)
-
-
-def raw_kernel(start, count, has_behind, has_ahead, *refs):
+def raw_kernel(start, count, has_below, has_above, *refs):
     steps_ref, seed_ref, dual_ref, ya_ref, yb_ref, z_ref, *halo_refs, raw_ref = refs
-    behind_ref = halo_refs[0] if has_behind else None
-    ahead_ref = halo_refs[-1] if has_ahead else None
+    below_ref = halo_refs[0] if has_below else None
+    above_ref = halo_refs[-1] if has_above else None
     _, depth, rows, lanes = seed_ref.shape
     shift = Shifts(rows, lanes)
-    way = half_way((rows, lanes))
     time_step = HORIZON / jnp.full((rows, lanes), steps_ref[0], jnp.int32).astype(jnp.float32)
-    seed = halo_planes(seed_ref, start, count, 0, behind_ref, ahead_ref)
-    dual = halo_planes(dual_ref, start, count, 9, behind_ref, ahead_ref)
+    seed = halo_planes(seed_ref, start, count, 0, below_ref, above_ref)
+    dual = halo_planes(dual_ref, start, count, 9, below_ref, above_ref)
     pull_x = [
         stretch_pull([c[p] for c in seed[3:]], [c[p] for c in dual[3:]], 0) for p in range(count + 2)
     ]
     for q in range(count):
-        p, at = place_of(start + q, depth), q + 1
+        p, at = start + q, q + 1
         conf = [c[at] for c in seed[3:]]
         pulled = [c[at] for c in dual[3:]]
         seed_y = [shift.edges(ya_ref, yb_ref, f * depth + p) for f in range(9)]
@@ -220,14 +197,14 @@
             xu, xd = dual[f][at + 1], dual[f][at - 1]
             laps.append((xu + xd) + (yu + yd) + (zu + zd) - 6.0 * here)
             if f < 3:
-                slopes.append((way * (xu - xd), 0.5 * (yu - yd), 0.5 * (zu - zd)))
+                slopes.append((0.5 * (xu - xd), 0.5 * (yu - yd), 0.5 * (zu - zd)))
         grads = []
         for f in range(3):
             here = seed[f][at]
             yu, yd = shift.y(here, *seed_y[f])
             zu, zd = shift.z(here, seed_z[f])
             xu, xd = seed[f][at + 1], seed[f][at - 1]
-            grads.append((way * (xu - xd), 0.5 * (yu - yd), 0.5 * (zu - zd)))
+            grads.append((0.5 * (xu - xd), 0.5 * (yu - yd), 0.5 * (zu - zd)))
         pull_y = stretch_pull(conf, pulled, 1)
         pull_z = stretch_pull(conf, pulled, 2)
         above_y = stretch_pull([c[0] for c in seed_y[3:]], [c[0] for c in dual_y[3:]], 1)
@@ -236,7 +213,7 @@
         for m in range(3):
             yu, yd = shift.y(pull_y[m], above_y[m], below_y[m])
             zu, zd = shift.z(pull_z[m], edge_z[m])
-            flux = way * (pull_x[at + 1][m] - pull_x[at - 1][m]) + 0.5 * ((yu - yd) + (zu - zd))
+            flux = 0.5 * ((pull_x[at + 1][m] - pull_x[at - 1][m]) + (yu - yd) + (zu - zd))
             raw_ref[m, q] = dual[m][at] + time_step * (VISCOSITY * laps[m] - flux)
         half = half_factor(conf)
         stress = []
@@ -261,15 +238,14 @@
             raw_ref[3 + n, q] = pulled[n] + time_step * change
 
 
-def next_kernel(steps_ref, seed_ref, ya_ref, yb_ref, z_ref, behind_ref, ahead_ref, next_ref):
+def next_kernel(steps_ref, seed_ref, ya_ref, yb_ref, z_ref, below_ref, above_ref, next_ref):
     _, depth, rows, lanes = seed_ref.shape
     shift = Shifts(rows, lanes)
-    way = half_way((rows, lanes))
     time_step = HORIZON / jnp.full((rows, lanes), steps_ref[0], jnp.int32).astype(jnp.float32)
-    seed = halo_planes(seed_ref, 0, depth, 0, behind_ref, ahead_ref)
+    seed = halo_planes(seed_ref, 0, depth, 0, below_ref, above_ref)
     halves = [half_factor([c[p] for c in seed[3:]]) for p in range(depth + 2)]
-    for q in range(depth):
-        p, at = place_of(q, depth), q + 1
+    for p in range(depth):
+        at = p + 1
         conf = [c[at] for c in seed[3:]]
         ey = [shift.edges(ya_ref, yb_ref, f * depth + p) for f in range(9)]
         ez = [z_ref[f, p] for f in range(9)]
@@ -281,7 +257,7 @@
             xu, xd = seed[f][at + 1], seed[f][at - 1]
             laps.append((xu + xd) + (yu + yd) + (zu + zd) - 6.0 * here)
             if f < 3:
-                grads.append((way * (xu - xd), 0.5 * (yu - yd), 0.5 * (zu - zd)))
+                grads.append((0.5 * (xu - xd), 0.5 * (yu - yd), 0.5 * (zu - zd)))
         half = halves[at]
         half_above, half_below = half_factor([c[0] for c in ey[3:]]), half_factor([c[1] for c in ey[3:]])
         half_z = half_factor(ez[3:])
@@ -291,7 +267,7 @@
             zu, zd = shift.z(half * conf[cz], half_z * ez[3 + cz])
             xu = halves[at + 1] * seed[3 + cx][at + 1]
             xd = halves[at - 1] * seed[3 + cx][at - 1]
-            divergence = way * (xu - xd) + 0.5 * ((yu - yd) + (zu - zd))
+            divergence = 0.5 * ((xu - xd) + (yu - yd) + (zu - zd))
             next_ref[i, p] = seed[i][at] + time_step * (VISCOSITY * laps[i] + divergence)
         for n, (i, j) in enumerate(PAIRS):
             stretch = 0.0
@@ -304,14 +280,13 @@
 
 def average_kernel(*refs):
     *pairs, out_ref = refs
-    step = 0
+    plane = 0
     for raw_ref, image_ref in zip(pairs[::2], pairs[1::2]):
         for q in range(raw_ref.shape[1]):
-            place = place_of(step, out_ref.shape[1])
             for f, sign in enumerate(SIGNS):
                 raw, image = raw_ref[f, q], image_ref[f, q]
-                out_ref[f, place] = 0.5 * (raw + image if sign > 0 else raw - image)
-            step += 1
+                out_ref[f, plane] = 0.5 * (raw + image if sign > 0 else raw - image)
+            plane += 1
 
 
 def call(kernel, shape, steps, *arrays):
@@ -329,12 +304,9 @@
 
 def per_device(seed_state, costate, step_count):
     depth = seed_state.shape[1]
-    start_face, end_face = (jnp.concatenate([x[:, p] for x in (seed_state, costate)], 0) for p in (0, -1))
-    upwards = facing() == 0
-    last = jnp.where(upwards, end_face, start_face)
-    first = jnp.where(upwards, start_face, end_face)
-    behind = ahead(last, 1)
-    front = ahead(first, -1)
+    first, last = (jnp.concatenate([x[:, p] for x in (seed_state, costate)], 0) for p in (0, -1))
+    below = ring(last, "gx", 1)
+    above = ring(first, "gx", -1)
     lanes, *rows = pack(seed_state, costate)
     ya, yb = rows_y(rows)
     z = call(unpack_kernel, (18,) + seed_state.shape[1:], (), *lanes_z(lanes))
@@ -343,18 +315,18 @@
     for start, count in ((0, depth - 1), (depth - 1, 1)):
         if count == 0:
             continue
-        has_behind, has_ahead = start == 0, start + count == depth
+        has_below, has_above = start == 0, start + count == depth
         raw = call(
-            functools.partial(raw_kernel, start, count, has_behind, has_ahead),
+            functools.partial(raw_kernel, start, count, has_below, has_above),
             (9, count) + seed_state.shape[2:],
             (step_count,),
             *(seed_state, costate, ya, yb, z),
-            *((behind,) if has_behind else ()),
-            *((front,) if has_ahead else ()),
+            *((below,) if has_below else ()),
+            *((above,) if has_above else ()),
         )
         partner = lax.ppermute(raw, "gy", [(i, walls - 1 - i) for i in range(walls)])
         pairs += [raw, jnp.flip(partner, axis=2)]
-    next_state = call(next_kernel, seed_state.shape, (step_count,), seed_state, ya, yb, z, behind, front)
+    next_state = call(next_kernel, seed_state.shape, (step_count,), seed_state, ya, yb, z, below, above)
     return next_state, call(average_kernel, seed_state.shape, (), *pairs)
 
 

time: 19.1 us -> 18.9 us (0.990)
  waiting for transfers between devices: 4.68 us -> 3.9 us
  starting transfers between devices: 9.49 us -> 10.1 us
    ppermute x2 -> x4, starting transfers between devices: 1.72 us -> 6.94 us  [ring(): lax.ppermute(array, axis, [(i, (i + step) % size) for i in range(size)])]
    ppermute x2 -> x0, starting transfers between devices: 5.17 us -> none  [ahead(): return lax.ppermute(array, ('gx', 'gz'), pairs)]
    ppermute x2, waiting for transfers between devices: 3.39 us -> 2.12 us  [per_device(): lax.ppermute(raw, 'gy', [(i, walls - 1 - i) for i in range(walls)])]
    ppermute x2, starting transfers between devices: 2.61 us -> 3.19 us  [per_device(): lax.ppermute(raw, 'gy', [(i, walls - 1 - i) for i in range(walls)])]
    ppermute x2 -> x4, waiting for transfers between devices: 1.26 us -> 1.78 us  [ring(): lax.ppermute(array, axis, [(i, (i + step) % size) for i in range(size)])]
  transfers between devices with their start and end apart: 6 -> 6, of which waited for: 4 -> 5; matrix products, arithmetic and copies ran while one was open for 0% -> 0% of each run, Pallas kernels for 9% -> 9%
where the time goes in v4:
time: 18.9 us; the launch traced here: 18.7 us
  starting transfers between devices  10.1 us (53%)
  waiting for transfers between devices  3.9 us (21%)
  Pallas kernels  2.28 us (12%)
  between operations  1.32 us (7%)
  local copies, waits for them, and re-layouts  1.06 us (6%)
    ppermute x4, starting transfers between devices, ring(): lax.ppermute(array, axis, [(i, (i + step) % size) for i in range(size)])  6.94 us
    ppermute x2, starting transfers between devices, per_device(): lax.ppermute(raw, 'gy', [(i, walls - 1 - i) for i in range(walls)])  3.19 us
    ppermute x2, waiting for transfers between devices, per_device(): lax.ppermute(raw, 'gy', [(i, walls - 1 - i) for i in range(walls)])  2.12 us
    pallas_call x5, Pallas kernels, call(): pl.pallas_call(kernel, out_shape=jax.ShapeDtypeStruct(shape, jnp.float32)...  2.07 us
    ppermute x4, waiting for transfers between devices, ring(): lax.ppermute(array, axis, [(i, (i + step) % size) for i in range(size)])  1.78 us
    squeeze x1, local copies, waits for them, and re-layouts, per_device(): x[:, p]  1.02 us
  transfers between devices with their start and end apart: 6, of which 5 were waited for; matrix products, arithmetic and copies ran while one was open for 0% of the time, Pallas kernels for 9%

profile of v4, /device:TPU:0, one launch (start us, length us, event | category | flops | bytes accessed | tf_op | source)
XLA Modules:
  0.0 18.7 jit_solution(14401656534335856526)
XLA Ops:
  0.6 1.0 %slice_bitcast_fusion = (f32[9,16,128]{2,1,0:T(8,128)S(1)}, f32[9,16,128]{2,1,0:T(8,128)S(1)}, f32[9,16,128]{2,1,0:T(8,128)S(1)}, f32[9,16,128]{2,1,0:T(8,128)S(1)}) fusion(f32[9,2,16,128]{3,2,1,0:T(8,128)} %refs_2_.3, f32[9,2,16,128]{3,2,1,0:T(8,128)} %refs_1_.3), kind=kLoop, calls=%fused_computation.2 | loop fusion | bytes 589824 | tf_op jit(solution)/shard_map/squeeze | solution.py:307
  1.7 3.1 %collective-permute-start.2 = (f32[18,16,128]{2,1,0:T(8,128)S(1)}, f32[18,16,128]{2,1,0:T(8,128)S(1)}, u32[]{:S(2)}, u32[]{:S(2)}) collective-permute-start(f32[18,16,128]{2,1,0:T(8,128)S(1)} %pad_maximum_fusion), channel_id=1, source_target_pairs={{0,4},{4,8},{8,12},{12,0},{1,5},{5,9},{9,13},{13,1},{2,6},{6,10},{... | collective-permute-start | bytes 442376 | tf_op jit(solution)/shard_map/ppermute | solution.py:21
  4.8 0.0 copy-start
  4.8 0.0 copy-start.1
  4.8 2.1 %collective-permute-start.3 = (f32[18,16,128]{2,1,0:T(8,128)S(1)}, f32[18,16,128]{2,1,0:T(8,128)S(1)}, u32[]{:S(2)}, u32[]{:S(2)}) collective-permute-start(f32[18,16,128]{2,1,0:T(8,128)S(1)} %pad_maximum_fusion.1), channel_id=1, source_target_pairs={{0,12},{4,0},{8,4},{12,8},{1,13},{5,1},{9,5},{13,9},{2,14},{6,2},{... | collective-permute-start | bytes 442376 | tf_op jit(solution)/shard_map/ppermute | solution.py:21
  6.9 0.0 copy-done
  6.9 0.0 copy-done.1
  6.9 0.2 %shard_map.50 = (f32[1,16,128]{2,1,0:T(8,128)S(1)}, f32[36,128]{1,0:T(8,128)S(1)}) custom-call(f32[9,2,16,128]{3,2,1,0:T(8,128)S(1)} %copy-done, f32[9,2,16,128]{3,2,1,0:T(8,128)S(1)} %copy-done.1), custom_call_target="tpu_custom_call" | custom-call | flops 1000000 | bytes 300000 | tf_op jit(solution)/shard_map/pallas_call | solution.py:85
  7.1 1.7 %collective-permute-start = (f32[36,128]{1,0:T(8,128)S(1)}, f32[36,128]{1,0:T(8,128)S(1)}, u32[]{:S(2)}, u32[]{:S(2)}) collective-permute-start(f32[36,128]{1,0:T(8,128)S(1)} %get-tuple-element.4), channel_id=1, source_target_pairs={{0,2},{2,0},{1,3},{3,1},{4,6},{6,4},{5,7},{7,5},{8,10},{10,8},{9,1... | collective-permute-start | bytes 55304 | tf_op jit(solution)/shard_map/ppermute | solution.py:21
  8.8 0.0 collective-permute-start.1
  9.5 0.5 %collective-permute-done.1.above_ref.below_ref = f32[1,16,128]{2,1,0:T(8,128)S(1)} collective-permute-done((f32[1,16,128]{2,1,0:T(8,128)S(1)}, f32[1,16,128]{2,1,0:T(8,128)S(1)}, u32[]{:S(2)}, u32[]{:S(2)}) %collective-permute-start.1) | collective-permute-done | bytes 8224 | tf_op jit(solution)/shard_map/ppermute | solution.py:21
  10.0 0.2 %shard_map.51.z_ref.refs_5_ = f32[18,2,16,128]{3,2,1,0:T(8,128)S(1)} custom-call(f32[1,16,128]{2,1,0:T(8,128)S(1)} %collective-permute-done.1.above_ref.below_ref, f32[1,16,128]{2,1,0:T(8,128)S(1)} %collective-permute-done.1.above_ref.below_ref), custom_call_target="tpu_custom_call" | custom-call | flops 1000000 | bytes 1000000 | tf_op jit(solution)/shard_map/pallas_call | solution.py:295
  10.2 0.7 %collective-permute-done.ya_ref.yb_ref.refs_3_.refs_4_ = f32[36,128]{1,0:T(8,128)S(1)} collective-permute-done((f32[36,128]{1,0:T(8,128)S(1)}, f32[36,128]{1,0:T(8,128)S(1)}, u32[]{:S(2)}, u32[]{:S(2)}) %collective-permute-start) | collective-permute-done | bytes 18464 | tf_op jit(solution)/shard_map/ppermute | solution.py:21
  11.0 0.5 %collective-permute-done.2.below_ref.refs_6_ = f32[18,16,128]{2,1,0:T(8,128)S(1)} collective-permute-done((f32[18,16,128]{2,1,0:T(8,128)S(1)}, f32[18,16,128]{2,1,0:T(8,128)S(1)}, u32[]{:S(2)}, u32[]{:S(2)}) %collective-permute-start.2) | collective-permute-done | bytes 147488 | tf_op jit(solution)/shard_map/ppermute | solution.py:21
  11.5 0.2 shard_map.53.refs_0_
  11.7 1.8 %collective-permute-start.4 = (f32[9,1,16,128]{3,2,1,0:T(8,128)S(1)}, f32[9,1,16,128]{3,2,1,0:T(8,128)S(1)}, u32[]{:S(2)}, u32[]{:S(2)}) collective-permute-start(f32[9,1,16,128]{3,2,1,0:T(8,128)S(1)} %shard_map.53.refs_0_), channel_id=1, source_target_pairs={{0,2},{2,0},{1,3},{3,1},{4,6},{6,4},{5,7},{7,5},{8,10},{10,8},{9,1... | collective-permute-start | bytes 221192 | tf_op jit(solution)/shard_map/ppermute | solution.py:327
  13.4 0.0 collective-permute-done.3.above_ref.refs_6_
  13.4 0.2 shard_map.54.refs_2_
  13.6 1.4 %collective-permute-start.5 = (f32[9,1,16,128]{3,2,1,0:T(8,128)S(1)}, f32[9,1,16,128]{3,2,1,0:T(8,128)S(1)}, u32[]{:S(2)}, u32[]{:S(2)}) collective-permute-start(f32[9,1,16,128]{3,2,1,0:T(8,128)S(1)} %shard_map.54.refs_2_), channel_id=1, source_target_pairs={{0,2},{2,0},{1,3},{3,1},{4,6},{6,4},{5,7},{7,5},{8,10},{10,8},{9,1... | collective-permute-start | bytes 221192 | tf_op jit(solution)/shard_map/ppermute | solution.py:327
  15.0 0.9 %shard_map.52 = f32[9,2,16,128]{3,2,1,0:T(8,128)} custom-call(s32[1]{0:T(128)S(6)} %copy.13.steps_ref.refs_0_, f32[9,2,16,128]{3,2,1,0:T(8,128)S(1)} %copy-done, f32[36,128]{1,0:T(8,128)S(1)} %collective-permute-done.ya_ref.yb_ref.refs_3_.refs_4_, f32[36,128]{1,0:T(8,128)S(1)} %collective-permute-done.ya_ref.yb_ref.refs_3_.refs_4_, ...), custom_call_target="tpu_custom_call" | custom-call | flops 1000000 | bytes 1000000 | tf_op jit(solution)/shard_map/pallas_call | solution.py:295
  15.9 0.7 %collective-permute-done.4 = f32[9,1,16,128]{3,2,1,0:T(8,128)S(1)} collective-permute-done((f32[9,1,16,128]{3,2,1,0:T(8,128)S(1)}, f32[9,1,16,128]{3,2,1,0:T(8,128)S(1)}, u32[]{:S(2)}, u32[]{:S(2)}) %collective-permute-start.4) | collective-permute-done | bytes 73760 | tf_op jit(solution)/shard_map/ppermute | solution.py:327
  16.6 1.4 %collective-permute-done.5 = f32[9,1,16,128]{3,2,1,0:T(8,128)S(1)} collective-permute-done((f32[9,1,16,128]{3,2,1,0:T(8,128)S(1)}, f32[9,1,16,128]{3,2,1,0:T(8,128)S(1)}, u32[]{:S(2)}, u32[]{:S(2)}) %collective-permute-start.5) | collective-permute-done | bytes 73760 | tf_op jit(solution)/shard_map/ppermute | solution.py:327
  18.0 0.7 %shard_map.55 = f32[9,2,16,128]{3,2,1,0:T(8,128)} custom-call(f32[9,1,16,128]{3,2,1,0:T(8,128)S(1)} %shard_map.53.refs_0_, f32[9,1,16,128]{3,2,1,0:T(8,128)S(1)} %rev.7.refs_1_, f32[9,1,16,128]{3,2,1,0:T(8,128)S(1)} %shard_map.54.refs_2_, f32[9,1,16,128]{3,2,1,0:T(8,128)S(1)} %rev.8.refs_3_), custom_call_target="tpu_custom_call" | custom-call | flops 1000000 | bytes 1000000 | tf_op jit(solution)/shard_map/pallas_call | solution.py:295
  (4 shorter events, 0.1 us)
Async XLA Ops:
  1.7 9.8 %collective-permute-start.2 = (f32[18,16,128]{2,1,0:T(8,128)S(1)}, f32[18,16,128]{2,1,0:T(8,128)S(1)}, u32[]{:S(2)}, u32[]{:S(2)}) collective-permute-start(f32[18,16,128]{2,1,0:T(8,128)S(1)} %pad_maximum_fusion), channel_id=1, source_target_pairs={{0,4},{4,8},{8,12},{12,0},{1,5},{5,9},{9,13},{13,1},{2,6},{6,10},{... | collective-permute-start | bytes 442376 | tf_op jit(solution)/shard_map/ppermute | solution.py:21
  4.8 2.1 %copy-start = (f32[9,2,16,128]{3,2,1,0:T(8,128)S(1)}, f32[9,2,16,128]{3,2,1,0:T(8,128)}, u32[]{:S(2)}) copy-start(f32[9,2,16,128]{3,2,1,0:T(8,128)} %refs_1_.3) | copy-start | bytes 442372
  4.8 2.1 %copy-start.1 = (f32[9,2,16,128]{3,2,1,0:T(8,128)S(1)}, f32[9,2,16,128]{3,2,1,0:T(8,128)}, u32[]{:S(2)}) copy-start(f32[9,2,16,128]{3,2,1,0:T(8,128)} %refs_2_.3) | copy-start | bytes 442372
  4.8 8.7 %collective-permute-start.3 = (f32[18,16,128]{2,1,0:T(8,128)S(1)}, f32[18,16,128]{2,1,0:T(8,128)S(1)}, u32[]{:S(2)}, u32[]{:S(2)}) collective-permute-start(f32[18,16,128]{2,1,0:T(8,128)S(1)} %pad_maximum_fusion.1), channel_id=1, source_target_pairs={{0,12},{4,0},{8,4},{12,8},{1,13},{5,1},{9,5},{13,9},{2,14},{6,2},{... | collective-permute-start | bytes 442376 | tf_op jit(solution)/shard_map/ppermute | solution.py:21
  7.1 3.8 %collective-permute-start = (f32[36,128]{1,0:T(8,128)S(1)}, f32[36,128]{1,0:T(8,128)S(1)}, u32[]{:S(2)}, u32[]{:S(2)}) collective-permute-start(f32[36,128]{1,0:T(8,128)S(1)} %get-tuple-element.4), channel_id=1, source_target_pairs={{0,2},{2,0},{1,3},{3,1},{4,6},{6,4},{5,7},{7,5},{8,10},{10,8},{9,1... | collective-permute-start | bytes 55304 | tf_op jit(solution)/shard_map/ppermute | solution.py:21
  8.8 1.2 %collective-permute-start.1 = (f32[1,16,128]{2,1,0:T(8,128)S(1)}, f32[1,16,128]{2,1,0:T(8,128)S(1)}, u32[]{:S(2)}, u32[]{:S(2)}) collective-permute-start(f32[1,16,128]{2,1,0:T(8,128)S(1)} %get-tuple-element.5), channel_id=1, source_target_pairs={{0,1},{1,0},{2,3},{3,2},{4,5},{5,4},{6,7},{7,6},{8,9},{9,8},{10,11... | collective-permute-start | bytes 24584 | tf_op jit(solution)/shard_map/ppermute | solution.py:21
  11.7 4.9 %collective-permute-start.4 = (f32[9,1,16,128]{3,2,1,0:T(8,128)S(1)}, f32[9,1,16,128]{3,2,1,0:T(8,128)S(1)}, u32[]{:S(2)}, u32[]{:S(2)}) collective-permute-start(f32[9,1,16,128]{3,2,1,0:T(8,128)S(1)} %shard_map.53.refs_0_), channel_id=1, source_target_pairs={{0,2},{2,0},{1,3},{3,1},{4,6},{6,4},{5,7},{7,5},{8,10},{10,8},{9,1... | collective-permute-start | bytes 221192 | tf_op jit(solution)/shard_map/ppermute | solution.py:327
  13.6 4.4 %collective-permute-start.5 = (f32[9,1,16,128]{3,2,1,0:T(8,128)S(1)}, f32[9,1,16,128]{3,2,1,0:T(8,128)S(1)}, u32[]{:S(2)}, u32[]{:S(2)}) collective-permute-start(f32[9,1,16,128]{3,2,1,0:T(8,128)S(1)} %shard_map.54.refs_2_), channel_id=1, source_target_pairs={{0,2},{2,0},{1,3},{3,1},{4,6},{6,4},{5,7},{7,5},{8,10},{10,8},{9,1... | collective-permute-start | bytes 221192 | tf_op jit(solution)/shard_map/ppermute | solution.py:327

commit v5 on v4

--- a/solution.py
+++ b/solution.py
@@ -153,36 +153,22 @@
     return (0.5 * (EXTENSIBILITY - 3.0)) / (EXTENSIBILITY - (conf[0] + conf[1] + conf[2]))
 
 
-def halo_planes(ref, start, count, offset, below_ref, above_ref):
+def halo_planes(ref, below, above):
     depth = ref.shape[1]
-    fields = []
-    for f in range(9):
-        planes = []
-        for p in range(start - 1, start + count + 1):
-            if p < 0:
-                planes.append(below_ref[offset + f])
-            elif p == depth:
-                planes.append(above_ref[offset + f])
-            else:
-                planes.append(ref[f, p])
-        fields.append(planes)
-    return fields
-
-
-def raw_kernel(start, count, has_below, has_above, *refs):
-    steps_ref, seed_ref, dual_ref, ya_ref, yb_ref, z_ref, *halo_refs, raw_ref = refs
-    below_ref = halo_refs[0] if has_below else None
-    above_ref = halo_refs[-1] if has_above else None
+    return [[below[f]] + [ref[f, p] for p in range(depth)] + [above[f]] for f in range(9)]
+
+
+def local_kernel(*refs):
+    steps_ref, seed_ref, dual_ref, ya_ref, yb_ref, z_ref, raw_ref = refs
     _, depth, rows, lanes = seed_ref.shape
     shift = Shifts(rows, lanes)
     time_step = HORIZON / jnp.full((rows, lanes), steps_ref[0], jnp.int32).astype(jnp.float32)
-    seed = halo_planes(seed_ref, start, count, 0, below_ref, above_ref)
-    dual = halo_planes(dual_ref, start, count, 9, below_ref, above_ref)
-    pull_x = [
-        stretch_pull([c[p] for c in seed[3:]], [c[p] for c in dual[3:]], 0) for p in range(count + 2)
-    ]
-    for q in range(count):
-        p, at = start + q, q + 1
+    nothing = [jnp.zeros((rows, lanes), jnp.float32)] * 9
+    seed = halo_planes(seed_ref, nothing, nothing)
+    dual = halo_planes(dual_ref, nothing, nothing)
+    pull_x = [stretch_pull([c[p] for c in seed[3:]], [c[p] for c in dual[3:]], 0) for p in range(depth + 2)]
+    for p in range(depth):
+        at = p + 1
         conf = [c[at] for c in seed[3:]]
         pulled = [c[at] for c in dual[3:]]
         seed_y = [shift.edges(ya_ref, yb_ref, f * depth + p) for f in range(9)]
@@ -214,7 +200,7 @@
             yu, yd = shift.y(pull_y[m], above_y[m], below_y[m])
             zu, zd = shift.z(pull_z[m], edge_z[m])
             flux = 0.5 * ((pull_x[at + 1][m] - pull_x[at - 1][m]) + (yu - yd) + (zu - zd))
-            raw_ref[m, q] = dual[m][at] + time_step * (VISCOSITY * laps[m] - flux)
+            raw_ref[m, p] = dual[m][at] + time_step * (VISCOSITY * laps[m] - flux)
         half = half_factor(conf)
         stress = []
         for n, (i, j) in enumerate(PAIRS):
@@ -235,14 +221,57 @@
         for n, (i, j) in enumerate(PAIRS):
             change = DIFFUSIVITY * laps[3 + n] + half * stress[n]
             change = change + (weight(i, i) + inner if i == j else weight(i, j) + weight(j, i))
-            raw_ref[3 + n, q] = pulled[n] + time_step * change
+            raw_ref[3 + n, p] = pulled[n] + time_step * change
+
+
+def add_halo(raw, side, time_step, seed_ref, dual_ref, plane, halo_ref):
+    half_side = 0.5 * side
+    speed = [halo_ref[f] for f in range(3)]
+    flow = [halo_ref[9 + f] for f in range(3)]
+    dual = [halo_ref[12 + f] for f in range(6)]
+    pull = stretch_pull([halo_ref[3 + f] for f in range(6)], dual, 0)
+    for m in range(3):
+        raw[m] = raw[m] + time_step * (VISCOSITY * flow[m] - half_side * pull[m])
+    conf = [seed_ref[3 + f, plane] for f in range(6)]
+    pulled = [dual_ref[3 + f, plane] for f in range(6)]
+    half = half_factor(conf)
+    inner = 0.0
+    for j in range(3):
+        inner = inner + flow[j] * conf[COMP[0][j]]
+    inner = inner * (half * half) * (-half_side * 2.0 / (EXTENSIBILITY - 3.0))
+    for n, (i, j) in enumerate(PAIRS):
+        change = DIFFUSIVITY * dual[n]
+        if i == j:
+            change = change + inner
+        if i == 0:
+            weight = 0.0
+            for m in range(3):
+                term = speed[m] * pulled[COMP[m][j]]
+                weight = weight + (term + term if m == j else term)
+            change = change + half_side * (weight - half * flow[j])
+        raw[3 + n] = raw[3 + n] + time_step * change
+
+
+def raw_kernel(start, count, has_below, has_above, *refs):
+    steps_ref, seed_ref, dual_ref, local_ref, *halo_refs, raw_ref = refs
+    _, depth, rows, lanes = seed_ref.shape
+    time_step = HORIZON / jnp.full((rows, lanes), steps_ref[0], jnp.int32).astype(jnp.float32)
+    for q in range(count):
+        p = start + q
+        raw = [local_ref[f, p] for f in range(9)]
+        if p == 0 and has_below:
+            add_halo(raw, -1.0, time_step, seed_ref, dual_ref, p, halo_refs[0])
+        if p == depth - 1 and has_above:
+            add_halo(raw, 1.0, time_step, seed_ref, dual_ref, p, halo_refs[-1])
+        for f in range(9):
+            raw_ref[f, q] = raw[f]
 
 
 def next_kernel(steps_ref, seed_ref, ya_ref, yb_ref, z_ref, below_ref, above_ref, next_ref):
     _, depth, rows, lanes = seed_ref.shape
     shift = Shifts(rows, lanes)
     time_step = HORIZON / jnp.full((rows, lanes), steps_ref[0], jnp.int32).astype(jnp.float32)
-    seed = halo_planes(seed_ref, 0, depth, 0, below_ref, above_ref)
+    seed = halo_planes(seed_ref, [below_ref[f] for f in range(9)], [above_ref[f] for f in range(9)])
     halves = [half_factor([c[p] for c in seed[3:]]) for p in range(depth + 2)]
     for p in range(depth):
         at = p + 1
@@ -310,6 +339,7 @@
     lanes, *rows = pack(seed_state, costate)
     ya, yb = rows_y(rows)
     z = call(unpack_kernel, (18,) + seed_state.shape[1:], (), *lanes_z(lanes))
+    local = call(local_kernel, seed_state.shape, (step_count,), seed_state, costate, ya, yb, z)
     walls = lax.axis_size("gy")
     pairs = []
     for start, count in ((0, depth - 1), (depth - 1, 1)):
@@ -320,7 +350,7 @@
             functools.partial(raw_kernel, start, count, has_below, has_above),
             (9, count) + seed_state.shape[2:],
             (step_count,),
-            *(seed_state, costate, ya, yb, z),
+            *(seed_state, costate, local),
             *((below,) if has_below else ()),
             *((above,) if has_above else ()),
         )

time: 18.9 us -> 18.6 us (0.984)
  waiting for transfers between devices: 3.9 us -> 3.51 us
    ppermute x4, waiting for transfers between devices: 1.78 us -> 1.5 us  [ring(): lax.ppermute(array, axis, [(i, (i + step) % size) for i in range(size)])]
    pallas_call x5 -> x6, Pallas kernels: 2.07 us -> 2.1 us  [call(): pl.pallas_call(kernel, out_shape=jax.ShapeDtypeStruct(shape, jnp.float32)...]
where the time goes in v5:
time: 18.6 us; the launch traced here: 18.5 us
  starting transfers between devices  10.2 us (55%)
  waiting for transfers between devices  3.51 us (19%)
  Pallas kernels  2.32 us (12%)
  between operations  1.32 us (7%)
  local copies, waits for them, and re-layouts  1.06 us (6%)
    ppermute x4, starting transfers between devices, ring(): lax.ppermute(array, axis, [(i, (i + step) % size) for i in range(size)])  6.94 us
    ppermute x2, starting transfers between devices, per_device(): lax.ppermute(raw, 'gy', [(i, walls - 1 - i) for i in range(walls)])  3.31 us
    pallas_call x6, Pallas kernels, call(): pl.pallas_call(kernel, out_shape=jax.ShapeDtypeStruct(shape, jnp.float32)...  2.1 us
    ppermute x2, waiting for transfers between devices, per_device(): lax.ppermute(raw, 'gy', [(i, walls - 1 - i) for i in range(walls)])  2 us
    ppermute x4, waiting for transfers between devices, ring(): lax.ppermute(array, axis, [(i, (i + step) % size) for i in range(size)])  1.5 us
    squeeze x1, local copies, waits for them, and re-layouts, per_device(): x[:, p]  1.02 us
  transfers between devices with their start and end apart: 6, of which 5 were waited for; matrix products, arithmetic and copies ran while one was open for 0% of the time, Pallas kernels for 9%

profile of v5, /device:TPU:0, one launch (start us, length us, event | category | flops | bytes accessed | tf_op | source)
XLA Modules:
  0.0 18.5 jit_solution(5477177191014860655)
XLA Ops:
  0.6 1.0 %slice_bitcast_fusion = (f32[9,16,128]{2,1,0:T(8,128)S(1)}, f32[9,16,128]{2,1,0:T(8,128)S(1)}, f32[9,16,128]{2,1,0:T(8,128)S(1)}, f32[9,16,128]{2,1,0:T(8,128)S(1)}) fusion(f32[9,2,16,128]{3,2,1,0:T(8,128)} %refs_2_.5, f32[9,2,16,128]{3,2,1,0:T(8,128)} %refs_1_.5), kind=kLoop, calls=%fused_computation.2 | loop fusion | bytes 589824 | tf_op jit(solution)/shard_map/squeeze | solution.py:336
  1.7 3.1 %collective-permute-start.2 = (f32[18,16,128]{2,1,0:T(8,128)S(1)}, f32[18,16,128]{2,1,0:T(8,128)S(1)}, u32[]{:S(2)}, u32[]{:S(2)}) collective-permute-start(f32[18,16,128]{2,1,0:T(8,128)S(1)} %pad_maximum_fusion), channel_id=1, source_target_pairs={{0,4},{4,8},{8,12},{12,0},{1,5},{5,9},{9,13},{13,1},{2,6},{6,10},{... | collective-permute-start | bytes 442376 | tf_op jit(solution)/shard_map/ppermute | solution.py:21
  4.8 0.0 copy-start
  4.8 0.0 copy-start.1
  4.8 2.1 %collective-permute-start.3 = (f32[18,16,128]{2,1,0:T(8,128)S(1)}, f32[18,16,128]{2,1,0:T(8,128)S(1)}, u32[]{:S(2)}, u32[]{:S(2)}) collective-permute-start(f32[18,16,128]{2,1,0:T(8,128)S(1)} %pad_maximum_fusion.1), channel_id=1, source_target_pairs={{0,12},{4,0},{8,4},{12,8},{1,13},{5,1},{9,5},{13,9},{2,14},{6,2},{... | collective-permute-start | bytes 442376 | tf_op jit(solution)/shard_map/ppermute | solution.py:21
  6.9 0.0 copy-done
  6.9 0.0 copy-done.1
  6.9 0.2 %shard_map.50 = (f32[1,16,128]{2,1,0:T(8,128)S(1)}, f32[36,128]{1,0:T(8,128)S(1)}) custom-call(f32[9,2,16,128]{3,2,1,0:T(8,128)S(1)} %copy-done, f32[9,2,16,128]{3,2,1,0:T(8,128)S(1)} %copy-done.1), custom_call_target="tpu_custom_call" | custom-call | flops 1000000 | bytes 300000 | tf_op jit(solution)/shard_map/pallas_call | solution.py:85
  7.1 1.7 %collective-permute-start = (f32[36,128]{1,0:T(8,128)S(1)}, f32[36,128]{1,0:T(8,128)S(1)}, u32[]{:S(2)}, u32[]{:S(2)}) collective-permute-start(f32[36,128]{1,0:T(8,128)S(1)} %get-tuple-element.4), channel_id=1, source_target_pairs={{0,2},{2,0},{1,3},{3,1},{4,6},{6,4},{5,7},{7,5},{8,10},{10,8},{9,1... | collective-permute-start | bytes 55304 | tf_op jit(solution)/shard_map/ppermute | solution.py:21
  8.8 0.0 collective-permute-start.1
  9.5 0.5 %collective-permute-done.1.above_ref.below_ref = f32[1,16,128]{2,1,0:T(8,128)S(1)} collective-permute-done((f32[1,16,128]{2,1,0:T(8,128)S(1)}, f32[1,16,128]{2,1,0:T(8,128)S(1)}, u32[]{:S(2)}, u32[]{:S(2)}) %collective-permute-start.1) | collective-permute-done | bytes 8224 | tf_op jit(solution)/shard_map/ppermute | solution.py:21
  10.0 0.2 %shard_map.51.z_ref.refs_5_ = f32[18,2,16,128]{3,2,1,0:T(8,128)S(1)} custom-call(f32[1,16,128]{2,1,0:T(8,128)S(1)} %collective-permute-done.1.above_ref.below_ref, f32[1,16,128]{2,1,0:T(8,128)S(1)} %collective-permute-done.1.above_ref.below_ref), custom_call_target="tpu_custom_call" | custom-call | flops 1000000 | bytes 1000000 | tf_op jit(solution)/shard_map/pallas_call | solution.py:324
  10.2 0.7 %collective-permute-done.ya_ref.yb_ref.refs_3_.refs_4_ = f32[36,128]{1,0:T(8,128)S(1)} collective-permute-done((f32[36,128]{1,0:T(8,128)S(1)}, f32[36,128]{1,0:T(8,128)S(1)}, u32[]{:S(2)}, u32[]{:S(2)}) %collective-permute-start) | collective-permute-done | bytes 18464 | tf_op jit(solution)/shard_map/ppermute | solution.py:21
  11.0 0.3 %shard_map.53.refs_3_ = f32[9,2,16,128]{3,2,1,0:T(8,128)S(1)} custom-call(s32[1]{0:T(128)S(6)} %copy.13.steps_ref.refs_0_, f32[9,2,16,128]{3,2,1,0:T(8,128)S(1)} %copy-done, f32[9,2,16,128]{3,2,1,0:T(8,128)S(1)} %copy-done.1, f32[36,128]{1,0:T(8,128)S(1)} %collective-permute-done.ya_ref.yb_ref.refs_3_.refs_4_, ...), custom_call_target="tpu_custom_call" | custom-call | flops 1000000 | bytes 1000000 | tf_op jit(solution)/shard_map/pallas_call | solution.py:324
  11.2 0.3 %collective-permute-done.2.below_ref.refs_4_ = f32[18,16,128]{2,1,0:T(8,128)S(1)} collective-permute-done((f32[18,16,128]{2,1,0:T(8,128)S(1)}, f32[18,16,128]{2,1,0:T(8,128)S(1)}, u32[]{:S(2)}, u32[]{:S(2)}) %collective-permute-start.2) | collective-permute-done | bytes 147488 | tf_op jit(solution)/shard_map/ppermute | solution.py:21
  11.5 1.8 %collective-permute-start.4 = (f32[9,1,16,128]{3,2,1,0:T(8,128)S(1)}, f32[9,1,16,128]{3,2,1,0:T(8,128)S(1)}, u32[]{:S(2)}, u32[]{:S(2)}) collective-permute-start(f32[9,1,16,128]{3,2,1,0:T(8,128)S(1)} %shard_map.54.refs_0_), channel_id=1, source_target_pairs={{0,2},{2,0},{1,3},{3,1},{4,6},{6,4},{5,7},{7,5},{8,10},{10,8},{9,1... | collective-permute-start | bytes 221192 | tf_op jit(solution)/shard_map/ppermute | solution.py:357
  13.3 0.0 collective-permute-done.3.above_ref.refs_4_
  13.4 1.5 %collective-permute-start.5 = (f32[9,1,16,128]{3,2,1,0:T(8,128)S(1)}, f32[9,1,16,128]{3,2,1,0:T(8,128)S(1)}, u32[]{:S(2)}, u32[]{:S(2)}) collective-permute-start(f32[9,1,16,128]{3,2,1,0:T(8,128)S(1)} %shard_map.55.refs_2_), channel_id=1, source_target_pairs={{0,2},{2,0},{1,3},{3,1},{4,6},{6,4},{5,7},{7,5},{8,10},{10,8},{9,1... | collective-permute-start | bytes 221192 | tf_op jit(solution)/shard_map/ppermute | solution.py:357
  14.9 0.9 %shard_map.52 = f32[9,2,16,128]{3,2,1,0:T(8,128)} custom-call(s32[1]{0:T(128)S(6)} %copy.13.steps_ref.refs_0_, f32[9,2,16,128]{3,2,1,0:T(8,128)S(1)} %copy-done, f32[36,128]{1,0:T(8,128)S(1)} %collective-permute-done.ya_ref.yb_ref.refs_3_.refs_4_, f32[36,128]{1,0:T(8,128)S(1)} %collective-permute-done.ya_ref.yb_ref.refs_3_.refs_4_, ...), custom_call_target="tpu_custom_call" | custom-call | flops 1000000 | bytes 1000000 | tf_op jit(solution)/shard_map/pallas_call | solution.py:324
  15.8 0.7 %collective-permute-done.4 = f32[9,1,16,128]{3,2,1,0:T(8,128)S(1)} collective-permute-done((f32[9,1,16,128]{3,2,1,0:T(8,128)S(1)}, f32[9,1,16,128]{3,2,1,0:T(8,128)S(1)}, u32[]{:S(2)}, u32[]{:S(2)}) %collective-permute-start.4) | collective-permute-done | bytes 73760 | tf_op jit(solution)/shard_map/ppermute | solution.py:357
  16.5 1.3 %collective-permute-done.5 = f32[9,1,16,128]{3,2,1,0:T(8,128)S(1)} collective-permute-done((f32[9,1,16,128]{3,2,1,0:T(8,128)S(1)}, f32[9,1,16,128]{3,2,1,0:T(8,128)S(1)}, u32[]{:S(2)}, u32[]{:S(2)}) %collective-permute-start.5) | collective-permute-done | bytes 73760 | tf_op jit(solution)/shard_map/ppermute | solution.py:357
  17.8 0.7 %shard_map.56 = f32[9,2,16,128]{3,2,1,0:T(8,128)} custom-call(f32[9,1,16,128]{3,2,1,0:T(8,128)S(1)} %shard_map.54.refs_0_, f32[9,1,16,128]{3,2,1,0:T(8,128)S(1)} %rev.7.refs_1_, f32[9,1,16,128]{3,2,1,0:T(8,128)S(1)} %shard_map.55.refs_2_, f32[9,1,16,128]{3,2,1,0:T(8,128)S(1)} %rev.8.refs_3_), custom_call_target="tpu_custom_call" | custom-call | flops 1000000 | bytes 1000000 | tf_op jit(solution)/shard_map/pallas_call | solution.py:324
  (6 shorter events, 0.1 us)
Async XLA Ops:
  1.7 9.8 %collective-permute-start.2 = (f32[18,16,128]{2,1,0:T(8,128)S(1)}, f32[18,16,128]{2,1,0:T(8,128)S(1)}, u32[]{:S(2)}, u32[]{:S(2)}) collective-permute-start(f32[18,16,128]{2,1,0:T(8,128)S(1)} %pad_maximum_fusion), channel_id=1, source_target_pairs={{0,4},{4,8},{8,12},{12,0},{1,5},{5,9},{9,13},{13,1},{2,6},{6,10},{... | collective-permute-start | bytes 442376 | tf_op jit(solution)/shard_map/ppermute | solution.py:21
  4.8 2.1 %copy-start = (f32[9,2,16,128]{3,2,1,0:T(8,128)S(1)}, f32[9,2,16,128]{3,2,1,0:T(8,128)}, u32[]{:S(2)}) copy-start(f32[9,2,16,128]{3,2,1,0:T(8,128)} %refs_1_.5) | copy-start | bytes 442372
  4.8 2.1 %copy-start.1 = (f32[9,2,16,128]{3,2,1,0:T(8,128)S(1)}, f32[9,2,16,128]{3,2,1,0:T(8,128)}, u32[]{:S(2)}) copy-start(f32[9,2,16,128]{3,2,1,0:T(8,128)} %refs_2_.5) | copy-start | bytes 442372
  4.8 8.5 %collective-permute-start.3 = (f32[18,16,128]{2,1,0:T(8,128)S(1)}, f32[18,16,128]{2,1,0:T(8,128)S(1)}, u32[]{:S(2)}, u32[]{:S(2)}) collective-permute-start(f32[18,16,128]{2,1,0:T(8,128)S(1)} %pad_maximum_fusion.1), channel_id=1, source_target_pairs={{0,12},{4,0},{8,4},{12,8},{1,13},{5,1},{9,5},{13,9},{2,14},{6,2},{... | collective-permute-start | bytes 442376 | tf_op jit(solution)/shard_map/ppermute | solution.py:21
  7.1 3.8 %collective-permute-start = (f32[36,128]{1,0:T(8,128)S(1)}, f32[36,128]{1,0:T(8,128)S(1)}, u32[]{:S(2)}, u32[]{:S(2)}) collective-permute-start(f32[36,128]{1,0:T(8,128)S(1)} %get-tuple-element.4), channel_id=1, source_target_pairs={{0,2},{2,0},{1,3},{3,1},{4,6},{6,4},{5,7},{7,5},{8,10},{10,8},{9,1... | collective-permute-start | bytes 55304 | tf_op jit(solution)/shard_map/ppermute | solution.py:21
  8.8 1.2 %collective-permute-start.1 = (f32[1,16,128]{2,1,0:T(8,128)S(1)}, f32[1,16,128]{2,1,0:T(8,128)S(1)}, u32[]{:S(2)}, u32[]{:S(2)}) collective-permute-start(f32[1,16,128]{2,1,0:T(8,128)S(1)} %get-tuple-element.5), channel_id=1, source_target_pairs={{0,1},{1,0},{2,3},{3,2},{4,5},{5,4},{6,7},{7,6},{8,9},{9,8},{10,11... | collective-permute-start | bytes 24584 | tf_op jit(solution)/shard_map/ppermute | solution.py:21
  11.5 4.9 %collective-permute-start.4 = (f32[9,1,16,128]{3,2,1,0:T(8,128)S(1)}, f32[9,1,16,128]{3,2,1,0:T(8,128)S(1)}, u32[]{:S(2)}, u32[]{:S(2)}) collective-permute-start(f32[9,1,16,128]{3,2,1,0:T(8,128)S(1)} %shard_map.54.refs_0_), channel_id=1, source_target_pairs={{0,2},{2,0},{1,3},{3,1},{4,6},{6,4},{5,7},{7,5},{8,10},{10,8},{9,1... | collective-permute-start | bytes 221192 | tf_op jit(solution)/shard_map/ppermute | solution.py:357
  13.4 4.4 %collective-permute-start.5 = (f32[9,1,16,128]{3,2,1,0:T(8,128)S(1)}, f32[9,1,16,128]{3,2,1,0:T(8,128)S(1)}, u32[]{:S(2)}, u32[]{:S(2)}) collective-permute-start(f32[9,1,16,128]{3,2,1,0:T(8,128)S(1)} %shard_map.55.refs_2_), channel_id=1, source_target_pairs={{0,2},{2,0},{1,3},{3,1},{4,6},{6,4},{5,7},{7,5},{8,10},{10,8},{9,1... | collective-permute-start | bytes 221192 | tf_op jit(solution)/shard_map/ppermute | solution.py:357

commit v6 on v5

--- a/solution.py
+++ b/solution.py
@@ -307,15 +307,31 @@
             next_ref[3 + n, p] = conf[n] + time_step * (DIFFUSIVITY * laps[3 + n] + stretch - stress)
 
 
-def average_kernel(*refs):
-    *pairs, out_ref = refs
-    plane = 0
-    for raw_ref, image_ref in zip(pairs[::2], pairs[1::2]):
+def average_kernel(planes, *refs):
+    raw_ref, image_ref, *_, out_ref, mean_ref, sem = refs
+    for f, sign in enumerate(SIGNS):
         for q in range(raw_ref.shape[1]):
-            for f, sign in enumerate(SIGNS):
-                raw, image = raw_ref[f, q], image_ref[f, q]
-                out_ref[f, plane] = 0.5 * (raw + image if sign > 0 else raw - image)
-            plane += 1
+            raw, image = raw_ref[f, q], image_ref[f, q]
+            mean_ref[f, q] = 0.5 * (raw + image if sign > 0 else raw - image)
+    copy = pltpu.make_async_copy(mean_ref, out_ref.at[:, planes], sem)
+    copy.start()
+    copy.wait()
+
+
+def average(start, shape, raw, image, so_far):
+    vmem = pl.BlockSpec(memory_space=pltpu.VMEM)
+    hbm = pl.BlockSpec(memory_space=pltpu.HBM)
+    earlier = () if so_far is None else (so_far,)
+    return pl.pallas_call(
+        functools.partial(average_kernel, pl.ds(start, raw.shape[1])),
+        out_shape=jax.ShapeDtypeStruct(shape, jnp.float32),
+        in_specs=[vmem] * 2 + [hbm] * len(earlier),
+        out_specs=hbm,
+        scratch_shapes=[pltpu.VMEM(raw.shape, jnp.float32), pltpu.SemaphoreType.DMA],
+        input_output_aliases={2: 0} if earlier else {},
+        cost_estimate=estimate(1_000_000),
+        compiler_params=grant(),
+    )(raw, image, *earlier)
 
 
 def call(kernel, shape, steps, *arrays):
@@ -341,7 +357,7 @@
     z = call(unpack_kernel, (18,) + seed_state.shape[1:], (), *lanes_z(lanes))
     local = call(local_kernel, seed_state.shape, (step_count,), seed_state, costate, ya, yb, z)
     walls = lax.axis_size("gy")
-    pairs = []
+    gradient = None
     for start, count in ((0, depth - 1), (depth - 1, 1)):
         if count == 0:
             continue
@@ -355,9 +371,9 @@
             *((above,) if has_above else ()),
         )
         partner = lax.ppermute(raw, "gy", [(i, walls - 1 - i) for i in range(walls)])
-        pairs += [raw, jnp.flip(partner, axis=2)]
+        gradient = average(start, seed_state.shape, raw, jnp.flip(partner, axis=2), gradient)
     next_state = call(next_kernel, seed_state.shape, (step_count,), seed_state, ya, yb, z, below, above)
-    return next_state, call(average_kernel, seed_state.shape, (), *pairs)
+    return next_state, gradient
 
 
 def solution(mesh):

time: 18.6 us -> 18.6 us (level)
  waiting for transfers between devices: 3.51 us -> 2.84 us
  Pallas kernels: 2.32 us -> 2.95 us
    pallas_call x0 -> x2, Pallas kernels: none -> 1.31 us  [average(): pl.pallas_call(functools.partial(average_kernel, pl.ds(start, raw.shape[1...]
    pallas_call x6 -> x5, Pallas kernels: 2.1 us -> 1.42 us  [call(): pl.pallas_call(kernel, out_shape=jax.ShapeDtypeStruct(shape, jnp.float32)...]
    ppermute x2, waiting for transfers between devices: 2 us -> 1.34 us  [per_device(): lax.ppermute(raw, 'gy', [(i, walls - 1 - i) for i in range(walls)])]
  transfers between devices with their start and end apart: 6 -> 6, of which waited for: 5 -> 5; matrix products, arithmetic and copies ran while one was open for 0% -> 0% of each run, Pallas kernels for 9% -> 12%
where the time goes in v6:
time: 18.6 us; the launch traced here: 18.4 us
  starting transfers between devices  10.2 us (55%)
  Pallas kernels  2.95 us (16%)
  waiting for transfers between devices  2.84 us (15%)
  between operations  1.33 us (7%)
  local copies, waits for them, and re-layouts  1.06 us (6%)
    ppermute x4, starting transfers between devices, ring(): lax.ppermute(array, axis, [(i, (i + step) % size) for i in range(size)])  6.94 us
    ppermute x2, starting transfers between devices, per_device(): lax.ppermute(raw, 'gy', [(i, walls - 1 - i) for i in range(walls)])  3.31 us
    ppermute x4, waiting for transfers between devices, ring(): lax.ppermute(array, axis, [(i, (i + step) % size) for i in range(size)])  1.5 us
    pallas_call x5, Pallas kernels, call(): pl.pallas_call(kernel, out_shape=jax.ShapeDtypeStruct(shape, jnp.float32)...  1.42 us
    ppermute x2, waiting for transfers between devices, per_device(): lax.ppermute(raw, 'gy', [(i, walls - 1 - i) for i in range(walls)])  1.34 us
    pallas_call x2, Pallas kernels, average(): pl.pallas_call(functools.partial(average_kernel, pl.ds(start, raw.shape[1...  1.31 us
    squeeze x1, local copies, waits for them, and re-layouts, per_device(): x[:, p]  1.02 us
  transfers between devices with their start and end apart: 6, of which 5 were waited for; matrix products, arithmetic and copies ran while one was open for 0% of the time, Pallas kernels for 12%

profile of v6, /device:TPU:0, one launch (start us, length us, event | category | flops | bytes accessed | tf_op | source)
XLA Modules:
  0.0 18.4 jit_solution(14641334254852244557)
XLA Ops:
  0.6 1.0 %slice_bitcast_fusion = (f32[9,16,128]{2,1,0:T(8,128)S(1)}, f32[9,16,128]{2,1,0:T(8,128)S(1)}, f32[9,16,128]{2,1,0:T(8,128)S(1)}, f32[9,16,128]{2,1,0:T(8,128)S(1)}) fusion(f32[9,2,16,128]{3,2,1,0:T(8,128)} %refs_2_.5, f32[9,2,16,128]{3,2,1,0:T(8,128)} %refs_1_.5), kind=kLoop, calls=%fused_computation.2 | loop fusion | bytes 589824 | tf_op jit(solution)/shard_map/squeeze | solution.py:352
  1.7 3.1 %collective-permute-start.2 = (f32[18,16,128]{2,1,0:T(8,128)S(1)}, f32[18,16,128]{2,1,0:T(8,128)S(1)}, u32[]{:S(2)}, u32[]{:S(2)}) collective-permute-start(f32[18,16,128]{2,1,0:T(8,128)S(1)} %pad_maximum_fusion), channel_id=1, source_target_pairs={{0,4},{4,8},{8,12},{12,0},{1,5},{5,9},{9,13},{13,1},{2,6},{6,10},{... | collective-permute-start | bytes 442376 | tf_op jit(solution)/shard_map/ppermute | solution.py:21
  4.8 0.0 copy-start
  4.8 0.0 copy-start.1
  4.8 2.1 %collective-permute-start.3 = (f32[18,16,128]{2,1,0:T(8,128)S(1)}, f32[18,16,128]{2,1,0:T(8,128)S(1)}, u32[]{:S(2)}, u32[]{:S(2)}) collective-permute-start(f32[18,16,128]{2,1,0:T(8,128)S(1)} %pad_maximum_fusion.1), channel_id=1, source_target_pairs={{0,12},{4,0},{8,4},{12,8},{1,13},{5,1},{9,5},{13,9},{2,14},{6,2},{... | collective-permute-start | bytes 442376 | tf_op jit(solution)/shard_map/ppermute | solution.py:21
  6.9 0.0 copy-done
  6.9 0.0 copy-done.1
  6.9 0.2 %shard_map.50 = (f32[1,16,128]{2,1,0:T(8,128)S(1)}, f32[36,128]{1,0:T(8,128)S(1)}) custom-call(f32[9,2,16,128]{3,2,1,0:T(8,128)S(1)} %copy-done, f32[9,2,16,128]{3,2,1,0:T(8,128)S(1)} %copy-done.1), custom_call_target="tpu_custom_call" | custom-call | flops 1000000 | bytes 300000 | tf_op jit(solution)/shard_map/pallas_call | solution.py:85
  7.1 1.7 %collective-permute-start = (f32[36,128]{1,0:T(8,128)S(1)}, f32[36,128]{1,0:T(8,128)S(1)}, u32[]{:S(2)}, u32[]{:S(2)}) collective-permute-start(f32[36,128]{1,0:T(8,128)S(1)} %get-tuple-element.4), channel_id=1, source_target_pairs={{0,2},{2,0},{1,3},{3,1},{4,6},{6,4},{5,7},{7,5},{8,10},{10,8},{9,1... | collective-permute-start | bytes 55304 | tf_op jit(solution)/shard_map/ppermute | solution.py:21
  8.8 0.0 collective-permute-start.1
  9.5 0.5 %collective-permute-done.1.above_ref.below_ref = f32[1,16,128]{2,1,0:T(8,128)S(1)} collective-permute-done((f32[1,16,128]{2,1,0:T(8,128)S(1)}, f32[1,16,128]{2,1,0:T(8,128)S(1)}, u32[]{:S(2)}, u32[]{:S(2)}) %collective-permute-start.1) | collective-permute-done | bytes 8224 | tf_op jit(solution)/shard_map/ppermute | solution.py:21
  10.0 0.2 %shard_map.51.z_ref.refs_5_ = f32[18,2,16,128]{3,2,1,0:T(8,128)S(1)} custom-call(f32[1,16,128]{2,1,0:T(8,128)S(1)} %collective-permute-done.1.above_ref.below_ref, f32[1,16,128]{2,1,0:T(8,128)S(1)} %collective-permute-done.1.above_ref.below_ref), custom_call_target="tpu_custom_call" | custom-call | flops 1000000 | bytes 1000000 | tf_op jit(solution)/shard_map/pallas_call | solution.py:340
  10.2 0.7 %collective-permute-done.ya_ref.yb_ref.refs_3_.refs_4_ = f32[36,128]{1,0:T(8,128)S(1)} collective-permute-done((f32[36,128]{1,0:T(8,128)S(1)}, f32[36,128]{1,0:T(8,128)S(1)}, u32[]{:S(2)}, u32[]{:S(2)}) %collective-permute-start) | collective-permute-done | bytes 18464 | tf_op jit(solution)/shard_map/ppermute | solution.py:21
  11.0 0.3 %shard_map.53.refs_3_ = f32[9,2,16,128]{3,2,1,0:T(8,128)S(1)} custom-call(s32[1]{0:T(128)S(6)} %copy.15.steps_ref.refs_0_, f32[9,2,16,128]{3,2,1,0:T(8,128)S(1)} %copy-done, f32[9,2,16,128]{3,2,1,0:T(8,128)S(1)} %copy-done.1, f32[36,128]{1,0:T(8,128)S(1)} %collective-permute-done.ya_ref.yb_ref.refs_3_.refs_4_, ...), custom_call_target="tpu_custom_call" | custom-call | flops 1000000 | bytes 1000000 | tf_op jit(solution)/shard_map/pallas_call | solution.py:340
  11.2 0.3 %collective-permute-done.2.below_ref.refs_4_ = f32[18,16,128]{2,1,0:T(8,128)S(1)} collective-permute-done((f32[18,16,128]{2,1,0:T(8,128)S(1)}, f32[18,16,128]{2,1,0:T(8,128)S(1)}, u32[]{:S(2)}, u32[]{:S(2)}) %collective-permute-start.2) | collective-permute-done | bytes 147488 | tf_op jit(solution)/shard_map/ppermute | solution.py:21
  11.5 1.8 %collective-permute-start.5 = (f32[9,1,16,128]{3,2,1,0:T(8,128)S(1)}, f32[9,1,16,128]{3,2,1,0:T(8,128)S(1)}, u32[]{:S(2)}, u32[]{:S(2)}) collective-permute-start(f32[9,1,16,128]{3,2,1,0:T(8,128)S(1)} %shard_map.55.refs_0_), channel_id=1, source_target_pairs={{0,2},{2,0},{1,3},{3,1},{4,6},{6,4},{5,7},{7,5},{8,10},{10,8},{9,1... | collective-permute-start | bytes 221192 | tf_op jit(solution)/shard_map/ppermute | solution.py:373
  13.3 0.0 collective-permute-done.3.above_ref.refs_4_
  13.4 1.5 %collective-permute-start.4 = (f32[9,1,16,128]{3,2,1,0:T(8,128)S(1)}, f32[9,1,16,128]{3,2,1,0:T(8,128)S(1)}, u32[]{:S(2)}, u32[]{:S(2)}) collective-permute-start(f32[9,1,16,128]{3,2,1,0:T(8,128)S(1)} %shard_map.54.refs_0_), channel_id=1, source_target_pairs={{0,2},{2,0},{1,3},{3,1},{4,6},{6,4},{5,7},{7,5},{8,10},{10,8},{9,1... | collective-permute-start | bytes 221192 | tf_op jit(solution)/shard_map/ppermute | solution.py:373
  14.9 0.9 %shard_map.52 = f32[9,2,16,128]{3,2,1,0:T(8,128)} custom-call(s32[1]{0:T(128)S(6)} %copy.15.steps_ref.refs_0_, f32[9,2,16,128]{3,2,1,0:T(8,128)S(1)} %copy-done, f32[36,128]{1,0:T(8,128)S(1)} %collective-permute-done.ya_ref.yb_ref.refs_3_.refs_4_, f32[36,128]{1,0:T(8,128)S(1)} %collective-permute-done.ya_ref.yb_ref.refs_3_.refs_4_, ...), custom_call_target="tpu_custom_call" | custom-call | flops 1000000 | bytes 1000000 | tf_op jit(solution)/shard_map/pallas_call | solution.py:340
  15.8 0.7 %collective-permute-done.5 = f32[9,1,16,128]{3,2,1,0:T(8,128)S(1)} collective-permute-done((f32[9,1,16,128]{3,2,1,0:T(8,128)S(1)}, f32[9,1,16,128]{3,2,1,0:T(8,128)S(1)}, u32[]{:S(2)}, u32[]{:S(2)}) %collective-permute-start.5) | collective-permute-done | bytes 73760 | tf_op jit(solution)/shard_map/ppermute | solution.py:373
  16.5 0.7 %shard_map.56.refs_2_ = f32[9,2,16,128]{3,2,1,0:T(8,128)} custom-call(f32[9,1,16,128]{3,2,1,0:T(8,128)S(1)} %shard_map.55.refs_0_, f32[9,1,16,128]{3,2,1,0:T(8,128)S(1)} %rev.8.refs_1_), custom_call_target="tpu_custom_call" | custom-call | flops 1000000 | bytes 1000000 | tf_op jit(solution)/shard_map/pallas_call | solution.py:325
  17.1 0.6 %collective-permute-done.4 = f32[9,1,16,128]{3,2,1,0:T(8,128)S(1)} collective-permute-done((f32[9,1,16,128]{3,2,1,0:T(8,128)S(1)}, f32[9,1,16,128]{3,2,1,0:T(8,128)S(1)}, u32[]{:S(2)}, u32[]{:S(2)}) %collective-permute-start.4) | collective-permute-done | bytes 73760 | tf_op jit(solution)/shard_map/ppermute | solution.py:373
  17.8 0.7 %shard_map.57 = f32[9,2,16,128]{3,2,1,0:T(8,128)} custom-call(f32[9,1,16,128]{3,2,1,0:T(8,128)S(1)} %shard_map.54.refs_0_, f32[9,1,16,128]{3,2,1,0:T(8,128)S(1)} %rev.7.refs_1_, f32[9,2,16,128]{3,2,1,0:T(8,128)} %shard_map.56.refs_2_), custom_call_target="tpu_custom_call", output_to_operand_aliasing={{}: (2, {})} | custom-call | flops 1000000 | bytes 1000000 | tf_op jit(solution)/shard_map/pallas_call | solution.py:325
  (6 shorter events, 0.1 us)
Async XLA Ops:
  1.7 9.8 %collective-permute-start.2 = (f32[18,16,128]{2,1,0:T(8,128)S(1)}, f32[18,16,128]{2,1,0:T(8,128)S(1)}, u32[]{:S(2)}, u32[]{:S(2)}) collective-permute-start(f32[18,16,128]{2,1,0:T(8,128)S(1)} %pad_maximum_fusion), channel_id=1, source_target_pairs={{0,4},{4,8},{8,12},{12,0},{1,5},{5,9},{9,13},{13,1},{2,6},{6,10},{... | collective-permute-start | bytes 442376 | tf_op jit(solution)/shard_map/ppermute | solution.py:21
  4.8 2.1 %copy-start = (f32[9,2,16,128]{3,2,1,0:T(8,128)S(1)}, f32[9,2,16,128]{3,2,1,0:T(8,128)}, u32[]{:S(2)}) copy-start(f32[9,2,16,128]{3,2,1,0:T(8,128)} %refs_1_.5) | copy-start | bytes 442372
  4.8 2.1 %copy-start.1 = (f32[9,2,16,128]{3,2,1,0:T(8,128)S(1)}, f32[9,2,16,128]{3,2,1,0:T(8,128)}, u32[]{:S(2)}) copy-start(f32[9,2,16,128]{3,2,1,0:T(8,128)} %refs_2_.5) | copy-start | bytes 442372
  4.8 8.5 %collective-permute-start.3 = (f32[18,16,128]{2,1,0:T(8,128)S(1)}, f32[18,16,128]{2,1,0:T(8,128)S(1)}, u32[]{:S(2)}, u32[]{:S(2)}) collective-permute-start(f32[18,16,128]{2,1,0:T(8,128)S(1)} %pad_maximum_fusion.1), channel_id=1, source_target_pairs={{0,12},{4,0},{8,4},{12,8},{1,13},{5,1},{9,5},{13,9},{2,14},{6,2},{... | collective-permute-start | bytes 442376 | tf_op jit(solution)/shard_map/ppermute | solution.py:21
  7.1 3.8 %collective-permute-start = (f32[36,128]{1,0:T(8,128)S(1)}, f32[36,128]{1,0:T(8,128)S(1)}, u32[]{:S(2)}, u32[]{:S(2)}) collective-permute-start(f32[36,128]{1,0:T(8,128)S(1)} %get-tuple-element.4), channel_id=1, source_target_pairs={{0,2},{2,0},{1,3},{3,1},{4,6},{6,4},{5,7},{7,5},{8,10},{10,8},{9,1... | collective-permute-start | bytes 55304 | tf_op jit(solution)/shard_map/ppermute | solution.py:21
  8.8 1.2 %collective-permute-start.1 = (f32[1,16,128]{2,1,0:T(8,128)S(1)}, f32[1,16,128]{2,1,0:T(8,128)S(1)}, u32[]{:S(2)}, u32[]{:S(2)}) collective-permute-start(f32[1,16,128]{2,1,0:T(8,128)S(1)} %get-tuple-element.5), channel_id=1, source_target_pairs={{0,1},{1,0},{2,3},{3,2},{4,5},{5,4},{6,7},{7,6},{8,9},{9,8},{10,11... | collective-permute-start | bytes 24584 | tf_op jit(solution)/shard_map/ppermute | solution.py:21
  11.5 4.9 %collective-permute-start.5 = (f32[9,1,16,128]{3,2,1,0:T(8,128)S(1)}, f32[9,1,16,128]{3,2,1,0:T(8,128)S(1)}, u32[]{:S(2)}, u32[]{:S(2)}) collective-permute-start(f32[9,1,16,128]{3,2,1,0:T(8,128)S(1)} %shard_map.55.refs_0_), channel_id=1, source_target_pairs={{0,2},{2,0},{1,3},{3,1},{4,6},{6,4},{5,7},{7,5},{8,10},{10,8},{9,1... | collective-permute-start | bytes 221192 | tf_op jit(solution)/shard_map/ppermute | solution.py:373
  13.4 4.4 %collective-permute-start.4 = (f32[9,1,16,128]{3,2,1,0:T(8,128)S(1)}, f32[9,1,16,128]{3,2,1,0:T(8,128)S(1)}, u32[]{:S(2)}, u32[]{:S(2)}) collective-permute-start(f32[9,1,16,128]{3,2,1,0:T(8,128)S(1)} %shard_map.54.refs_0_), channel_id=1, source_target_pairs={{0,2},{2,0},{1,3},{3,1},{4,6},{6,4},{5,7},{7,5},{8,10},{10,8},{9,1... | collective-permute-start | bytes 221192 | tf_op jit(solution)/shard_map/ppermute | solution.py:373

commit v7 on v6

--- a/solution.py
+++ b/solution.py
@@ -24,6 +24,30 @@
 def line(array, axis, step):
     size = lax.axis_size(axis)
     return lax.ppermute(array, axis, [(i, i + step) for i in range(size) if 0 <= i + step < size])
+
+
+def faces_kernel(seed_ref, dual_ref, first_ref, last_ref, sems):
+    fields, depth = seed_ref.shape[:2]
+    for n, (plane, face_ref) in enumerate(((depth - 1, last_ref), (0, first_ref))):
+        for m, ref in enumerate((seed_ref, dual_ref)):
+            for f in range(fields):
+                pltpu.make_async_copy(ref.at[f, plane], face_ref.at[m * fields + f], sems.at[n]).start()
+    for n, face_ref in enumerate((last_ref, first_ref)):
+        pltpu.make_async_copy(face_ref, face_ref, sems.at[n]).wait()
+
+
+def faces(seed_state, costate):
+    fields, _, rows, lanes = seed_state.shape
+    vmem = pl.BlockSpec(memory_space=pltpu.VMEM)
+    return pl.pallas_call(
+        faces_kernel,
+        out_shape=[jax.ShapeDtypeStruct((2 * fields, rows, lanes), jnp.float32)] * 2,
+        in_specs=[pl.BlockSpec(memory_space=pltpu.HBM)] * 2,
+        out_specs=[vmem] * 2,
+        scratch_shapes=[pltpu.SemaphoreType.DMA((2,))],
+        cost_estimate=estimate(600_000),
+        compiler_params=grant(),
+    )(*(pltpu.with_memory_space_constraint(x, pltpu.HBM) for x in (seed_state, costate)))
 
 
 def pack_kernel(seed_ref, dual_ref, lanes_ref, *rows_refs):
@@ -349,7 +373,7 @@
 
 def per_device(seed_state, costate, step_count):
     depth = seed_state.shape[1]
-    first, last = (jnp.concatenate([x[:, p] for x in (seed_state, costate)], 0) for p in (0, -1))
+    first, last = faces(seed_state, costate)
     below = ring(last, "gx", 1)
     above = ring(first, "gx", -1)
     lanes, *rows = pack(seed_state, costate)

time: 18.6 us -> 18.6 us (level)
  local copies, waits for them, and re-layouts: 1.06 us -> 0.04 us
  Pallas kernels: 2.95 us -> 3.93 us
    squeeze x1 -> x0, local copies, waits for them, and re-layouts: 1.02 us -> none  [per_device(): x[:, p]]
    pallas_call x0 -> x1, Pallas kernels: none -> 0.98 us  [faces(): pl.pallas_call(faces_kernel, out_shape=[jax.ShapeDtypeStruct((2 * fields,...]
where the time goes in v7:
time: 18.6 us; the launch traced here: 18.4 us
  starting transfers between devices  10.1 us (54%)
  Pallas kernels  3.93 us (21%)
  waiting for transfers between devices  2.99 us (16%)
  between operations  1.34 us (7%)
    ppermute x4, starting transfers between devices, ring(): lax.ppermute(array, axis, [(i, (i + step) % size) for i in range(size)])  6.88 us
    ppermute x2, starting transfers between devices, per_device(): lax.ppermute(raw, 'gy', [(i, walls - 1 - i) for i in range(walls)])  3.23 us
    ppermute x4, waiting for transfers between devices, ring(): lax.ppermute(array, axis, [(i, (i + step) % size) for i in range(size)])  1.57 us
    pallas_call x5, Pallas kernels, call(): pl.pallas_call(kernel, out_shape=jax.ShapeDtypeStruct(shape, jnp.float32)...  1.42 us
    ppermute x2, waiting for transfers between devices, per_device(): lax.ppermute(raw, 'gy', [(i, walls - 1 - i) for i in range(walls)])  1.41 us
    pallas_call x2, Pallas kernels, average(): pl.pallas_call(functools.partial(average_kernel, pl.ds(start, raw.shape[1...  1.31 us
    pallas_call x1, Pallas kernels, faces(): pl.pallas_call(faces_kernel, out_shape=[jax.ShapeDtypeStruct((2 * fields,...  0.98 us
  transfers between devices with their start and end apart: 6, of which 5 were waited for; matrix products, arithmetic and copies ran while one was open for 0% of the time, Pallas kernels for 12%

profile of v7, /device:TPU:0, one launch (start us, length us, event | category | flops | bytes accessed | tf_op | source)
XLA Modules:
  0.0 18.4 jit_solution(6912460694754564061)
XLA Ops:
  0.6 0.0 copy-start
  0.6 0.0 copy-start.1
  0.6 1.0 %shard_map.52 = (f32[18,16,128]{2,1,0:T(8,128)S(1)}, f32[18,16,128]{2,1,0:T(8,128)S(1)}) custom-call(f32[9,2,16,128]{3,2,1,0:T(8,128)} %refs_1_.5, f32[9,2,16,128]{3,2,1,0:T(8,128)} %refs_2_.5), custom_call_target="tpu_custom_call" | custom-call | flops 1000000 | bytes 600000 | tf_op jit(solution)/shard_map/pallas_call | solution.py:42
  1.6 3.1 %collective-permute-start.2 = (f32[18,16,128]{2,1,0:T(8,128)S(1)}, f32[18,16,128]{2,1,0:T(8,128)S(1)}, u32[]{:S(2)}, u32[]{:S(2)}) collective-permute-start(f32[18,16,128]{2,1,0:T(8,128)S(1)} %get-tuple-element.8), channel_id=1, source_target_pairs={{0,4},{4,8},{8,12},{12,0},{1,5},{5,9},{9,13},{13,1},{2,6},{6,10},{... | collective-permute-start | bytes 442376 | tf_op jit(solution)/shard_map/ppermute | solution.py:21
  4.7 2.1 %collective-permute-start.3 = (f32[18,16,128]{2,1,0:T(8,128)S(1)}, f32[18,16,128]{2,1,0:T(8,128)S(1)}, u32[]{:S(2)}, u32[]{:S(2)}) collective-permute-start(f32[18,16,128]{2,1,0:T(8,128)S(1)} %get-tuple-element.9), channel_id=1, source_target_pairs={{0,12},{4,0},{8,4},{12,8},{1,13},{5,1},{9,5},{13,9},{2,14},{6,2},{... | collective-permute-start | bytes 442376 | tf_op jit(solution)/shard_map/ppermute | solution.py:21
  6.8 0.0 copy-done
  6.8 0.0 copy-done.1
  6.8 0.2 %shard_map.50 = (f32[1,16,128]{2,1,0:T(8,128)S(1)}, f32[36,128]{1,0:T(8,128)S(1)}) custom-call(f32[9,2,16,128]{3,2,1,0:T(8,128)S(1)} %copy-done, f32[9,2,16,128]{3,2,1,0:T(8,128)S(1)} %copy-done.1), custom_call_target="tpu_custom_call" | custom-call | flops 1000000 | bytes 300000 | tf_op jit(solution)/shard_map/pallas_call | solution.py:109
  7.0 1.7 %collective-permute-start = (f32[36,128]{1,0:T(8,128)S(1)}, f32[36,128]{1,0:T(8,128)S(1)}, u32[]{:S(2)}, u32[]{:S(2)}) collective-permute-start(f32[36,128]{1,0:T(8,128)S(1)} %get-tuple-element.6), channel_id=1, source_target_pairs={{0,2},{2,0},{1,3},{3,1},{4,6},{6,4},{5,7},{7,5},{8,10},{10,8},{9,1... | collective-permute-start | bytes 55304 | tf_op jit(solution)/shard_map/ppermute | solution.py:21
  8.7 0.0 collective-permute-start.1
  9.4 0.5 %collective-permute-done.1.above_ref.below_ref = f32[1,16,128]{2,1,0:T(8,128)S(1)} collective-permute-done((f32[1,16,128]{2,1,0:T(8,128)S(1)}, f32[1,16,128]{2,1,0:T(8,128)S(1)}, u32[]{:S(2)}, u32[]{:S(2)}) %collective-permute-start.1) | collective-permute-done | bytes 8224 | tf_op jit(solution)/shard_map/ppermute | solution.py:21
  9.9 0.2 %shard_map.51.z_ref.refs_5_ = f32[18,2,16,128]{3,2,1,0:T(8,128)S(1)} custom-call(f32[1,16,128]{2,1,0:T(8,128)S(1)} %collective-permute-done.1.above_ref.below_ref, f32[1,16,128]{2,1,0:T(8,128)S(1)} %collective-permute-done.1.above_ref.below_ref), custom_call_target="tpu_custom_call" | custom-call | flops 1000000 | bytes 1000000 | tf_op jit(solution)/shard_map/pallas_call | solution.py:364
  10.1 0.7 %collective-permute-done.ya_ref.yb_ref.refs_3_.refs_4_ = f32[36,128]{1,0:T(8,128)S(1)} collective-permute-done((f32[36,128]{1,0:T(8,128)S(1)}, f32[36,128]{1,0:T(8,128)S(1)}, u32[]{:S(2)}, u32[]{:S(2)}) %collective-permute-start) | collective-permute-done | bytes 18464 | tf_op jit(solution)/shard_map/ppermute | solution.py:21
  10.9 0.3 %shard_map.54.refs_3_ = f32[9,2,16,128]{3,2,1,0:T(8,128)S(1)} custom-call(s32[1]{0:T(128)S(6)} %copy.7.steps_ref.refs_0_, f32[9,2,16,128]{3,2,1,0:T(8,128)S(1)} %copy-done, f32[9,2,16,128]{3,2,1,0:T(8,128)S(1)} %copy-done.1, f32[36,128]{1,0:T(8,128)S(1)} %collective-permute-done.ya_ref.yb_ref.refs_3_.refs_4_, ...), custom_call_target="tpu_custom_call" | custom-call | flops 1000000 | bytes 1000000 | tf_op jit(solution)/shard_map/pallas_call | solution.py:364
  11.2 0.3 %collective-permute-done.2.below_ref.refs_4_ = f32[18,16,128]{2,1,0:T(8,128)S(1)} collective-permute-done((f32[18,16,128]{2,1,0:T(8,128)S(1)}, f32[18,16,128]{2,1,0:T(8,128)S(1)}, u32[]{:S(2)}, u32[]{:S(2)}) %collective-permute-start.2) | collective-permute-done | bytes 147488 | tf_op jit(solution)/shard_map/ppermute | solution.py:21
  11.5 1.8 %collective-permute-start.5 = (f32[9,1,16,128]{3,2,1,0:T(8,128)S(1)}, f32[9,1,16,128]{3,2,1,0:T(8,128)S(1)}, u32[]{:S(2)}, u32[]{:S(2)}) collective-permute-start(f32[9,1,16,128]{3,2,1,0:T(8,128)S(1)} %shard_map.56.refs_0_), channel_id=1, source_target_pairs={{0,2},{2,0},{1,3},{3,1},{4,6},{6,4},{5,7},{7,5},{8,10},{10,8},{9,1... | collective-permute-start | bytes 221192 | tf_op jit(solution)/shard_map/ppermute | solution.py:397
  13.3 0.0 collective-permute-done.3.above_ref.refs_4_
  13.3 1.5 %collective-permute-start.4 = (f32[9,1,16,128]{3,2,1,0:T(8,128)S(1)}, f32[9,1,16,128]{3,2,1,0:T(8,128)S(1)}, u32[]{:S(2)}, u32[]{:S(2)}) collective-permute-start(f32[9,1,16,128]{3,2,1,0:T(8,128)S(1)} %shard_map.55.refs_0_), channel_id=1, source_target_pairs={{0,2},{2,0},{1,3},{3,1},{4,6},{6,4},{5,7},{7,5},{8,10},{10,8},{9,1... | collective-permute-start | bytes 221192 | tf_op jit(solution)/shard_map/ppermute | solution.py:397
  14.8 0.9 %shard_map.53 = f32[9,2,16,128]{3,2,1,0:T(8,128)} custom-call(s32[1]{0:T(128)S(6)} %copy.7.steps_ref.refs_0_, f32[9,2,16,128]{3,2,1,0:T(8,128)S(1)} %copy-done, f32[36,128]{1,0:T(8,128)S(1)} %collective-permute-done.ya_ref.yb_ref.refs_3_.refs_4_, f32[36,128]{1,0:T(8,128)S(1)} %collective-permute-done.ya_ref.yb_ref.refs_3_.refs_4_, ...), custom_call_target="tpu_custom_call" | custom-call | flops 1000000 | bytes 1000000 | tf_op jit(solution)/shard_map/pallas_call | solution.py:364
  15.6 0.9 %collective-permute-done.5 = f32[9,1,16,128]{3,2,1,0:T(8,128)S(1)} collective-permute-done((f32[9,1,16,128]{3,2,1,0:T(8,128)S(1)}, f32[9,1,16,128]{3,2,1,0:T(8,128)S(1)}, u32[]{:S(2)}, u32[]{:S(2)}) %collective-permute-start.5) | collective-permute-done | bytes 73760 | tf_op jit(solution)/shard_map/ppermute | solution.py:397
  16.6 0.7 %shard_map.57.refs_2_ = f32[9,2,16,128]{3,2,1,0:T(8,128)} custom-call(f32[9,1,16,128]{3,2,1,0:T(8,128)S(1)} %shard_map.56.refs_0_, f32[9,1,16,128]{3,2,1,0:T(8,128)S(1)} %rev.8.refs_1_), custom_call_target="tpu_custom_call" | custom-call | flops 1000000 | bytes 1000000 | tf_op jit(solution)/shard_map/pallas_call | solution.py:349
  17.2 0.5 %collective-permute-done.4 = f32[9,1,16,128]{3,2,1,0:T(8,128)S(1)} collective-permute-done((f32[9,1,16,128]{3,2,1,0:T(8,128)S(1)}, f32[9,1,16,128]{3,2,1,0:T(8,128)S(1)}, u32[]{:S(2)}, u32[]{:S(2)}) %collective-permute-start.4) | collective-permute-done | bytes 73760 | tf_op jit(solution)/shard_map/ppermute | solution.py:397
  17.8 0.7 %shard_map.58 = f32[9,2,16,128]{3,2,1,0:T(8,128)} custom-call(f32[9,1,16,128]{3,2,1,0:T(8,128)S(1)} %shard_map.55.refs_0_, f32[9,1,16,128]{3,2,1,0:T(8,128)S(1)} %rev.7.refs_1_, f32[9,2,16,128]{3,2,1,0:T(8,128)} %shard_map.57.refs_2_), custom_call_target="tpu_custom_call", output_to_operand_aliasing={{}: (2, {})} | custom-call | flops 1000000 | bytes 1000000 | tf_op jit(solution)/shard_map/pallas_call | solution.py:349
  (4 shorter events, 0.1 us)
Async XLA Ops:
  0.6 6.2 %copy-start = (f32[9,2,16,128]{3,2,1,0:T(8,128)S(1)}, f32[9,2,16,128]{3,2,1,0:T(8,128)}, u32[]{:S(2)}) copy-start(f32[9,2,16,128]{3,2,1,0:T(8,128)} %refs_1_.5) | copy-start | bytes 442372
  0.6 6.2 %copy-start.1 = (f32[9,2,16,128]{3,2,1,0:T(8,128)S(1)}, f32[9,2,16,128]{3,2,1,0:T(8,128)}, u32[]{:S(2)}) copy-start(f32[9,2,16,128]{3,2,1,0:T(8,128)} %refs_2_.5) | copy-start | bytes 442372
  1.6 9.8 %collective-permute-start.2 = (f32[18,16,128]{2,1,0:T(8,128)S(1)}, f32[18,16,128]{2,1,0:T(8,128)S(1)}, u32[]{:S(2)}, u32[]{:S(2)}) collective-permute-start(f32[18,16,128]{2,1,0:T(8,128)S(1)} %get-tuple-element.8), channel_id=1, source_target_pairs={{0,4},{4,8},{8,12},{12,0},{1,5},{5,9},{9,13},{13,1},{2,6},{6,10},{... | collective-permute-start | bytes 442376 | tf_op jit(solution)/shard_map/ppermute | solution.py:21
  4.7 8.6 %collective-permute-start.3 = (f32[18,16,128]{2,1,0:T(8,128)S(1)}, f32[18,16,128]{2,1,0:T(8,128)S(1)}, u32[]{:S(2)}, u32[]{:S(2)}) collective-permute-start(f32[18,16,128]{2,1,0:T(8,128)S(1)} %get-tuple-element.9), channel_id=1, source_target_pairs={{0,12},{4,0},{8,4},{12,8},{1,13},{5,1},{9,5},{13,9},{2,14},{6,2},{... | collective-permute-start | bytes 442376 | tf_op jit(solution)/shard_map/ppermute | solution.py:21
  7.0 3.8 %collective-permute-start = (f32[36,128]{1,0:T(8,128)S(1)}, f32[36,128]{1,0:T(8,128)S(1)}, u32[]{:S(2)}, u32[]{:S(2)}) collective-permute-start(f32[36,128]{1,0:T(8,128)S(1)} %get-tuple-element.6), channel_id=1, source_target_pairs={{0,2},{2,0},{1,3},{3,1},{4,6},{6,4},{5,7},{7,5},{8,10},{10,8},{9,1... | collective-permute-start | bytes 55304 | tf_op jit(solution)/shard_map/ppermute | solution.py:21
  8.7 1.2 %collective-permute-start.1 = (f32[1,16,128]{2,1,0:T(8,128)S(1)}, f32[1,16,128]{2,1,0:T(8,128)S(1)}, u32[]{:S(2)}, u32[]{:S(2)}) collective-permute-start(f32[1,16,128]{2,1,0:T(8,128)S(1)} %get-tuple-element.7), channel_id=1, source_target_pairs={{0,1},{1,0},{2,3},{3,2},{4,5},{5,4},{6,7},{7,6},{8,9},{9,8},{10,11... | collective-permute-start | bytes 24584 | tf_op jit(solution)/shard_map/ppermute | solution.py:21
  11.5 5.1 %collective-permute-start.5 = (f32[9,1,16,128]{3,2,1,0:T(8,128)S(1)}, f32[9,1,16,128]{3,2,1,0:T(8,128)S(1)}, u32[]{:S(2)}, u32[]{:S(2)}) collective-permute-start(f32[9,1,16,128]{3,2,1,0:T(8,128)S(1)} %shard_map.56.refs_0_), channel_id=1, source_target_pairs={{0,2},{2,0},{1,3},{3,1},{4,6},{6,4},{5,7},{7,5},{8,10},{10,8},{9,1... | collective-permute-start | bytes 221192 | tf_op jit(solution)/shard_map/ppermute | solution.py:397
  13.3 4.4 %collective-permute-start.4 = (f32[9,1,16,128]{3,2,1,0:T(8,128)S(1)}, f32[9,1,16,128]{3,2,1,0:T(8,128)S(1)}, u32[]{:S(2)}, u32[]{:S(2)}) collective-permute-start(f32[9,1,16,128]{3,2,1,0:T(8,128)S(1)} %shard_map.55.refs_0_), channel_id=1, source_target_pairs={{0,2},{2,0},{1,3},{3,1},{4,6},{6,4},{5,7},{7,5},{8,10},{10,8},{9,1... | collective-permute-start | bytes 221192 | tf_op jit(solution)/shard_map/ppermute | solution.py:397
